TPU v7x, 128 devices: a whole 4x4x4 slice. The times are simulated.
128 devices in a mesh: dp: 16 (over y, x_lo, core), mp: 8 (over x_hi, z).
Axes of the slice: x: 4 (x_hi: 2, x_lo: 2; x = x_hi * 2 + x_lo), y: 4, z: 4, core: 2. Of those that a mesh axis runs over, the one named last changes fastest.
Arguments:
- block_input: bfloat16 [16, 16, 8, 8, 2048], P('dp', None, None, None, 'mp'), may hold values from -6 to 6
- spatial_out: bfloat16 [16, 16, 8, 8, 2048], P('dp', None, None, None, 'mp'), may hold values from -6 to 6
- cotangent: bfloat16 [16, 16, 8, 8, 2048], P('dp', None, None, None, 'mp'), may hold values from -0.59765625 to 0.59765625
- spatial_kernel: bfloat16 [3, 3, 2048, 2048], P(None, None, None, 'mp'), may hold values from -0.046875 to 0.046875
- temporal_kernel: bfloat16 [3, 2048, 2048], P(None, None, 'mp'), may hold values from -0.078125 to 0.078125
- norm_gain: float32 [2048], P('mp'), may hold values from 0.1 to 1.9
- norm_bias: float32 [2048], P('mp'), may hold values from -1 to 1
Outputs:
- input_grad: bfloat16 [16, 16, 8, 8, 2048], P('dp', None, None, None, 'mp')
- spatial_kernel_grad: float32 [3, 3, 2048, 2048], P(None, None, 'dp', 'mp')
- temporal_kernel_grad: float32 [3, 2048, 2048], P(None, 'dp', 'mp')
- gain_grad: float32 [2048], P('mp')
- bias_grad: float32 [2048], P('mp')
All inputs are finite; a program needn't handle non-finite values.
Results may differ from a plain program's by a relative error of at most 0.005.
Values may be sent and summed in bfloat16 or wider, within the bound.
No kernel may reach another device: no remote copies, remote signals or barrier semaphores. Data moves between devices by JAX's collectives and lax.ppermute only.
A program may use at most 192 MiB of HBM per device.

v0:
```python
import jax
import jax.numpy as jnp
from jax import lax
from jax.sharding import PartitionSpec as P

C = 2048
G = 32
FR = 16
HT = 8
WD = 8


EPSILON = 1e-05


def shifted(values, clip_count, step_f, step_y, step_x):
    channels = values.shape[1]
    volume = values.reshape(clip_count, FR, HT, WD, channels)
    padded = jnp.pad(volume, ((0, 0), (1, 1), (1, 1), (1, 1), (0, 0)))
    window = padded[
        :,
        1 + step_f : 1 + step_f + FR,
        1 + step_y : 1 + step_y + HT,
        1 + step_x : 1 + step_x + WD,
        :,
    ]
    return window.reshape(-1, channels)


def contract_rows(left, right):
    return lax.dot_general(
        left, right, (((0,), (0,)), ((), ())), preferred_element_type=jnp.float32
    )


def contract_cols(left, right):
    return lax.dot_general(
        left, right, (((1,), (1,)), ((), ())), preferred_element_type=jnp.float32
    )


def group_stats(flat, clip_count):
    channels = flat.shape[1]
    grouped = flat.reshape(clip_count, -1, channels // (C // G), C // G)
    center = jnp.mean(grouped, axis=(1, 3), keepdims=True)
    spread = jnp.mean(jnp.square(grouped - center), axis=(1, 3), keepdims=True)
    inverse = lax.rsqrt(spread + EPSILON)
    return (((grouped - center) * inverse).reshape(flat.shape), inverse)


def group_backward(upstream, normed_hat, inverse, clip_count):
    channels = upstream.shape[1]
    grad_groups = upstream.reshape(clip_count, -1, channels // (C // G), C // G)
    hat_groups = normed_hat.reshape(grad_groups.shape)
    first = jnp.mean(grad_groups, axis=(1, 3), keepdims=True)
    second = jnp.mean(grad_groups * hat_groups, axis=(1, 3), keepdims=True)
    return (inverse * (grad_groups - first - hat_groups * second)).reshape(upstream.shape)


def local(
    block_input, spatial_out, cotangent, spatial_kernel, temporal_kernel, norm_gain, norm_bias
):
    clip_count = block_input.shape[0]
    local_width = block_input.shape[4]
    flat_in = block_input.reshape(-1, local_width).astype(jnp.float32)
    normed_hat, inverse = group_stats(flat_in, clip_count)
    normed = normed_hat * norm_gain + norm_bias
    gate = jax.nn.sigmoid(normed)
    hidden = (normed * gate).astype(jnp.bfloat16)
    saved = spatial_out.reshape(-1, local_width)
    upstream = cotangent.reshape(-1, local_width)
    temporal_term = contract_cols(shifted(upstream, clip_count, 1, 0, 0), temporal_kernel[0])
    for offset in range(1, 3):
        temporal_term = temporal_term + contract_cols(
            shifted(upstream, clip_count, 1 - offset, 0, 0), temporal_kernel[offset]
        )
    saved_grad = lax.psum_scatter(temporal_term, "mp", scatter_dimension=1, tiled=True).astype(
        jnp.bfloat16
    )
    saved_full = lax.all_gather(saved, "mp", axis=1, tiled=True)
    temporal_local = jnp.stack(
        [
            contract_rows(shifted(saved_full, clip_count, offset - 1, 0, 0), upstream)
            for offset in range(3)
        ]
    )
    temporal_grad = lax.psum_scatter(temporal_local, "dp", scatter_dimension=1, tiled=True)
    spatial_term = jnp.zeros((upstream.shape[0], spatial_kernel.shape[2]), jnp.float32)
    for tap_y in range(3):
        for tap_x in range(3):
            spatial_term = spatial_term + contract_cols(
                shifted(saved_grad, clip_count, 0, 1 - tap_y, 1 - tap_x),
                spatial_kernel[tap_y, tap_x],
            )
    hidden_grad = lax.psum_scatter(spatial_term, "mp", scatter_dimension=1, tiled=True)
    hidden_full = lax.all_gather(hidden, "mp", axis=1, tiled=True)
    spatial_local = jnp.stack(
        [
            jnp.stack(
                [
                    contract_rows(
                        shifted(hidden_full, clip_count, 0, tap_y - 1, tap_x - 1), saved_grad
                    )
                    for tap_x in range(3)
                ]
            )
            for tap_y in range(3)
        ]
    )
    spatial_grad = lax.psum_scatter(spatial_local, "dp", scatter_dimension=2, tiled=True)
    normed_grad = hidden_grad * gate * (1.0 + normed * (1.0 - gate))
    gain_grad, bias_grad = lax.psum(
        (jnp.sum(normed_grad * normed_hat, axis=0), jnp.sum(normed_grad, axis=0)), "dp"
    )
    branch = group_backward(normed_grad * norm_gain, normed_hat, inverse, clip_count)
    input_grad = (
        (upstream.astype(jnp.float32) + branch).astype(jnp.bfloat16).reshape(block_input.shape)
    )
    return (input_grad, spatial_grad, temporal_grad, gain_grad, bias_grad)


def solution(mesh):
    placed = (
        P("dp", None, None, None, "mp"),
        P("dp", None, None, None, "mp"),
        P("dp", None, None, None, "mp"),
        P(None, None, None, "mp"),
        P(None, None, "mp"),
        P("mp"),
        P("mp"),
    )
    return jax.shard_map(
        local,
        mesh=mesh,
        in_specs=placed,
        out_specs=(
            P("dp", None, None, None, "mp"),
            P(None, None, "dp", "mp"),
            P(None, "dp", "mp"),
            P("mp"),
            P("mp"),
        ),
        check_vma=False,
    )
```

profile of v0, /device:TPU:6, one launch (start us, length us, event | category | flops | bytes accessed | tf_op | source)
XLA Modules:
  0.0 748.1 jit_solution(919838330639746423)
XLA Ops:
  7.2 1.3 pad_slice_fusion.18
  8.5 2.7 fusion.33
  11.2 1.3 fusion.31
  12.5 4.5 add_add_fusion.1
  17.1 0.2 reduce-scatter.7.cloned.1.call-start
  17.3 115.2 %reduce-scatter.5.cloned.1.call-done = f32[1024,256]{1,0:T(8,128)} async-done(((f32[1024,2048]{1,0:T(8,128)}), f32[1024,256]{1,0:T(8,128)}) %reduce-scatter.5.cloned.1.call-update) | async-done | bytes 1048592 | tf_op jit(solution)/shard_map/reduce_scatter | solution.py:77
  132.4 1.4 convert_element_type.59
  133.8 0.8 pad_slice_fusion.10
  134.6 6.1 fusion.20
  140.7 4.5 fusion.14
  145.2 4.5 fusion.16
  149.7 4.5 fusion.18
  154.2 4.5 fusion.22
  158.7 4.5 fusion.24
  163.2 4.5 fusion.26
  167.7 4.5 fusion.28
  172.2 25.5 %add_add_fusion = f32[1024,2048]{1,0:T(8,128)} fusion(f32[1024,2048]{1,0:T(8,128)} %fusion.14, f32[1024,2048]{1,0:T(8,128)} %fusion.16, f32[1024,2048]{1,0:T(8,128)} %fusion.18, f32[1024,2048]{1,0:T(8,128)} %fusion.20, f32[1024,2048]{1,0:T(8,128)} %fusion.22, f32[1024,2048]{1,0:T(8,128)} %fusion.24, f32[1024,2048]{1,0:T(8,128)} %fusion.28, ...), kind=kOutput, calls=%fused_computation.11 | convolution fusion | flops 1090519040 | bytes 77070336 | tf_op jit(solution)/shard_map/dot_general | solution.py:37
  197.8 0.7 all-gather.5.cloned.1.call-update
  198.4 0.4 all-gather.3.cloned.1.call-start
  198.9 0.2 convert_reduce_fusion
  199.4 0.2 multiply_reduce_fusion.2
  199.7 0.1 reduce_sum.73
  200.0 109.8 %reduce-scatter.7.cloned.1.call-done = f32[1024,256]{1,0:T(8,128)} async-done(((f32[1024,2048]{1,0:T(8,128)}), f32[1024,256]{1,0:T(8,128)}) %reduce-scatter.7.cloned.1.call-update) | async-done | bytes 1048592 | tf_op jit(solution)/shard_map/reduce_scatter | solution.py:95
  309.9 2.8 multiply_reduce_fusion
  312.7 70.9 %all-gather.5.cloned.1.call-done = bf16[1024,2048]{1,0:T(8,128)(2,1)} async-done(((bf16[1024,256]{1,0:T(8,128)(2,1)}), bf16[1024,2048]{1,0:T(8,128)(2,1)}) %all-gather.5.cloned.1.call-update) | async-done | bytes 4194320 | tf_op jit(solution)/shard_map/all_gather | solution.py:80
  383.7 4.7 copy.17
  388.4 1.4 convolution_bitcast_fusion
  389.8 1.7 fusion.6
  391.5 1.7 fusion.9
  393.2 3.0 pad_maximum_fusion.1
  396.3 61.7 %all-gather.3.cloned.1.call-done = bf16[1024,2048]{1,0:T(8,128)(2,1)} async-done(((bf16[1024,256]{1,0:T(8,128)(2,1)}), bf16[1024,2048]{1,0:T(8,128)(2,1)}) %all-gather.3.cloned.1.call-update) | async-done | bytes 4194320 | tf_op jit(solution)/shard_map/all_gather | solution.py:96
  458.0 21.6 %pad_slice_fusion.7 = (bf16[1,16,8,8,2048]{4,3,2,1,0:T(8,128)(2,1)S(1)}, bf16[1,16,8,8,2048]{4,3,2,1,0:T(8,128)(2,1)S(1)}, bf16[1,16,8,8,2048]{4,3,2,1,0:T(8,128...) fusion(bf16[1,16,8,8,2048]{4,3,2,1,0:T(8,128)(2,1)} %bitcast.164), kind=kLoop, calls=%fused_computation.7 | loop fusion | bytes 37748736 | tf_op jit(solution)/shard_map/slice | solution.py:20
  479.6 3.7 convolution_bitcast_fusion.3
  483.4 1.4 convolution_bitcast_fusion.2
  484.7 0.8 copy-done.3
  485.6 2.8 convolution_bitcast_fusion.1
  488.3 2.0 maximum_bitcast_fusion.2
  490.4 3.6 convolution_bitcast_fusion.6
  494.0 2.7 convolution_bitcast_fusion.4
  496.7 1.4 convolution_bitcast_fusion.9
  498.0 1.4 convolution_bitcast_fusion.8
  499.4 2.7 convolution_bitcast_fusion.7
  502.1 2.7 convolution_bitcast_fusion.5
  504.8 2.8 maximum_bitcast_fusion
  507.7 7.1 pad_maximum_fusion
  515.5 26.8 %all-reduce.4 = (f32[256]{0:T(256)}, f32[256]{0:T(256)}) all-reduce(f32[256]{0:T(256)S(1)} %get-tuple-element.5, f32[256]{0:T(256)S(1)} %get-tuple-element.8), channel_id=1, replica_groups=mesh['dp'=16,'mp'=8] {'dp'}, use_global_device_ids=true, to_apply=%region_13.14 | all-reduce | flops 512 | bytes 4096 | tf_op jit(solution)/shard_map/psum | solution.py:112
  542.4 1.2 add_convert_fusion
  543.6 197.5 %reduce-scatter.9.cloned.1.call-done = f32[3,3,128,256]{3,2,1,0:T(8,128)} async-done(((f32[3,3,2048,256]{3,2,1,0:T(8,128)}), f32[3,3,128,256]{3,2,1,0:T(8,128)}) %reduce-scatter.9.cloned.1.call-update) | async-done | bytes 1179664 | tf_op jit(solution)/shard_map/reduce_scatter | solution.py:110
  (55 shorter events, 1.7 us)
Async XLA Ops:
  7.2 125.3 %reduce-scatter.5.cloned.1.call-start = ((), (), s32[]{:S(2)}) async-start(), calls=%async_computation.4 | async-start | bytes 9437184 | tf_op jit(solution)/shard_map/reduce_scatter | solution.py:77
  8.5 2.7 copy-start.1
  8.5 2.7 copy-start.6
  17.1 292.8 %reduce-scatter.7.cloned.1.call-start = ((), (), s32[]{:S(2)}) async-start(), calls=%async_computation.5 | async-start | bytes 9437184 | tf_op jit(solution)/shard_map/reduce_scatter | solution.py:95
  132.4 8.3 %slice-start = ((s8[9437184]{0:T(1024)(128)(4,1)}), s8[1048576]{0:T(1024)(128)(4,1)S(1)}, s32[]{:S(2)}) async-start(s8[9437184]{0:T(1024)(128)(4,1)} %bitcast.157), calls=%async_computation.10 | async-start | bytes 2097152
  133.8 6.9 slice-start.1
  134.6 6.1 slice-start.2
  197.7 1.2 copy-start
  197.7 112.2 %copy-start.8 = (f32[256]{0:T(256)S(1)}, f32[256]{0:T(256)}, u32[]{:S(2)}) copy-start(f32[256]{0:T(256)} %param.12) | copy-start | bytes 3076
  197.7 112.2 %copy-start.9 = (f32[256]{0:T(256)S(1)}, f32[256]{0:T(256)}, u32[]{:S(2)}) copy-start(f32[256]{0:T(256)} %param.13) | copy-start | bytes 3076
  197.7 186.0 %all-gather.5.cloned.1.call-start = ((), (), s32[]{:S(2)}) async-start(), calls=%async_computation.8 | async-start | bytes 4718592 | tf_op jit(solution)/shard_map/all_gather | solution.py:80
  198.4 259.5 %all-gather.3.cloned.1.call-start = ((), (), s32[]{:S(2)}) async-start(), calls=%async_computation.6 | async-start | bytes 4718592 | tf_op jit(solution)/shard_map/all_gather | solution.py:96
  312.7 230.9 %reduce-scatter.11.cloned.1.call-start = ((), (), s32[]{:S(2)}) async-start(), calls=%async_computation.9 | async-start | bytes 6684672 | tf_op jit(solution)/shard_map/reduce_scatter | solution.py:87
  383.7 4.7 copy-start.5
  396.2 344.9 %reduce-scatter.9.cloned.1.call-start = ((), (), s32[]{:S(2)}) async-start(), calls=%async_computation.7 | async-start | bytes 20054016 | tf_op jit(solution)/shard_map/reduce_scatter | solution.py:110
  479.6 3.8 copy-start.4
  483.3 2.2 copy-start.3
  499.4 2.7 copy-start.2
  502.1 2.7 copy-start.7
Sparse Core Ops, SparseCore 0:
  17.2 115.2 reduce-scatter.4
  197.8 111.9 reduce-scatter.6
  312.0 71.5 all-gather.4
  386.3 71.6 all-gather.2
  460.8 73.3 reduce-scatter.10
  537.0 204.0 reduce-scatter.8
where the time goes:
time: 755 us; the launch traced here: 748 us
  waiting for transfers between devices  556 us (74%)
  matrix products  98.5 us (13%)
  local copies, waits for them, and re-layouts  30.2 us (4%)
  blocking collectives  26.8 us (4%)
  other arithmetic  21.2 us (3%)
  between operations  14.6 us (2%)
    reduce_scatter x1, waiting for transfers between devices, local(): lax.psum_scatter(spatial_local, 'dp', scatter_dimension=2, tiled=True)  198 us
    reduce_scatter x1, waiting for transfers between devices, local(): lax.psum_scatter(temporal_term, 'mp', scatter_dimension=1, tiled=True)  115 us
    reduce_scatter x1, waiting for transfers between devices, local(): lax.psum_scatter(spatial_term, 'mp', scatter_dimension=1, tiled=True)  110 us
    dot_general x12, matrix products, contract_cols(): lax.dot_general(left, right, (((1,), (1,)), ((), ())), preferred_element_...  71.5 us
    all_gather x1, waiting for transfers between devices, local(): saved_full = lax.all_gather(saved, 'mp', axis=1, tiled=True)  70.9 us
    all_gather x1, waiting for transfers between devices, local(): hidden_full = lax.all_gather(hidden, 'mp', axis=1, tiled=True)  61.7 us
    dot_general x12, matrix products, contract_rows(): lax.dot_general(left, right, (((0,), (0,)), ((), ())), preferred_element_...  27.1 us
    psum x1, blocking collectives, local(): lax.psum((jnp.sum(normed_grad * normed_hat, axis=0), jnp.sum(normed_grad,...  26.8 us
  transfers between devices with their start and end apart: 6, of which 5 were waited for; matrix products, arithmetic and copies ran while one was open for 10% of the time, Pallas kernels for 0%

commit v1 on v0

v1 whole, which is shorter than its diff:
```python
import itertools

import jax
import jax.numpy as jnp
from jax import lax
from jax.experimental import pallas as pl
from jax.experimental.pallas import tpu as pltpu
from jax.sharding import PartitionSpec as P

C = 2048
G = 32
FR = 16
HT = 8
WD = 8
EPSILON = 1e-05

ROWS = FR * HT * WD
CH = 256
SUB = 64
BF = jnp.bfloat16
F32 = jnp.float32
VMEM = 60 * 1024 * 1024


def linear(x, y, z, c):
    return (4 * y + 2 * (x % 2) + c) * 8 + 4 * (x // 2) + z


def send(value, to):
    pairs = []
    for x, y, z, c in itertools.product(range(4), range(4), range(4), range(2)):
        tx, ty, tz, tc = to(x, y, z, c)
        pairs.append((linear(x, y, z, c), linear(tx % 4, ty % 4, tz % 4, tc)))
    return lax.ppermute(value, ("dp", "mp"), pairs)


def to_z(step):
    return lambda x, y, z, c: (x, y, z + step, c)


def to_y(step):
    return lambda x, y, z, c: (x, y + step, z, c)


def to_core(x, y, z, c):
    return (x, y, z, 1 - c)


def to_half(x, y, z, c):
    return (x ^ 2, y, z, c)


def to_pair(x, y, z, c):
    return (x ^ 1, y, z, c)


def to_both(x, y, z, c):
    return (x ^ 3, y, z, c)


def to_pair_core(x, y, z, c):
    return (x ^ 1, y, z, 1 - c)


BLOCK_OF = ((0, 2, 1, 3), (1, 3, 0, 2))


def to_owner(flip):
    def to(x, y, z, c):
        half, pair = x // 2, x % 2
        block = BLOCK_OF[half][y]
        return (2 * (flip ^ c) + block % 2, 2 * half + block // 2, z, pair)

    return to


def contract_cols(left, right):
    return lax.dot_general(left, right, (((1,), (1,)), ((), ())), preferred_element_type=F32)


def contract_inner(left, right):
    return lax.dot_general(left, right, (((1,), (0,)), ((), ())), preferred_element_type=F32)


def params():
    return pltpu.CompilerParams(vmem_limit_bytes=VMEM)


def temporal_dgrad_body(index, mine, other, w_mine, w_other, out, padded):
    padded[pl.ds(0, 1)] = jnp.zeros((1, 64, 2 * CH), BF)
    padded[pl.ds(FR + 1, 1)] = jnp.zeros((1, 64, 2 * CH), BF)
    padded[pl.ds(1, FR), :, pl.ds(0, CH)] = mine[...]
    padded[pl.ds(1, FR), :, pl.ds(CH, CH)] = other[...]
    total = jnp.zeros((ROWS, CH), F32)
    for tap in range(3):
        rows = padded[pl.ds(2 - tap, FR)].reshape(ROWS, 2 * CH)
        weights = jnp.concatenate([w_mine[tap], w_other[:, tap].reshape(CH, CH)], axis=1)
        total = total + contract_cols(rows, weights)
    out[...] = total.astype(out.dtype)


def spatial_dgrad_body(index, mine, other, w_mine, w_other, out, padded):
    padded[...] = jnp.zeros(padded.shape, BF)
    padded[pl.ds(1, HT), pl.ds(1, WD), :, pl.ds(0, CH)] = mine[...]
    padded[pl.ds(1, HT), pl.ds(1, WD), :, pl.ds(CH, CH)] = other[...]
    total = jnp.zeros((ROWS, CH), F32)
    for tap in range(9):
        rows = padded[pl.ds(2 - tap // 3, HT), pl.ds(2 - tap % 3, WD)].reshape(ROWS, 2 * CH)
        weights = jnp.concatenate([w_mine[tap], w_other[:, tap].reshape(CH, CH)], axis=1)
        total = total + contract_cols(rows, weights)
    out[...] = total.astype(out.dtype)


def dgrad(body, pad_shape, taps, index, mine, other, w_mine, w_other, kind):
    whole = lambda shape: pl.BlockSpec(shape, lambda i, ix: (0,) * len(shape))
    return pl.pallas_call(
        body,
        grid_spec=pltpu.PrefetchScalarGridSpec(
            num_scalar_prefetch=1,
            grid=(1,),
            in_specs=[
                whole(mine.shape),
                whole(other.shape),
                pl.BlockSpec((taps, CH, CH), lambda i, ix: (0, ix[0], 0)),
                pl.BlockSpec((2, taps, CH // 2, CH), lambda i, ix: (ix[1], 0, 0, 0)),
            ],
            out_specs=whole((ROWS, CH)),
            scratch_shapes=[pltpu.VMEM(pad_shape, BF)],
        ),
        out_shape=jax.ShapeDtypeStruct((ROWS, CH), kind),
        compiler_params=params(),
        cost_estimate=pl.CostEstimate(
            flops=2 * taps * ROWS * 2 * CH * CH,
            bytes_accessed=2 * (4 * ROWS * CH + 2 * taps * CH * CH),
            transcendentals=0,
        ),
    )(index, mine, other, w_mine, w_other)


def wgrad_body(first, spatial, index, left, *refs):
    fields, (out, padded) = refs[:8], refs[8:]
    step = pl.program_id(0)

    @pl.when(step == 0)
    def _():
        padded[...] = jnp.zeros(padded.shape, BF)
        for clip in range(4):
            for side in range(2):
                cols = pl.ds(side * CH, CH)
                if spatial:
                    padded[clip, pl.ds(1, HT), pl.ds(1, WD), :, cols] = fields[2 * clip + side][...]
                else:
                    padded[clip, pl.ds(1, FR), :, cols] = fields[2 * clip + side][...]

    tap = step + first
    if spatial:
        right = padded[:, pl.ds(2 - tap // 3, HT), pl.ds(2 - tap % 3, WD)]
    else:
        right = padded[:, pl.ds(2 - tap, FR)]
    result = contract_inner(left[...].reshape(4 * SUB, 4 * ROWS), right.reshape(4 * ROWS, 2 * CH))
    result = result.astype(BF)
    for block in range(4):
        out[index[block], 0] = result[block * SUB : (block + 1) * SUB]


def wgrad(spatial, first, taps, index, left, fields):
    pad_shape = (4, HT + 2, WD + 2, FR, 2 * CH) if spatial else (4, FR + 2, HT * WD, 2 * CH)
    whole = lambda shape: pl.BlockSpec(shape, lambda i, ix: (0,) * len(shape))

    def body(*refs):
        wgrad_body(first, spatial, *refs)

    return pl.pallas_call(
        body,
        grid_spec=pltpu.PrefetchScalarGridSpec(
            num_scalar_prefetch=1,
            grid=(taps,),
            in_specs=[whole(left.shape)] + [whole(f.shape) for f in fields],
            out_specs=pl.BlockSpec((4, 1, SUB, 2 * CH), lambda i, ix: (0, i, 0, 0)),
            scratch_shapes=[pltpu.VMEM(pad_shape, BF)],
        ),
        out_shape=jax.ShapeDtypeStruct((4, taps, SUB, 2 * CH), BF),
        compiler_params=params(),
        cost_estimate=pl.CostEstimate(
            flops=2 * taps * 4 * ROWS * 4 * SUB * 2 * CH,
            bytes_accessed=2 * (4 * ROWS * 3 * CH + taps * CH * 2 * CH),
            transcendentals=0,
        ),
    )(index, left, *fields)


def per_group(values):
    return jnp.repeat(jnp.sum(values.reshape(-1, C // G), axis=1), C // G)


def local(
    block_input, spatial_out, cotangent, spatial_kernel, temporal_kernel, norm_gain, norm_bias
):
    dp, mp = lax.axis_index("dp"), lax.axis_index("mp")
    y, pair, core = dp // 4, (dp // 2) % 2, dp % 2
    half, z = mp // 4, mp % 4
    quarter = 2 * pair + core
    y_core_groups = [[4 * a + 2 * p + b for a in range(4) for b in range(2)] for p in range(2)]
    z_groups = [[0, 1, 2, 3], [4, 5, 6, 7]]

    cot = cotangent.reshape(FR, HT * WD, CH)
    spatial_kernel = spatial_kernel.reshape(9, C, CH)

    def other_kernel(kernel):
        start = (1 - half) * 1024 + y * 256 + core * 128
        part = lax.dynamic_slice_in_dim(kernel, start, 128, axis=1)
        part = send(part, to_half)
        return lax.all_gather(part, "dp", axis=0, axis_index_groups=y_core_groups)

    cot_other = send(cot, to_half)
    tk_other = other_kernel(temporal_kernel)
    sk_other = other_kernel(spatial_kernel)

    flat_in = block_input.reshape(FR, HT * WD, CH).transpose(1, 0, 2).reshape(ROWS, CH).astype(F32)
    count = ROWS * (C // G)
    center = per_group(jnp.sum(flat_in, axis=0)) / count
    spread = per_group(jnp.sum(jnp.square(flat_in - center), axis=0)) / count
    inverse = lax.rsqrt(spread + EPSILON)
    normed_hat = (flat_in - center) * inverse
    normed = normed_hat * norm_gain + norm_bias
    gate = jax.nn.sigmoid(normed)
    hidden = (normed * gate).astype(BF)

    def gather_left(flat):
        turned = flat.T.reshape(4, SUB, ROWS)
        pick = lambda k: lax.dynamic_index_in_dim(turned, quarter ^ k, 0, keepdims=False)
        parts = [pick(0), send(pick(1), to_core), send(pick(2), to_pair), send(pick(3), to_pair_core)]
        return lax.all_gather(
            jnp.concatenate(parts, axis=1), "mp", axis=0, axis_index_groups=z_groups
        )

    def gather_fields(mine, other):
        pair_mine, pair_other = send(mine, to_pair), send(mine, to_both)
        near, far = (mine, other), (pair_mine, pair_other)
        return (
            near
            + tuple(send(v, to_core) for v in near)
            + far
            + tuple(send(v, to_core) for v in far)
        )

    def scatter_z(call):
        parts = {}
        for k in (1, 3, 2, 0):
            to = (z + k) % 4
            index = jnp.stack([half * 4 + to, to]).astype(jnp.int32)
            part = call(index, F32 if k == 0 else BF)
            parts[k] = send(part, to_z(k)) if k else part
        return parts[0] + (parts[1].astype(F32) + parts[3].astype(F32)) + parts[2].astype(F32)

    saved_left = gather_left(spatial_out.reshape(ROWS, CH))
    hidden_left = gather_left(hidden)

    saved_grad = scatter_z(
        lambda index, kind: dgrad(
            temporal_dgrad_body,
            (FR + 2, HT * WD, 2 * CH),
            3,
            index,
            cot,
            cot_other,
            temporal_kernel,
            tk_other,
            kind,
        )
    ).astype(BF)
    saved_grad = saved_grad.reshape(FR, HT * WD, CH).transpose(1, 0, 2).reshape(HT, WD, FR, CH)
    sg_other = send(saved_grad, to_half)

    hidden_grad = scatter_z(
        lambda index, kind: dgrad(
            spatial_dgrad_body,
            (HT + 2, WD + 2, FR, 2 * CH),
            9,
            index,
            saved_grad,
            sg_other,
            spatial_kernel,
            sk_other,
            kind,
        )
    )

    slots = jnp.array([[0, 2, 1, 3], [2, 0, 3, 1]], jnp.int32)[half]
    order = (slots - y) % 4

    def kernel_grad(spatial, first, taps, left, fields):
        parts = wgrad(spatial, first, taps, order, left, fields)
        total = parts[0].astype(F32)
        for k in (1, 3, 2):
            total = total + send(parts[k], to_y(k)).astype(F32)
        total = total.astype(BF)
        mine, other = total[:, :, :CH], total[:, :, CH:]
        same = (half == core)
        got = [
            send(jnp.where(same, mine, other), to_owner(0)),
            send(jnp.where(same, other, mine), to_owner(1)),
        ]
        low = jnp.where(half == 0, got[0], got[1])
        high = jnp.where(half == 0, got[1], got[0])
        return jnp.concatenate([low, high], axis=1).astype(F32)

    cot_fields = gather_fields(cot, cot_other)
    temporal_grad = kernel_grad(False, 0, 3, saved_left, cot_fields)
    sg_fields = gather_fields(saved_grad, sg_other)
    spatial_grad = jnp.stack(
        [kernel_grad(True, 3 * row, 3, hidden_left, sg_fields) for row in range(3)]
    )

    normed_grad = hidden_grad * gate * (1.0 + normed * (1.0 - gate))
    gain_sum = jnp.sum(normed_grad * normed_hat, axis=0)
    bias_sum = jnp.sum(normed_grad, axis=0)
    first = per_group(bias_sum * norm_gain) / count
    second = per_group(gain_sum * norm_gain) / count
    branch = inverse * (normed_grad * norm_gain - first - normed_hat * second)
    branch = branch.reshape(HT * WD, FR, CH).transpose(1, 0, 2)
    input_grad = (cot.astype(F32) + branch).astype(BF).reshape(block_input.shape)

    sums = jnp.stack([gain_sum, bias_sum])
    for to in (to_core, to_pair, to_y(2)):
        sums = sums + send(sums, to)
    sums = sums + send(sums, to_y(1))
    return (input_grad, spatial_grad, temporal_grad, sums[0], sums[1])


def solution(mesh):
    placed = (
        P("dp", None, None, None, "mp"),
        P("dp", None, None, None, "mp"),
        P("dp", None, None, None, "mp"),
        P(None, None, None, "mp"),
        P(None, None, "mp"),
        P("mp"),
        P("mp"),
    )
    return jax.shard_map(
        local,
        mesh=mesh,
        in_specs=placed,
        out_specs=(
            P("dp", None, None, None, "mp"),
            P(None, None, "dp", "mp"),
            P(None, "dp", "mp"),
            P("mp"),
            P("mp"),
        ),
        check_vma=False,
    )
```

time: 755 us -> 283 us (0.37)
  waiting for transfers between devices: 556 us -> 88.3 us
  matrix products: 98.5 us -> 0 us
  Pallas kernels: 0 us -> 74.4 us
  starting transfers between devices: 0.83 us -> 71.1 us
  blocking collectives: 26.8 us -> 0 us
  local copies, waits for them, and re-layouts: 30.2 us -> 13.2 us
    reduce_scatter x4 -> x0, waiting for transfers between devices: 423 us -> none  [the longest x1 198 us: local(): lax.psum_scatter(spatial_local, 'dp', scatter_dimension=2, tiled=True)]
    all_gather x2 -> x4, waiting for transfers between devices: 133 us -> 0.04 us  [the longest x2 0.02 us: other_kernel(): return lax.all_gather(part, 'dp', axis=0, axis_index_groups=y_core_groups)]
    dot_general x24 -> x0, matrix products: 98.5 us -> none  [the longest x12 71.5 us: contract_cols(): lax.dot_general(left, right, (((1,), (1,)), ((), ())), preferred_element_...]
    ppermute x0 -> x52, waiting for transfers between devices: none -> 88.2 us  [send(): return lax.ppermute(value, ('dp', 'mp'), pairs)]
    pallas_call x0 -> x12, Pallas kernels: none -> 74.4 us  [the longest x8 40.6 us: dgrad(): pl.pallas_call(body, grid_spec=pltpu.PrefetchScalarGridSpec(num_scalar_pr...]
    ppermute x0 -> x52, starting transfers between devices: none -> 70.9 us  [send(): return lax.ppermute(value, ('dp', 'mp'), pairs)]
    psum x1 -> x0, blocking collectives: 26.8 us -> none  [local(): lax.psum((jnp.sum(normed_grad * normed_hat, axis=0), jnp.sum(normed_grad,...]
    slice x3 -> x1, local copies, waits for them, and re-layouts: 23.6 us -> 0.57 us  [local(): return (input_grad, spatial_grad, temporal_grad, sums[0], sums[1])]
  transfers between devices with their start and end apart: 6 -> 56, of which waited for: 5 -> 18; matrix products, arithmetic and copies ran while one was open for 10% -> 8% of each run, Pallas kernels for 0% -> 24%
where the time goes in v1:
time: 283 us; the launch traced here: 280 us
  waiting for transfers between devices  88.3 us (31%)
  Pallas kernels  74.4 us (26%)
  starting transfers between devices  71.1 us (25%)
  other arithmetic  18.8 us (7%)
  between operations  14.4 us (5%)
  local copies, waits for them, and re-layouts  13.2 us (5%)
    ppermute x52, waiting for transfers between devices, send(): return lax.ppermute(value, ('dp', 'mp'), pairs)  88.2 us
    ppermute x52, starting transfers between devices, send(): return lax.ppermute(value, ('dp', 'mp'), pairs)  70.9 us
    pallas_call x8, Pallas kernels, dgrad(): pl.pallas_call(body, grid_spec=pltpu.PrefetchScalarGridSpec(num_scalar_pr...  40.6 us
    pallas_call x4, Pallas kernels, wgrad(): pl.pallas_call(body, grid_spec=pltpu.PrefetchScalarGridSpec(num_scalar_pr...  33.8 us
  transfers between devices with their start and end apart: 56, of which 18 were waited for; matrix products, arithmetic and copies ran while one was open for 8% of the time, Pallas kernels for 24%

profile of v1, /device:TPU:6, one launch (start us, length us, event | category | flops | bytes accessed | tf_op | source)
XLA Modules:
  0.0 280.2 jit_solution(6681760692611989003)
XLA Ops:
  9.8 6.7 %collective-permute-done.1 = bf16[3,128,256]{2,1,0:T(8,128)(2,1)S(1)} collective-permute-done((bf16[3,128,256]{2,1,0:T(8,128)(2,1)S(1)}, bf16[3,128,256]{2,1,0:T(8,128)(2,1)S(1)}, u32[]{:S(2)}, u32[]{:S(2)}) %collective-permute-start.1) | collective-permute-done | bytes 196640 | tf_op jit(solution)/shard_map/ppermute | solution.py:34
  19.9 14.3 %collective-permute-done.6 = bf16[9,128,256]{2,1,0:T(8,128)(2,1)S(1)} collective-permute-done((bf16[9,128,256]{2,1,0:T(8,128)(2,1)S(1)}, bf16[9,128,256]{2,1,0:T(8,128)(2,1)S(1)}, u32[]{:S(2)}, u32[]{:S(2)}) %collective-permute-start.6) | collective-permute-done | bytes 589856 | tf_op jit(solution)/shard_map/ppermute | solution.py:34
  37.3 3.9 %collective-permute-done.36 = bf16[64,1024]{1,0:T(8,128)(2,1)S(1)} collective-permute-done((bf16[64,1024]{1,0:T(8,128)(2,1)S(1)}, bf16[64,1024]{1,0:T(8,128)(2,1)S(1)}, u32[]{:S(2)}, u32[]{:S(2)}) %collective-permute-start.36) | collective-permute-done | bytes 131104 | tf_op jit(solution)/shard_map/ppermute | solution.py:34
  41.2 1.7 collective-permute-done.35
  47.8 12.5 %collective-permute-done.other.refs_3_ = bf16[16,64,256]{2,1,0:T(8,128)(2,1)S(1)} collective-permute-done((bf16[16,64,256]{2,1,0:T(8,128)(2,1)}, bf16[16,64,256]{2,1,0:T(8,128)(2,1)S(1)}, u32[]{:S(2)}, u32[]{:S(2)}) %collective-permute-start) | collective-permute-done | bytes 524320 | tf_op jit(solution)/shard_map/ppermute | solution.py:34
  61.2 4.0 %shard_map.122 = bf16[1024,256]{1,0:T(8,128)(2,1)} custom-call(s32[2]{0:T(128)} %pad_add_fusion.3.index, bf16[16,64,256]{2,1,0:T(8,128)(2,1)} %bitcast.mine.refs_2_, bf16[16,64,256]{2,1,0:T(8,128)(2,1)} %copy-done.4, bf16[3,2048,256]{2,1,0:T(8,128)(2,1)} %w_mine.7, bf16[8,3,128,256]{3,2,1,0:T(8,128)(2,1)} %bitcast.142), custom_call_target="tpu_custom_call" | custom-call | flops 805306368 | bytes 2883584 | tf_op jit(solution)/shard_map/pallas_call | solution.py:116
  65.2 3.8 %collective-permute-start.4 = (bf16[1024,256]{1,0:T(8,128)(2,1)}, bf16[1024,256]{1,0:T(8,128)(2,1)S(1)}, u32[]{:S(2)}, u32[]{:S(2)}) collective-permute-start(bf16[1024,256]{1,0:T(8,128)(2,1)} %shard_map.122), channel_id=1, source_target_pairs={{0,2},{8,10},{1,3},{9,11},{2,0},{10,8},{3,1},{11,9},{32,34},{40,42... | collective-permute-start | bytes 1572872 | tf_op jit(solution)/shard_map/ppermute | solution.py:34
  69.0 4.0 %shard_map.121 = bf16[1024,256]{1,0:T(8,128)(2,1)} custom-call(s32[2]{0:T(128)} %get-tuple-element.50.index, bf16[16,64,256]{2,1,0:T(8,128)(2,1)} %bitcast.mine.refs_2_, bf16[16,64,256]{2,1,0:T(8,128)(2,1)} %copy-done.4, bf16[3,2048,256]{2,1,0:T(8,128)(2,1)} %w_mine.7, bf16[8,3,128,256]{3,2,1,0:T(8,128)(2,1)} %bitcast.143), custom_call_target="tpu_custom_call" | custom-call | flops 805306368 | bytes 2883584 | tf_op jit(solution)/shard_map/pallas_call | solution.py:116
  73.6 4.0 %shard_map.120 = bf16[1024,256]{1,0:T(8,128)(2,1)} custom-call(s32[2]{0:T(128)} %get-tuple-element.49.index, bf16[16,64,256]{2,1,0:T(8,128)(2,1)} %bitcast.mine.refs_2_, bf16[16,64,256]{2,1,0:T(8,128)(2,1)} %copy-done.4, bf16[3,2048,256]{2,1,0:T(8,128)(2,1)} %w_mine.7, bf16[8,3,128,256]{3,2,1,0:T(8,128)(2,1)} %bitcast.144), custom_call_target="tpu_custom_call" | custom-call | flops 805306368 | bytes 2883584 | tf_op jit(solution)/shard_map/pallas_call | solution.py:116
  80.1 4.1 %shard_map.119 = f32[1024,256]{1,0:T(8,128)} custom-call(s32[2]{0:T(128)} %pad_add_fusion.index, bf16[16,64,256]{2,1,0:T(8,128)(2,1)} %bitcast.mine.refs_2_, bf16[16,64,256]{2,1,0:T(8,128)(2,1)} %copy-done.4, bf16[3,2048,256]{2,1,0:T(8,128)(2,1)} %w_mine.7, bf16[8,3,128,256]{3,2,1,0:T(8,128)(2,1)} %bitcast.145), custom_call_target="tpu_custom_call" | custom-call | flops 805306368 | bytes 2883584 | tf_op jit(solution)/shard_map/pallas_call | solution.py:116
  84.2 1.6 collective-permute-start.40
  85.7 6.6 %collective-permute-done.3 = bf16[1024,256]{1,0:T(8,128)(2,1)S(1)} collective-permute-done((bf16[1024,256]{1,0:T(8,128)(2,1)}, bf16[1024,256]{1,0:T(8,128)(2,1)S(1)}, u32[]{:S(2)}, u32[]{:S(2)}) %collective-permute-start.3) | collective-permute-done | bytes 524320 | tf_op jit(solution)/shard_map/ppermute | solution.py:34
  92.3 1.5 add_convert_fusion
  94.2 1.6 collective-permute-start.5
  97.8 11.1 %collective-permute-done.40.refs_7_ = bf16[16,64,256]{2,1,0:T(8,128)(2,1)} collective-permute-done((bf16[16,64,256]{2,1,0:T(8,128)(2,1)}, bf16[16,64,256]{2,1,0:T(8,128)(2,1)}, u32[]{:S(2)}, u32[]{:S(2)}) %collective-permute-start.40) | collective-permute-done | bytes 524320 | tf_op jit(solution)/shard_map/ppermute | solution.py:34
  109.7 6.0 %shard_map.126 = bf16[1024,256]{1,0:T(8,128)(2,1)} custom-call(s32[2]{0:T(128)} %pad_add_fusion.3.index, bf16[8,8,16,256]{3,2,1,0:T(8,128)(2,1)} %bitcast.147, bf16[8,8,16,256]{3,2,1,0:T(8,128)(2,1)} %copy-done.2, bf16[9,2048,256]{2,1,0:T(8,128)(2,1)} %bitcast.134, bf16[8,9,128,256]{3,2,1,0:T(8,128)(2,1)} %bitcast.138), custom_call_target="tpu_custom_call" | custom-call | flops 2415919104 | bytes 4456448 | tf_op jit(solution)/shard_map/pallas_call | solution.py:116
  115.8 2.3 collective-permute-start.9
  118.1 6.0 %shard_map.125 = bf16[1024,256]{1,0:T(8,128)(2,1)} custom-call(s32[2]{0:T(128)} %get-tuple-element.50.index, bf16[8,8,16,256]{3,2,1,0:T(8,128)(2,1)} %bitcast.148, bf16[8,8,16,256]{3,2,1,0:T(8,128)(2,1)} %copy-done.2, bf16[9,2048,256]{2,1,0:T(8,128)(2,1)} %bitcast.135, bf16[8,9,128,256]{3,2,1,0:T(8,128)(2,1)} %bitcast.139), custom_call_target="tpu_custom_call" | custom-call | flops 2415919104 | bytes 4456448 | tf_op jit(solution)/shard_map/pallas_call | solution.py:116
  124.1 6.2 %shard_map.124 = bf16[1024,256]{1,0:T(8,128)(2,1)} custom-call(s32[2]{0:T(128)} %get-tuple-element.49.index, bf16[8,8,16,256]{3,2,1,0:T(8,128)(2,1)} %bitcast.149, bf16[8,8,16,256]{3,2,1,0:T(8,128)(2,1)} %copy-done.2, bf16[9,2048,256]{2,1,0:T(8,128)(2,1)} %bitcast.136, bf16[8,9,128,256]{3,2,1,0:T(8,128)(2,1)} %bitcast.140), custom_call_target="tpu_custom_call" | custom-call | flops 2415919104 | bytes 4456448 | tf_op jit(solution)/shard_map/pallas_call | solution.py:116
  130.3 1.7 collective-permute-start.8
  132.3 8.4 %shard_map.130 = bf16[4,3,64,512]{3,2,1,0:T(8,128)(2,1)} custom-call(s32[4]{0:T(128)} %and_select_fusion.refs_0_, bf16[4,64,4096]{2,1,0:T(8,128)(2,1)} %bitcast.171, bf16[16,64,256]{2,1,0:T(8,128)(2,1)} %bitcast.mine.refs_2_, bf16[16,64,256]{2,1,0:T(8,128)(2,1)} %copy-done.4, bf16[16,64,256]{2,1,0:T(8,128)(2,1)} %collective-permute-done.37.refs_4_, ...), custom_call_target="tpu_custom_call" | custom-call | flops 3221225472 | bytes 7077888 | tf_op jit(solution)/shard_map/pallas_call | solution.py:173
  140.7 6.3 %shard_map.123 = f32[1024,256]{1,0:T(8,128)} custom-call(s32[2]{0:T(128)} %pad_add_fusion.index, bf16[8,8,16,256]{3,2,1,0:T(8,128)(2,1)} %bitcast.150, bf16[8,8,16,256]{3,2,1,0:T(8,128)(2,1)} %copy-done.2, bf16[9,2048,256]{2,1,0:T(8,128)(2,1)} %bitcast.137, bf16[8,9,128,256]{3,2,1,0:T(8,128)(2,1)} %bitcast.141), custom_call_target="tpu_custom_call" | custom-call | flops 2415919104 | bytes 4456448 | tf_op jit(solution)/shard_map/pallas_call | solution.py:116
  147.9 2.4 fusion.19
  153.2 3.3 %collective-permute-start.45 = (bf16[3,64,512]{2,1,0:T(8,128)(2,1)}, bf16[3,64,512]{2,1,0:T(8,128)(2,1)}, u32[]{:S(2)}, u32[]{:S(2)}) collective-permute-start(bf16[3,64,512]{2,1,0:T(8,128)(2,1)} %get-tuple-element.10), channel_id=1, source_target_pairs={{0,64},{8,72},{1,65},{9,73},{2,66},{10,74},{3,67},{11,75},{32,96},... | collective-permute-start | bytes 589832 | tf_op jit(solution)/shard_map/ppermute | solution.py:34
  162.7 3.7 %collective-permute-done.44 = bf16[3,64,512]{2,1,0:T(8,128)(2,1)} collective-permute-done((bf16[3,64,512]{2,1,0:T(8,128)(2,1)S(1)}, bf16[3,64,512]{2,1,0:T(8,128)(2,1)}, u32[]{:S(2)}, u32[]{:S(2)}) %collective-permute-start.44) | collective-permute-done | bytes 196640 | tf_op jit(solution)/shard_map/ppermute | solution.py:34
  167.8 5.6 %collective-permute-start.46 = (bf16[3,64,256]{2,1,0:T(8,128)(2,1)S(1)}, bf16[3,64,256]{2,1,0:T(8,128)(2,1)S(1)}, u32[]{:S(2)}, u32[]{:S(2)}) collective-permute-start(bf16[3,64,256]{2,1,0:T(8,128)(2,1)S(1)} %get-tuple-element.31), channel_id=1, source_target_pairs={{0,0},{8,4},{1,1},{9,5},{2,2},{10,6},{3,3},{11,7},{32,32},{40,36},... | collective-permute-start | bytes 294920 | tf_op jit(solution)/shard_map/ppermute | solution.py:34
  173.4 1.9 collective-permute-start.47
  176.3 4.3 %collective-permute-done.46 = bf16[3,64,256]{2,1,0:T(8,128)(2,1)S(1)} collective-permute-done((bf16[3,64,256]{2,1,0:T(8,128)(2,1)S(1)}, bf16[3,64,256]{2,1,0:T(8,128)(2,1)S(1)}, u32[]{:S(2)}, u32[]{:S(2)}) %collective-permute-start.46) | collective-permute-done | bytes 98336 | tf_op jit(solution)/shard_map/ppermute | solution.py:34
  180.5 3.0 %collective-permute-done.47 = bf16[3,64,256]{2,1,0:T(8,128)(2,1)S(1)} collective-permute-done((bf16[3,64,256]{2,1,0:T(8,128)(2,1)S(1)}, bf16[3,64,256]{2,1,0:T(8,128)(2,1)S(1)}, u32[]{:S(2)}, u32[]{:S(2)}) %collective-permute-start.47) | collective-permute-done | bytes 98336 | tf_op jit(solution)/shard_map/ppermute | solution.py:34
  187.6 3.3 %collective-permute-done.49 = f32[2,256]{1,0:T(2,128)S(1)} collective-permute-done((f32[2,256]{1,0:T(2,128)S(1)}, f32[2,256]{1,0:T(2,128)S(1)}, u32[]{:S(2)}, u32[]{:S(2)}) %collective-permute-start.49) | collective-permute-done | bytes 2080 | tf_op jit(solution)/shard_map/ppermute | solution.py:34
  191.9 4.1 %collective-permute-done.50 = f32[2,256]{1,0:T(2,128)S(1)} collective-permute-done((f32[2,256]{1,0:T(2,128)S(1)}, f32[2,256]{1,0:T(2,128)S(1)}, u32[]{:S(2)}, u32[]{:S(2)}) %collective-permute-start.50) | collective-permute-done | bytes 2080 | tf_op jit(solution)/shard_map/ppermute | solution.py:34
  196.9 2.4 fusion.2
  199.3 1.5 collective-permute-done.51
  201.5 8.5 %shard_map.129 = bf16[4,3,64,512]{3,2,1,0:T(8,128)(2,1)} custom-call(s32[4]{0:T(128)} %and_select_fusion.refs_0_, bf16[4,64,4096]{2,1,0:T(8,128)(2,1)} %bitcast.172, bf16[8,8,16,256]{3,2,1,0:T(8,128)(2,1)} %bitcast.151, bf16[8,8,16,256]{3,2,1,0:T(8,128)(2,1)} %copy-done.2, bf16[8,8,16,256]{3,2,1,0:T(8,128)(2,1)} %collective-permute-done.13.refs_4_, ...), custom_call_target="tpu_custom_call" | custom-call | flops 3221225472 | bytes 7077888 | tf_op jit(solution)/shard_map/pallas_call | solution.py:173
  211.2 2.3 collective-permute-start.30
  213.6 8.5 %shard_map.128 = bf16[4,3,64,512]{3,2,1,0:T(8,128)(2,1)} custom-call(s32[4]{0:T(128)} %and_select_fusion.refs_0_, bf16[4,64,4096]{2,1,0:T(8,128)(2,1)} %bitcast.173, bf16[8,8,16,256]{3,2,1,0:T(8,128)(2,1)} %bitcast.152, bf16[8,8,16,256]{3,2,1,0:T(8,128)(2,1)} %copy-done.2, bf16[8,8,16,256]{3,2,1,0:T(8,128)(2,1)} %collective-permute-done.13.refs_4_, ...), custom_call_target="tpu_custom_call" | custom-call | flops 3221225472 | bytes 7077888 | tf_op jit(solution)/shard_map/pallas_call | solution.py:173
  223.2 3.3 %collective-permute-start.26 = (bf16[3,64,512]{2,1,0:T(8,128)(2,1)S(1)}, bf16[3,64,512]{2,1,0:T(8,128)(2,1)S(1)}, u32[]{:S(2)}, u32[]{:S(2)}) collective-permute-start(bf16[3,64,512]{2,1,0:T(8,128)(2,1)S(1)} %get-tuple-element.16), channel_id=1, source_target_pairs={{0,64},{8,72},{1,65},{9,73},{2,66},{10,74},{3,67},{11,75},{32,96},... | collective-permute-start | bytes 589832 | tf_op jit(solution)/shard_map/ppermute | solution.py:34
  227.4 8.5 %shard_map.127 = bf16[4,3,64,512]{3,2,1,0:T(8,128)(2,1)} custom-call(s32[4]{0:T(128)} %and_select_fusion.refs_0_, bf16[4,64,4096]{2,1,0:T(8,128)(2,1)} %bitcast.174, bf16[8,8,16,256]{3,2,1,0:T(8,128)(2,1)} %bitcast.153, bf16[8,8,16,256]{3,2,1,0:T(8,128)(2,1)} %copy-done.2, bf16[8,8,16,256]{3,2,1,0:T(8,128)(2,1)} %collective-permute-done.13.refs_4_, ...), custom_call_target="tpu_custom_call" | custom-call | flops 3221225472 | bytes 7077888 | tf_op jit(solution)/shard_map/pallas_call | solution.py:173
  239.3 2.5 collective-permute-start.20
  243.0 1.9 collective-permute-start.32
  244.9 4.1 %collective-permute-done.24 = bf16[3,64,512]{2,1,0:T(8,128)(2,1)S(1)} collective-permute-done((bf16[3,64,512]{2,1,0:T(8,128)(2,1)S(1)}, bf16[3,64,512]{2,1,0:T(8,128)(2,1)S(1)}, u32[]{:S(2)}, u32[]{:S(2)}) %collective-permute-start.24) | collective-permute-done | bytes 196640 | tf_op jit(solution)/shard_map/ppermute | solution.py:34
  249.0 1.9 collective-permute-start.33
  252.0 1.9 collective-permute-start.27
  254.0 3.4 %collective-permute-start.28 = (bf16[3,64,256]{2,1,0:T(8,128)(2,1)S(1)}, bf16[3,64,256]{2,1,0:T(8,128)(2,1)S(1)}, u32[]{:S(2)}, u32[]{:S(2)}) collective-permute-start(bf16[3,64,256]{2,1,0:T(8,128)(2,1)S(1)} %get-tuple-element.40), channel_id=1, source_target_pairs={{0,4},{8,0},{1,5},{9,1},{2,6},{10,2},{3,7},{11,3},{32,36},{40,32},... | collective-permute-start | bytes 294920 | tf_op jit(solution)/shard_map/ppermute | solution.py:34
  258.5 3.9 %collective-permute-start.22 = (bf16[3,64,256]{2,1,0:T(8,128)(2,1)S(1)}, bf16[3,64,256]{2,1,0:T(8,128)(2,1)S(1)}, u32[]{:S(2)}, u32[]{:S(2)}) collective-permute-start(bf16[3,64,256]{2,1,0:T(8,128)(2,1)S(1)} %get-tuple-element.35), channel_id=1, source_target_pairs={{0,0},{8,4},{1,1},{9,5},{2,2},{10,6},{3,3},{11,7},{32,32},{40,36},... | collective-permute-start | bytes 294920 | tf_op jit(solution)/shard_map/ppermute | solution.py:34
  262.4 4.9 %collective-permute-start.23 = (bf16[3,64,256]{2,1,0:T(8,128)(2,1)S(1)}, bf16[3,64,256]{2,1,0:T(8,128)(2,1)S(1)}, u32[]{:S(2)}, u32[]{:S(2)}) collective-permute-start(bf16[3,64,256]{2,1,0:T(8,128)(2,1)S(1)} %get-tuple-element.36), channel_id=1, source_target_pairs={{0,4},{8,0},{1,5},{9,1},{2,6},{10,2},{3,7},{11,3},{32,36},{40,32},... | collective-permute-start | bytes 294920 | tf_op jit(solution)/shard_map/ppermute | solution.py:34
  267.4 1.7 collective-permute-done.22
  269.1 3.5 %collective-permute-done.23 = bf16[3,64,256]{2,1,0:T(8,128)(2,1)S(1)} collective-permute-done((bf16[3,64,256]{2,1,0:T(8,128)(2,1)S(1)}, bf16[3,64,256]{2,1,0:T(8,128)(2,1)S(1)}, u32[]{:S(2)}, u32[]{:S(2)}) %collective-permute-start.23) | collective-permute-done | bytes 98336 | tf_op jit(solution)/shard_map/ppermute | solution.py:34
  (180 shorter events, 51.2 us)
Async XLA Ops:
  7.2 53.2 %all-gather.9.cloned.1.call-start = ((), (), s32[]{:S(2)}) async-start(), calls=%async_computation | async-start | bytes 1769472 | tf_op jit(solution)/shard_map/all_gather | solution.py:213
  8.3 8.2 %collective-permute-start.1 = (bf16[3,128,256]{2,1,0:T(8,128)(2,1)S(1)}, bf16[3,128,256]{2,1,0:T(8,128)(2,1)S(1)}, u32[]{:S(2)}, u32[]{:S(2)}) collective-permute-start(bf16[3,128,256]{2,1,0:T(8,128)(2,1)S(1)} %constant_dynamic-slice_fusion.2), channel_id=1, source_target_pairs={{0,4},{8,12},{1,5},{9,13},{2,6},{10,14},{3,7},{11,15},{32,36},{40,... | collective-permute-start | bytes 589832 | tf_op jit(solution)/shard_map/ppermute | solution.py:34
  17.2 91.8 %all-gather.11.cloned.1.call-start = ((), (), s32[]{:S(2)}) async-start(), calls=%async_computation.1 | async-start | bytes 5308416 | tf_op jit(solution)/shard_map/all_gather | solution.py:213
  18.4 15.8 %collective-permute-start.6 = (bf16[9,128,256]{2,1,0:T(8,128)(2,1)S(1)}, bf16[9,128,256]{2,1,0:T(8,128)(2,1)S(1)}, u32[]{:S(2)}, u32[]{:S(2)}) collective-permute-start(bf16[9,128,256]{2,1,0:T(8,128)(2,1)S(1)} %constant_dynamic-slice_fusion.1), channel_id=1, source_target_pairs={{0,4},{8,12},{1,5},{9,13},{2,6},{10,14},{3,7},{11,15},{32,36},{40,... | collective-permute-start | bytes 1769480 | tf_op jit(solution)/shard_map/ppermute | solution.py:34
  35.0 97.3 %all-gather.15.cloned.1.call-start = ((), (), s32[]{:S(2)}) async-start(), calls=%async_computation.3 | async-start | bytes 2621440 | tf_op jit(solution)/shard_map/all_gather | solution.py:233
  35.5 7.4 %collective-permute-start.35 = (bf16[64,1024]{1,0:T(8,128)(2,1)S(1)}, bf16[64,1024]{1,0:T(8,128)(2,1)S(1)}, u32[]{:S(2)}, u32[]{:S(2)}) collective-permute-start(bf16[64,1024]{1,0:T(8,128)(2,1)S(1)} %get-tuple-element.23), channel_id=1, source_target_pairs={{0,16},{8,24},{1,17},{9,25},{2,18},{10,26},{3,19},{11,27},{32,48},... | collective-permute-start | bytes 393224 | tf_op jit(solution)/shard_map/ppermute | solution.py:34
  43.8 157.7 %all-gather.13.cloned.1.call-start = ((), (), s32[]{:S(2)}) async-start(), calls=%async_computation.2 | async-start | bytes 2621440 | tf_op jit(solution)/shard_map/all_gather | solution.py:233
  43.8 16.6 %collective-permute-start = (bf16[16,64,256]{2,1,0:T(8,128)(2,1)}, bf16[16,64,256]{2,1,0:T(8,128)(2,1)S(1)}, u32[]{:S(2)}, u32[]{:S(2)}) collective-permute-start(bf16[16,64,256]{2,1,0:T(8,128)(2,1)} %bitcast.mine.refs_2_), channel_id=1, source_target_pairs={{0,4},{8,12},{1,5},{9,13},{2,6},{10,14},{3,7},{11,15},{32,36},{40,... | collective-permute-start | bytes 1572872 | tf_op jit(solution)/shard_map/ppermute | solution.py:34
  44.3 86.0 %collective-permute-start.37 = (bf16[16,64,256]{2,1,0:T(8,128)(2,1)}, bf16[16,64,256]{2,1,0:T(8,128)(2,1)}, u32[]{:S(2)}, u32[]{:S(2)}) collective-permute-start(bf16[16,64,256]{2,1,0:T(8,128)(2,1)} %bitcast.mine.refs_2_), channel_id=1, source_target_pairs={{0,8},{8,0},{1,9},{9,1},{2,10},{10,2},{3,11},{11,3},{32,40},{40,32... | collective-permute-start | bytes 1572872 | tf_op jit(solution)/shard_map/ppermute | solution.py:34
  44.9 52.4 %collective-permute-start.39 = (bf16[16,64,256]{2,1,0:T(8,128)(2,1)}, bf16[16,64,256]{2,1,0:T(8,128)(2,1)}, u32[]{:S(2)}, u32[]{:S(2)}) collective-permute-start(bf16[16,64,256]{2,1,0:T(8,128)(2,1)} %bitcast.mine.refs_2_), channel_id=1, source_target_pairs={{0,16},{8,24},{1,17},{9,25},{2,18},{10,26},{3,19},{11,27},{32,48},... | collective-permute-start | bytes 1572872 | tf_op jit(solution)/shard_map/ppermute | solution.py:34
  65.2 19.0 %collective-permute-start.4 = (bf16[1024,256]{1,0:T(8,128)(2,1)}, bf16[1024,256]{1,0:T(8,128)(2,1)S(1)}, u32[]{:S(2)}, u32[]{:S(2)}) collective-permute-start(bf16[1024,256]{1,0:T(8,128)(2,1)} %shard_map.122), channel_id=1, source_target_pairs={{0,2},{8,10},{1,3},{9,11},{2,0},{10,8},{3,1},{11,9},{32,34},{40,42... | collective-permute-start | bytes 1572872 | tf_op jit(solution)/shard_map/ppermute | solution.py:34
  72.9 19.4 %collective-permute-start.3 = (bf16[1024,256]{1,0:T(8,128)(2,1)}, bf16[1024,256]{1,0:T(8,128)(2,1)S(1)}, u32[]{:S(2)}, u32[]{:S(2)}) collective-permute-start(bf16[1024,256]{1,0:T(8,128)(2,1)} %shard_map.121), channel_id=1, source_target_pairs={{0,3},{8,11},{1,0},{9,8},{2,1},{10,9},{3,2},{11,10},{32,35},{40,43... | collective-permute-start | bytes 1572872 | tf_op jit(solution)/shard_map/ppermute | solution.py:34
  77.5 14.8 %collective-permute-start.2 = (bf16[1024,256]{1,0:T(8,128)(2,1)}, bf16[1024,256]{1,0:T(8,128)(2,1)S(1)}, u32[]{:S(2)}, u32[]{:S(2)}) collective-permute-start(bf16[1024,256]{1,0:T(8,128)(2,1)} %shard_map.120), channel_id=1, source_target_pairs={{0,1},{8,9},{1,2},{9,10},{2,3},{10,11},{3,0},{11,8},{32,33},{40,41... | collective-permute-start | bytes 1572872 | tf_op jit(solution)/shard_map/ppermute | solution.py:34
  84.2 24.8 %collective-permute-start.40 = (bf16[16,64,256]{2,1,0:T(8,128)(2,1)}, bf16[16,64,256]{2,1,0:T(8,128)(2,1)}, u32[]{:S(2)}, u32[]{:S(2)}) collective-permute-start(bf16[16,64,256]{2,1,0:T(8,128)(2,1)} %bitcast.mine.refs_2_), channel_id=1, source_target_pairs={{0,20},{8,28},{1,21},{9,29},{2,22},{10,30},{3,23},{11,31},{32,52},... | collective-permute-start | bytes 1572872 | tf_op jit(solution)/shard_map/ppermute | solution.py:34
  94.2 14.8 %collective-permute-start.5 = (bf16[8,8,16,256]{3,2,1,0:T(8,128)(2,1)S(1)}, bf16[8,8,16,256]{3,2,1,0:T(8,128)(2,1)S(1)}, u32[]{:S(2)}, u32[]{:S(2)}) collective-permute-start(bf16[8,8,16,256]{3,2,1,0:T(8,128)(2,1)S(1)} %bitcast.146), channel_id=1, source_target_pairs={{0,4},{8,12},{1,5},{9,13},{2,6},{10,14},{3,7},{11,15},{32,36},{40,... | collective-permute-start | bytes 1572872 | tf_op jit(solution)/shard_map/ppermute | solution.py:34
  97.3 34.7 %collective-permute-start.38 = (bf16[16,64,256]{2,1,0:T(8,128)(2,1)S(1)}, bf16[16,64,256]{2,1,0:T(8,128)(2,1)}, u32[]{:S(2)}, u32[]{:S(2)}) collective-permute-start(bf16[16,64,256]{2,1,0:T(8,128)(2,1)S(1)} %copy-done.5), channel_id=1, source_target_pairs={{0,8},{8,0},{1,9},{9,1},{2,10},{10,2},{3,11},{11,3},{32,40},{40,32... | collective-permute-start | bytes 1572872 | tf_op jit(solution)/shard_map/ppermute | solution.py:34
  97.3 35.0 %collective-permute-start.41 = (bf16[16,64,256]{2,1,0:T(8,128)(2,1)}, bf16[16,64,256]{2,1,0:T(8,128)(2,1)}, u32[]{:S(2)}, u32[]{:S(2)}) collective-permute-start(bf16[16,64,256]{2,1,0:T(8,128)(2,1)} %collective-permute-done.39.refs_6_), channel_id=1, source_target_pairs={{0,8},{8,0},{1,9},{9,1},{2,10},{10,2},{3,11},{11,3},{32,40},{40,32... | collective-permute-start | bytes 1572872 | tf_op jit(solution)/shard_map/ppermute | solution.py:34
  108.9 23.4 %collective-permute-start.42 = (bf16[16,64,256]{2,1,0:T(8,128)(2,1)}, bf16[16,64,256]{2,1,0:T(8,128)(2,1)}, u32[]{:S(2)}, u32[]{:S(2)}) collective-permute-start(bf16[16,64,256]{2,1,0:T(8,128)(2,1)} %collective-permute-done.40.refs_7_), channel_id=1, source_target_pairs={{0,8},{8,0},{1,9},{9,1},{2,10},{10,2},{3,11},{11,3},{32,40},{40,32... | collective-permute-start | bytes 1572872 | tf_op jit(solution)/shard_map/ppermute | solution.py:34
  115.8 31.2 %collective-permute-start.9 = (bf16[1024,256]{1,0:T(8,128)(2,1)}, bf16[1024,256]{1,0:T(8,128)(2,1)S(1)}, u32[]{:S(2)}, u32[]{:S(2)}) collective-permute-start(bf16[1024,256]{1,0:T(8,128)(2,1)} %shard_map.126), channel_id=1, source_target_pairs={{0,2},{8,10},{1,3},{9,11},{2,0},{10,8},{3,1},{11,9},{32,34},{40,42... | collective-permute-start | bytes 1572872 | tf_op jit(solution)/shard_map/ppermute | solution.py:34
  130.3 16.7 %collective-permute-start.8 = (bf16[1024,256]{1,0:T(8,128)(2,1)S(1)}, bf16[1024,256]{1,0:T(8,128)(2,1)S(1)}, u32[]{:S(2)}, u32[]{:S(2)}) collective-permute-start(bf16[1024,256]{1,0:T(8,128)(2,1)S(1)} %copy-done.9), channel_id=1, source_target_pairs={{0,3},{8,11},{1,0},{9,8},{2,1},{10,9},{3,2},{11,10},{32,35},{40,43... | collective-permute-start | bytes 1572872 | tf_op jit(solution)/shard_map/ppermute | solution.py:34
  132.0 15.8 %collective-permute-start.7 = (bf16[1024,256]{1,0:T(8,128)(2,1)}, bf16[1024,256]{1,0:T(8,128)(2,1)}, u32[]{:S(2)}, u32[]{:S(2)}) collective-permute-start(bf16[1024,256]{1,0:T(8,128)(2,1)} %shard_map.124), channel_id=1, source_target_pairs={{0,1},{8,9},{1,2},{9,10},{2,3},{10,11},{3,0},{11,8},{32,33},{40,41... | collective-permute-start | bytes 1572872 | tf_op jit(solution)/shard_map/ppermute | solution.py:34
  150.6 7.9 %collective-permute-start.11 = (bf16[64,1024]{1,0:T(8,128)(2,1)S(1)}, bf16[64,1024]{1,0:T(8,128)(2,1)S(1)}, u32[]{:S(2)}, u32[]{:S(2)}) collective-permute-start(bf16[64,1024]{1,0:T(8,128)(2,1)S(1)} %get-tuple-element.27), channel_id=1, source_target_pairs={{0,16},{8,24},{1,17},{9,25},{2,18},{10,26},{3,19},{11,27},{32,48},... | collective-permute-start | bytes 393224 | tf_op jit(solution)/shard_map/ppermute | solution.py:34
  153.2 9.6 %collective-permute-start.45 = (bf16[3,64,512]{2,1,0:T(8,128)(2,1)}, bf16[3,64,512]{2,1,0:T(8,128)(2,1)}, u32[]{:S(2)}, u32[]{:S(2)}) collective-permute-start(bf16[3,64,512]{2,1,0:T(8,128)(2,1)} %get-tuple-element.10), channel_id=1, source_target_pairs={{0,64},{8,72},{1,65},{9,73},{2,66},{10,74},{3,67},{11,75},{32,96},... | collective-permute-start | bytes 589832 | tf_op jit(solution)/shard_map/ppermute | solution.py:34
  156.4 10.0 %collective-permute-start.44 = (bf16[3,64,512]{2,1,0:T(8,128)(2,1)S(1)}, bf16[3,64,512]{2,1,0:T(8,128)(2,1)}, u32[]{:S(2)}, u32[]{:S(2)}) collective-permute-start(bf16[3,64,512]{2,1,0:T(8,128)(2,1)S(1)} %get-tuple-element.11), channel_id=1, source_target_pairs={{0,96},{8,104},{1,97},{9,105},{2,98},{10,106},{3,99},{11,107},{32,... | collective-permute-start | bytes 589832 | tf_op jit(solution)/shard_map/ppermute | solution.py:34
  157.5 9.0 %collective-permute-start.43 = (bf16[3,64,512]{2,1,0:T(8,128)(2,1)S(1)}, bf16[3,64,512]{2,1,0:T(8,128)(2,1)}, u32[]{:S(2)}, u32[]{:S(2)}) collective-permute-start(bf16[3,64,512]{2,1,0:T(8,128)(2,1)S(1)} %get-tuple-element.9), channel_id=1, source_target_pairs={{0,32},{8,40},{1,33},{9,41},{2,34},{10,42},{3,35},{11,43},{32,64},... | collective-permute-start | bytes 589832 | tf_op jit(solution)/shard_map/ppermute | solution.py:34
  159.3 25.0 %collective-permute-start.15 = (bf16[8,8,16,256]{3,2,1,0:T(8,128)(2,1)S(1)}, bf16[8,8,16,256]{3,2,1,0:T(8,128)(2,1)}, u32[]{:S(2)}, u32[]{:S(2)}) collective-permute-start(bf16[8,8,16,256]{3,2,1,0:T(8,128)(2,1)S(1)} %bitcast.154), channel_id=1, source_target_pairs={{0,16},{8,24},{1,17},{9,25},{2,18},{10,26},{3,19},{11,27},{32,48},... | collective-permute-start | bytes 1572872 | tf_op jit(solution)/shard_map/ppermute | solution.py:34
  160.5 24.4 %collective-permute-start.16 = (bf16[8,8,16,256]{3,2,1,0:T(8,128)(2,1)S(1)}, bf16[8,8,16,256]{3,2,1,0:T(8,128)(2,1)}, u32[]{:S(2)}, u32[]{:S(2)}) collective-permute-start(bf16[8,8,16,256]{3,2,1,0:T(8,128)(2,1)S(1)} %bitcast.155), channel_id=1, source_target_pairs={{0,20},{8,28},{1,21},{9,29},{2,22},{10,30},{3,23},{11,31},{32,52},... | collective-permute-start | bytes 1572872 | tf_op jit(solution)/shard_map/ppermute | solution.py:34
  167.8 12.7 %collective-permute-start.46 = (bf16[3,64,256]{2,1,0:T(8,128)(2,1)S(1)}, bf16[3,64,256]{2,1,0:T(8,128)(2,1)S(1)}, u32[]{:S(2)}, u32[]{:S(2)}) collective-permute-start(bf16[3,64,256]{2,1,0:T(8,128)(2,1)S(1)} %get-tuple-element.31), channel_id=1, source_target_pairs={{0,0},{8,4},{1,1},{9,5},{2,2},{10,6},{3,3},{11,7},{32,32},{40,36},... | collective-permute-start | bytes 294920 | tf_op jit(solution)/shard_map/ppermute | solution.py:34
  173.4 10.1 %collective-permute-start.47 = (bf16[3,64,256]{2,1,0:T(8,128)(2,1)S(1)}, bf16[3,64,256]{2,1,0:T(8,128)(2,1)S(1)}, u32[]{:S(2)}, u32[]{:S(2)}) collective-permute-start(bf16[3,64,256]{2,1,0:T(8,128)(2,1)S(1)} %get-tuple-element.32), channel_id=1, source_target_pairs={{0,4},{8,0},{1,5},{9,1},{2,6},{10,2},{3,7},{11,3},{32,36},{40,32},... | collective-permute-start | bytes 294920 | tf_op jit(solution)/shard_map/ppermute | solution.py:34
  175.3 26.1 %collective-permute-start.13 = (bf16[8,8,16,256]{3,2,1,0:T(8,128)(2,1)S(1)}, bf16[8,8,16,256]{3,2,1,0:T(8,128)(2,1)}, u32[]{:S(2)}, u32[]{:S(2)}) collective-permute-start(bf16[8,8,16,256]{3,2,1,0:T(8,128)(2,1)S(1)} %bitcast.156), channel_id=1, source_target_pairs={{0,8},{8,0},{1,9},{9,1},{2,10},{10,2},{3,11},{11,3},{32,40},{40,32... | collective-permute-start | bytes 1572872 | tf_op jit(solution)/shard_map/ppermute | solution.py:34
  184.3 17.1 %collective-permute-start.14 = (bf16[8,8,16,256]{3,2,1,0:T(8,128)(2,1)S(1)}, bf16[8,8,16,256]{3,2,1,0:T(8,128)(2,1)}, u32[]{:S(2)}, u32[]{:S(2)}) collective-permute-start(bf16[8,8,16,256]{3,2,1,0:T(8,128)(2,1)S(1)} %copy-done.3), channel_id=1, source_target_pairs={{0,8},{8,0},{1,9},{9,1},{2,10},{10,2},{3,11},{11,3},{32,40},{40,32... | collective-permute-start | bytes 1572872 | tf_op jit(solution)/shard_map/ppermute | solution.py:34
  184.3 17.1 %collective-permute-start.17 = (bf16[8,8,16,256]{3,2,1,0:T(8,128)(2,1)}, bf16[8,8,16,256]{3,2,1,0:T(8,128)(2,1)}, u32[]{:S(2)}, u32[]{:S(2)}) collective-permute-start(bf16[8,8,16,256]{3,2,1,0:T(8,128)(2,1)} %collective-permute-done.15.refs_6_), channel_id=1, source_target_pairs={{0,8},{8,0},{1,9},{9,1},{2,10},{10,2},{3,11},{11,3},{32,40},{40,32... | collective-permute-start | bytes 1572872 | tf_op jit(solution)/shard_map/ppermute | solution.py:34
  184.8 16.6 %collective-permute-start.18 = (bf16[8,8,16,256]{3,2,1,0:T(8,128)(2,1)}, bf16[8,8,16,256]{3,2,1,0:T(8,128)(2,1)}, u32[]{:S(2)}, u32[]{:S(2)}) collective-permute-start(bf16[8,8,16,256]{3,2,1,0:T(8,128)(2,1)} %collective-permute-done.16.refs_7_), channel_id=1, source_target_pairs={{0,8},{8,0},{1,9},{9,1},{2,10},{10,2},{3,11},{11,3},{32,40},{40,32... | collective-permute-start | bytes 1572872 | tf_op jit(solution)/shard_map/ppermute | solution.py:34
  211.1 25.9 %collective-permute-start.31 = (bf16[3,64,512]{2,1,0:T(8,128)(2,1)S(1)}, bf16[3,64,512]{2,1,0:T(8,128)(2,1)S(1)}, u32[]{:S(2)}, u32[]{:S(2)}) collective-permute-start(bf16[3,64,512]{2,1,0:T(8,128)(2,1)S(1)} %get-tuple-element.19), channel_id=1, source_target_pairs={{0,64},{8,72},{1,65},{9,73},{2,66},{10,74},{3,67},{11,75},{32,96},... | collective-permute-start | bytes 589832 | tf_op jit(solution)/shard_map/ppermute | solution.py:34
  211.2 27.0 %collective-permute-start.30 = (bf16[3,64,512]{2,1,0:T(8,128)(2,1)S(1)}, bf16[3,64,512]{2,1,0:T(8,128)(2,1)S(1)}, u32[]{:S(2)}, u32[]{:S(2)}) collective-permute-start(bf16[3,64,512]{2,1,0:T(8,128)(2,1)S(1)} %get-tuple-element.20), channel_id=1, source_target_pairs={{0,96},{8,104},{1,97},{9,105},{2,98},{10,106},{3,99},{11,107},{32,... | collective-permute-start | bytes 589832 | tf_op jit(solution)/shard_map/ppermute | solution.py:34
  213.5 25.7 %collective-permute-start.29 = (bf16[3,64,512]{2,1,0:T(8,128)(2,1)S(1)}, bf16[3,64,512]{2,1,0:T(8,128)(2,1)S(1)}, u32[]{:S(2)}, u32[]{:S(2)}) collective-permute-start(bf16[3,64,512]{2,1,0:T(8,128)(2,1)S(1)} %get-tuple-element.18), channel_id=1, source_target_pairs={{0,32},{8,40},{1,33},{9,41},{2,34},{10,42},{3,35},{11,43},{32,64},... | collective-permute-start | bytes 589832 | tf_op jit(solution)/shard_map/ppermute | solution.py:34
  223.2 19.7 %collective-permute-start.26 = (bf16[3,64,512]{2,1,0:T(8,128)(2,1)S(1)}, bf16[3,64,512]{2,1,0:T(8,128)(2,1)S(1)}, u32[]{:S(2)}, u32[]{:S(2)}) collective-permute-start(bf16[3,64,512]{2,1,0:T(8,128)(2,1)S(1)} %get-tuple-element.16), channel_id=1, source_target_pairs={{0,64},{8,72},{1,65},{9,73},{2,66},{10,74},{3,67},{11,75},{32,96},... | collective-permute-start | bytes 589832 | tf_op jit(solution)/shard_map/ppermute | solution.py:34
  226.5 16.5 %collective-permute-start.25 = (bf16[3,64,512]{2,1,0:T(8,128)(2,1)S(1)}, bf16[3,64,512]{2,1,0:T(8,128)(2,1)S(1)}, u32[]{:S(2)}, u32[]{:S(2)}) collective-permute-start(bf16[3,64,512]{2,1,0:T(8,128)(2,1)S(1)} %get-tuple-element.17), channel_id=1, source_target_pairs={{0,96},{8,104},{1,97},{9,105},{2,98},{10,106},{3,99},{11,107},{32,... | collective-permute-start | bytes 589832 | tf_op jit(solution)/shard_map/ppermute | solution.py:34
  237.0 12.0 %collective-permute-start.24 = (bf16[3,64,512]{2,1,0:T(8,128)(2,1)S(1)}, bf16[3,64,512]{2,1,0:T(8,128)(2,1)S(1)}, u32[]{:S(2)}, u32[]{:S(2)}) collective-permute-start(bf16[3,64,512]{2,1,0:T(8,128)(2,1)S(1)} %get-tuple-element.15), channel_id=1, source_target_pairs={{0,32},{8,40},{1,33},{9,41},{2,34},{10,42},{3,35},{11,43},{32,64},... | collective-permute-start | bytes 589832 | tf_op jit(solution)/shard_map/ppermute | solution.py:34
  238.3 13.7 %collective-permute-start.21 = (bf16[3,64,512]{2,1,0:T(8,128)(2,1)S(1)}, bf16[3,64,512]{2,1,0:T(8,128)(2,1)S(1)}, u32[]{:S(2)}, u32[]{:S(2)}) collective-permute-start(bf16[3,64,512]{2,1,0:T(8,128)(2,1)S(1)} %get-tuple-element.13), channel_id=1, source_target_pairs={{0,64},{8,72},{1,65},{9,73},{2,66},{10,74},{3,67},{11,75},{32,96},... | collective-permute-start | bytes 589832 | tf_op jit(solution)/shard_map/ppermute | solution.py:34
  239.3 14.7 %collective-permute-start.20 = (bf16[3,64,512]{2,1,0:T(8,128)(2,1)S(1)}, bf16[3,64,512]{2,1,0:T(8,128)(2,1)S(1)}, u32[]{:S(2)}, u32[]{:S(2)}) collective-permute-start(bf16[3,64,512]{2,1,0:T(8,128)(2,1)S(1)} %get-tuple-element.14), channel_id=1, source_target_pairs={{0,96},{8,104},{1,97},{9,105},{2,98},{10,106},{3,99},{11,107},{32,... | collective-permute-start | bytes 589832 | tf_op jit(solution)/shard_map/ppermute | solution.py:34
  242.9 14.5 %collective-permute-start.19 = (bf16[3,64,512]{2,1,0:T(8,128)(2,1)S(1)}, bf16[3,64,512]{2,1,0:T(8,128)(2,1)S(1)}, u32[]{:S(2)}, u32[]{:S(2)}) collective-permute-start(bf16[3,64,512]{2,1,0:T(8,128)(2,1)S(1)} %get-tuple-element.12), channel_id=1, source_target_pairs={{0,32},{8,40},{1,33},{9,41},{2,34},{10,42},{3,35},{11,43},{32,64},... | collective-permute-start | bytes 589832 | tf_op jit(solution)/shard_map/ppermute | solution.py:34
  243.0 19.4 %collective-permute-start.32 = (bf16[3,64,256]{2,1,0:T(8,128)(2,1)S(1)}, bf16[3,64,256]{2,1,0:T(8,128)(2,1)S(1)}, u32[]{:S(2)}, u32[]{:S(2)}) collective-permute-start(bf16[3,64,256]{2,1,0:T(8,128)(2,1)S(1)} %get-tuple-element.43), channel_id=1, source_target_pairs={{0,0},{8,4},{1,1},{9,5},{2,2},{10,6},{3,3},{11,7},{32,32},{40,36},... | collective-permute-start | bytes 294920 | tf_op jit(solution)/shard_map/ppermute | solution.py:34
  249.0 18.2 %collective-permute-start.33 = (bf16[3,64,256]{2,1,0:T(8,128)(2,1)S(1)}, bf16[3,64,256]{2,1,0:T(8,128)(2,1)S(1)}, u32[]{:S(2)}, u32[]{:S(2)}) collective-permute-start(bf16[3,64,256]{2,1,0:T(8,128)(2,1)S(1)} %get-tuple-element.44), channel_id=1, source_target_pairs={{0,4},{8,0},{1,5},{9,1},{2,6},{10,2},{3,7},{11,3},{32,36},{40,32},... | collective-permute-start | bytes 294920 | tf_op jit(solution)/shard_map/ppermute | solution.py:34
  252.0 15.3 %collective-permute-start.27 = (bf16[3,64,256]{2,1,0:T(8,128)(2,1)S(1)}, bf16[3,64,256]{2,1,0:T(8,128)(2,1)S(1)}, u32[]{:S(2)}, u32[]{:S(2)}) collective-permute-start(bf16[3,64,256]{2,1,0:T(8,128)(2,1)S(1)} %get-tuple-element.39), channel_id=1, source_target_pairs={{0,0},{8,4},{1,1},{9,5},{2,2},{10,6},{3,3},{11,7},{32,32},{40,36},... | collective-permute-start | bytes 294920 | tf_op jit(solution)/shard_map/ppermute | solution.py:34
  254.0 13.4 %collective-permute-start.28 = (bf16[3,64,256]{2,1,0:T(8,128)(2,1)S(1)}, bf16[3,64,256]{2,1,0:T(8,128)(2,1)S(1)}, u32[]{:S(2)}, u32[]{:S(2)}) collective-permute-start(bf16[3,64,256]{2,1,0:T(8,128)(2,1)S(1)} %get-tuple-element.40), channel_id=1, source_target_pairs={{0,4},{8,0},{1,5},{9,1},{2,6},{10,2},{3,7},{11,3},{32,36},{40,32},... | collective-permute-start | bytes 294920 | tf_op jit(solution)/shard_map/ppermute | solution.py:34
  258.5 10.6 %collective-permute-start.22 = (bf16[3,64,256]{2,1,0:T(8,128)(2,1)S(1)}, bf16[3,64,256]{2,1,0:T(8,128)(2,1)S(1)}, u32[]{:S(2)}, u32[]{:S(2)}) collective-permute-start(bf16[3,64,256]{2,1,0:T(8,128)(2,1)S(1)} %get-tuple-element.35), channel_id=1, source_target_pairs={{0,0},{8,4},{1,1},{9,5},{2,2},{10,6},{3,3},{11,7},{32,32},{40,36},... | collective-permute-start | bytes 294920 | tf_op jit(solution)/shard_map/ppermute | solution.py:34
  262.4 10.1 %collective-permute-start.23 = (bf16[3,64,256]{2,1,0:T(8,128)(2,1)S(1)}, bf16[3,64,256]{2,1,0:T(8,128)(2,1)S(1)}, u32[]{:S(2)}, u32[]{:S(2)}) collective-permute-start(bf16[3,64,256]{2,1,0:T(8,128)(2,1)S(1)} %get-tuple-element.36), channel_id=1, source_target_pairs={{0,4},{8,0},{1,5},{9,1},{2,6},{10,2},{3,7},{11,3},{32,36},{40,32},... | collective-permute-start | bytes 294920 | tf_op jit(solution)/shard_map/ppermute | solution.py:34
  (25 other events, 196.1 us)
Sparse Core Ops, SparseCore 0:
  17.3 26.6 all-gather.8
  45.7 34.5 all-gather.10
  81.9 31.0 all-gather.14
  159.4 32.5 all-gather.12

commit v2 on v1

v2 whole, which is shorter than its diff:
```python
import itertools

import jax
import jax.numpy as jnp
from jax import lax
from jax.experimental import pallas as pl
from jax.experimental.pallas import tpu as pltpu
from jax.sharding import PartitionSpec as P

C = 2048
G = 32
FR = 16
HT = 8
WD = 8
EPSILON = 1e-05

ROWS = FR * HT * WD
CH = 256
SUB = 64
BF = jnp.bfloat16
F32 = jnp.float32
VMEM = 60 * 1024 * 1024


def linear(x, y, z, c):
    return (4 * y + 2 * (x % 2) + c) * 8 + 4 * (x // 2) + z


def send(value, to):
    pairs = []
    for x, y, z, c in itertools.product(range(4), range(4), range(4), range(2)):
        tx, ty, tz, tc = to(x, y, z, c)
        pairs.append((linear(x, y, z, c), linear(tx % 4, ty % 4, tz % 4, tc)))
    return lax.ppermute(value, ("dp", "mp"), pairs)


def to_z(step):
    return lambda x, y, z, c: (x, y, z + step, c)


def to_y(step):
    return lambda x, y, z, c: (x, y + step, z, c)


def to_core(x, y, z, c):
    return (x, y, z, 1 - c)


def to_half(x, y, z, c):
    return (x ^ 2, y, z, c)


def to_pair(x, y, z, c):
    return (x ^ 1, y, z, c)


def to_both(x, y, z, c):
    return (x ^ 3, y, z, c)


def to_pair_core(x, y, z, c):
    return (x ^ 1, y, z, 1 - c)


BLOCK_OF = ((0, 2, 1, 3), (1, 3, 0, 2))


def to_owner(flip):
    def to(x, y, z, c):
        half, pair = x // 2, x % 2
        block = BLOCK_OF[half][y]
        return (2 * (flip ^ c) + block % 2, 2 * half + block // 2, z, pair)

    return to


def contract_cols(left, right):
    return lax.dot_general(left, right, (((1,), (1,)), ((), ())), preferred_element_type=F32)


def contract_inner(left, right):
    return lax.dot_general(left, right, (((1,), (0,)), ((), ())), preferred_element_type=F32)


def cost(microseconds):
    return pl.CostEstimate(flops=int(microseconds * 1.15e9), bytes_accessed=0, transcendentals=0)


def params():
    return pltpu.CompilerParams(vmem_limit_bytes=VMEM)


def fill(padded, mine, other, spatial):
    if spatial:
        inner = (pl.ds(1, HT), pl.ds(1, WD), slice(None))
    else:
        inner = (pl.ds(1, FR), slice(None))
    padded[...] = jnp.zeros(padded.shape, BF)
    padded[inner + (pl.ds(0, CH),)] = mine
    padded[inner + (pl.ds(CH, CH),)] = other


def tap_rows(spatial, tap):
    if spatial:
        return (pl.ds(2 - tap // 3, HT), pl.ds(2 - tap % 3, WD))
    return (pl.ds(2 - tap, FR),)


def dgrad_body(spatial, blocks, index, mine, other, w_mine, *refs):
    w_other, outs, padded = refs[:2], refs[-1 - blocks : -1], refs[-1]
    step = pl.program_id(0)
    core = index[0]

    @pl.when(step == 0)
    def _():
        fill(padded, mine[...], other[...], spatial)

    total = jnp.zeros((ROWS, CH), F32)
    for tap in range(9 if spatial else 3):
        rows = padded[tap_rows(spatial, tap)].reshape(ROWS, 2 * CH)
        near, far = [w[0, tap] for w in w_other]
        low = jnp.where(core == 0, near, far)
        high = jnp.where(core == 0, far, near)
        weights = jnp.concatenate([w_mine[tap], jnp.concatenate([low, high], axis=0)], axis=1)
        total = total + contract_cols(rows, weights)
    for place, out in enumerate(outs):

        @pl.when(step == place)
        def _():
            out[...] = total.astype(out.dtype)


def whole(shape):
    return pl.BlockSpec(shape, lambda i, ix: (0,) * len(shape))


def pad_shape(spatial):
    return (HT + 2, WD + 2, FR, 2 * CH) if spatial else (FR + 2, HT * WD, 2 * CH)


def dgrad(spatial, blocks, kinds, index, mine, other, w_mine, w_near, w_far, *waits):
    taps = 9 if spatial else 3
    near = pl.BlockSpec((1, taps, CH // 2, CH), lambda i, ix: (ix[1 + blocks + i], 0, 0, 0))
    far = pl.BlockSpec((1, taps, CH // 2, CH), lambda i, ix: (ix[1 + 2 * blocks + i], 0, 0, 0))
    return pl.pallas_call(
        lambda *refs: dgrad_body(spatial, blocks, *refs),
        grid_spec=pltpu.PrefetchScalarGridSpec(
            num_scalar_prefetch=1,
            grid=(blocks,),
            in_specs=[
                whole(mine.shape),
                whole(other.shape),
                pl.BlockSpec((taps, CH, CH), lambda i, ix: (0, ix[1 + i], 0)),
                near,
                far,
            ]
            + [pl.BlockSpec(memory_space=pl.ANY)] * len(waits),
            out_specs=[whole((ROWS, CH))] * blocks,
            scratch_shapes=[pltpu.VMEM(pad_shape(spatial), BF)],
        ),
        out_shape=[jax.ShapeDtypeStruct((ROWS, CH), kind) for kind in kinds],
        compiler_params=params(),
        cost_estimate=cost(2.0 + 3.2 * blocks if spatial else 7.0),
    )(index, mine, other, w_mine, w_near, w_far, *waits)


def wgrad_body(first, spatial, lefts, index, *refs):
    left, (mine, other, pair, both, swapped) = refs[:lefts], refs[lefts : lefts + 5]
    out, padded = refs[-2:]
    step = pl.program_id(0)

    @pl.when(step == 0)
    def _():
        fill(padded.at[0], mine[...], other[...], spatial)
        fill(padded.at[1], swapped[0], swapped[1], spatial)
        fill(padded.at[2], pair[...], both[...], spatial)
        fill(padded.at[3], swapped[2], swapped[3], spatial)

    right = padded[(slice(None),) + tap_rows(spatial, step + first)]
    blocks = jnp.concatenate([ref[...].reshape(-1, 4 * ROWS) for ref in left], axis=0)
    result = contract_inner(blocks, right.reshape(4 * ROWS, 2 * CH))
    result = result.astype(BF)
    for block in range(4):
        out[index[block], 0] = result[block * SUB : (block + 1) * SUB]


def wgrad(spatial, first, taps, index, left, fields, *waits):
    return pl.pallas_call(
        lambda *refs: wgrad_body(first, spatial, len(left), *refs),
        grid_spec=pltpu.PrefetchScalarGridSpec(
            num_scalar_prefetch=1,
            grid=(taps,),
            in_specs=[whole(f.shape) for f in left + fields]
            + [pl.BlockSpec(memory_space=pl.ANY)] * len(waits),
            out_specs=pl.BlockSpec((4, 1, SUB, 2 * CH), lambda i, ix: (0, i, 0, 0)),
            scratch_shapes=[pltpu.VMEM((4,) + pad_shape(spatial), BF)],
        ),
        out_shape=jax.ShapeDtypeStruct((4, taps, SUB, 2 * CH), BF),
        compiler_params=params(),
        cost_estimate=cost(4.7 + 1.25 * taps),
    )(index, *left, *fields, *waits)


def after(value, *others):
    return pl.pallas_call(
        lambda *refs: None,
        in_specs=[pl.BlockSpec(memory_space=pl.ANY)] * (1 + len(others)),
        out_specs=pl.BlockSpec(memory_space=pl.ANY),
        out_shape=jax.ShapeDtypeStruct(value.shape, value.dtype),
        input_output_aliases={0: 0},
        cost_estimate=pl.CostEstimate(flops=0, bytes_accessed=0, transcendentals=0),
    )(value, *others)


def together(*values):
    return pl.pallas_call(
        lambda *refs: None,
        in_specs=[pl.BlockSpec(memory_space=pl.ANY)] * len(values),
        out_specs=[pl.BlockSpec(memory_space=pl.ANY)] * len(values),
        out_shape=[jax.ShapeDtypeStruct(value.shape, value.dtype) for value in values],
        input_output_aliases={i: i for i in range(len(values))},
        cost_estimate=pl.CostEstimate(flops=0, bytes_accessed=0, transcendentals=0),
    )(*values)


def per_group(values):
    return jnp.repeat(jnp.sum(values.reshape(-1, C // G), axis=1), C // G)


def local(
    block_input, spatial_out, cotangent, spatial_kernel, temporal_kernel, norm_gain, norm_bias
):
    dp, mp = lax.axis_index("dp"), lax.axis_index("mp")
    y, pair, core = dp // 4, (dp // 2) % 2, dp % 2
    half, z = mp // 4, mp % 4
    quarter = 2 * pair + core
    y_core_groups = [[4 * a + 2 * p + b for a in range(4) for b in range(2)] for p in range(2)]
    y_groups = [[4 * a + b for a in range(4)] for b in range(4)]
    z_groups = [[0, 1, 2, 3], [4, 5, 6, 7]]

    cot = cotangent.reshape(FR, HT * WD, CH)
    spatial_kernel = spatial_kernel.reshape(9, C, CH)

    def exchange(turned):
        pick = lambda k: lax.dynamic_index_in_dim(turned, quarter ^ k, 0, keepdims=False)
        sent = send(pick(1), to_core), send(pick(2), to_pair), send(pick(3), to_pair_core)
        return pick(0), sent

    def kernel_part(kernel):
        start = (1 - half) * 1024 + y * 256 + core * 128
        return lax.dynamic_slice_in_dim(kernel, start, 128, axis=1)

    tk_part = send(kernel_part(temporal_kernel), to_half)
    own, parts = exchange(spatial_out.reshape(ROWS, CH).T.reshape(4, SUB, ROWS))
    tk_part, *parts = together(tk_part, *parts)
    saved_part = jnp.concatenate([own, *parts], axis=1)
    saved_left = (lax.all_gather(saved_part, "mp", axis=0, axis_index_groups=z_groups),)

    tk_parts = [send(tk_part, to_y(k)) for k in (1, 2, 3)]
    cot_other = send(cot, to_half)
    cot_other, *tk_parts = together(cot_other, *tk_parts)
    tk_near = jnp.stack([tk_part, *tk_parts])

    flat_in = block_input.reshape(FR, HT * WD, CH).transpose(1, 0, 2).reshape(ROWS, CH).astype(F32)
    count = ROWS * (C // G)
    center = per_group(jnp.sum(flat_in, axis=0)) / count
    spread = per_group(jnp.sum(jnp.square(flat_in - center), axis=0)) / count
    inverse = lax.rsqrt(spread + EPSILON)
    normed_hat = (flat_in - center) * inverse
    normed = normed_hat * norm_gain + norm_bias
    gate = jax.nn.sigmoid(normed)
    hidden = (normed * gate).astype(BF)

    def blocks_of(spatial, steps, *arrays):
        blocks = [(z + k) % 4 for k in steps]
        if spatial:
            near, far = [2 * b for b in blocks], [2 * b + 1 for b in blocks]
        else:
            near = far = [(y - b) % 4 for b in blocks]
        index = [0 if spatial else core] + [half * 4 + b for b in blocks] + near + far
        index = jnp.stack([jnp.int32(i) for i in index])
        kinds = [BF if k else F32 for k in steps]
        return dgrad(spatial, len(steps), kinds, index, *arrays)

    def total_of(mine, sent):
        one, two, three = [v.astype(F32) for v in sent]
        return mine + (one + three) + two

    tk_far = send(tk_near, to_core)
    own, parts = exchange(hidden.T.reshape(4, SUB, ROWS))
    tk_far, *parts = together(tk_far, *parts)
    hidden_part = jnp.concatenate([own, *parts], axis=1)
    hidden_left = (lax.all_gather(hidden_part, "mp", axis=0, axis_index_groups=z_groups),)

    arrays = (cot, cot_other, temporal_kernel, tk_near, tk_far)
    sk_part = send(after(kernel_part(spatial_kernel), tk_far), to_half)
    up, down, far, mine = blocks_of(False, (1, 3, 2, 0), *arrays, *saved_left)
    sk_part, up, down, far = together(sk_part, up, down, far)
    sk_other = lax.all_gather(sk_part, "dp", axis=0, axis_index_groups=y_core_groups)
    up, down, far = send(up, to_z(1)), send(down, to_z(3)), send(far, to_z(2))
    cot_late = after(cot, mine)
    cot_pair, cot_both = send(cot_late, to_pair), send(cot_late, to_both)
    up, down, far, cot_pair, cot_both = together(up, down, far, cot_pair, cot_both)
    saved_grad = total_of(mine, (up, far, down)).astype(BF)
    saved_grad = saved_grad.reshape(FR, HT * WD, CH).transpose(1, 0, 2).reshape(HT, WD, FR, CH)

    sg_other = send(saved_grad, to_half)
    cot_near = (cot, cot_other, cot_pair, cot_both)
    cot_swapped = send(jnp.stack(cot_near), to_core)
    sg_other, cot_swapped = together(sg_other, cot_swapped)

    arrays = (saved_grad, sg_other, spatial_kernel, sk_other, sk_other)
    up, down = blocks_of(True, (1, 3), *arrays)
    sg_late = after(saved_grad, up)
    up, down = send(up, to_z(1)), send(down, to_z(3))
    sg_pair, sg_both = send(sg_late, to_pair), send(sg_late, to_both)
    far, mine = blocks_of(True, (2, 0), *arrays, sg_late, *hidden_left)
    up, down, far, sg_pair, sg_both = together(up, down, far, sg_pair, sg_both)

    far = send(far, to_z(2))
    sg_near = (saved_grad, sg_other, sg_pair, sg_both)
    sg_swapped = send(jnp.stack(sg_near), to_core)

    slots = jnp.array([[0, 2, 1, 3], [2, 0, 3, 1]], jnp.int32)[half]
    temporal_parts = wgrad(False, 0, 3, slots, saved_left, cot_near + (cot_swapped,), up)
    temporal_total = lax.psum_scatter(
        temporal_parts, "dp", scatter_dimension=0, axis_index_groups=y_groups
    )
    far, sg_swapped = together(far, sg_swapped)
    order = (slots - y) % 4
    parts = wgrad(True, 0, 9, order, hidden_left, sg_near + (sg_swapped,), temporal_parts)
    hidden_grad = total_of(mine, (up, far, down))

    normed_grad = hidden_grad * gate * (1.0 + normed * (1.0 - gate))
    gain_sum = jnp.sum(normed_grad * normed_hat, axis=0)
    bias_sum = jnp.sum(normed_grad, axis=0)
    first = per_group(bias_sum * norm_gain) / count
    second = per_group(gain_sum * norm_gain) / count
    branch = inverse * (normed_grad * norm_gain - first - normed_hat * second)
    branch = branch.reshape(HT * WD, FR, CH).transpose(1, 0, 2)
    input_grad = (cot.astype(F32) + branch).astype(BF).reshape(block_input.shape)

    def to_owners(total):
        total = total.astype(BF)
        mine, other = total[:, :, :CH], total[:, :, CH:]
        same = half == core
        first, second = jnp.where(same, mine, other), jnp.where(same, other, mine)
        first, second = together(first, second)
        return send(first, to_owner(0)), send(second, to_owner(1))

    def owned(first, second):
        low, high = jnp.where(half == 0, first, second), jnp.where(half == 0, second, first)
        return jnp.concatenate([low, high], axis=1).astype(F32)

    sums = after(jnp.stack([gain_sum, bias_sum]), parts)
    sums = lax.all_gather(sums, "dp", axis=0)
    others = [send(parts[k], to_y(k)) for k in (1, 2, 3)]
    *others, sums = together(*others, sums)
    total = parts[0].astype(F32)
    for other in others:
        total = total + other.astype(F32)
    owned_parts = together(*to_owners(total), *to_owners(after(temporal_total, sums)))
    spatial_owned, temporal_owned = owned_parts[:2], owned_parts[2:]
    sums = jnp.sum(sums, axis=0)
    temporal_grad = owned(*temporal_owned)
    spatial_grad = owned(*spatial_owned).reshape(3, 3, CH // 2, CH)
    return (input_grad, spatial_grad, temporal_grad, sums[0], sums[1])


def solution(mesh):
    placed = (
        P("dp", None, None, None, "mp"),
        P("dp", None, None, None, "mp"),
        P("dp", None, None, None, "mp"),
        P(None, None, None, "mp"),
        P(None, None, "mp"),
        P("mp"),
        P("mp"),
    )
    return jax.shard_map(
        local,
        mesh=mesh,
        in_specs=placed,
        out_specs=(
            P("dp", None, None, None, "mp"),
            P(None, None, "dp", "mp"),
            P(None, "dp", "mp"),
            P("mp"),
            P("mp"),
        ),
        check_vma=False,
    )
```

time: 283 us -> 273 us (0.965)
  Pallas kernels: 74.4 us -> 51.5 us
  starting transfers between devices: 71.1 us -> 50.6 us
  blocking collectives: 0 us -> 17.2 us
  local copies, waits for them, and re-layouts: 13.2 us -> 23 us
  other arithmetic: 18.8 us -> 27.6 us
    pallas_call x12 -> x22, Pallas kernels: 74.4 us -> 51.5 us  [the longest x3 26.6 us: dgrad(): pl.pallas_call(lambda *refs: dgrad_body(spatial, blocks, *refs), grid_spe...]
    ppermute x52 -> x33, starting transfers between devices: 70.9 us -> 50.5 us  [send(): return lax.ppermute(value, ('dp', 'mp'), pairs)]
    all_gather x0 -> x1, blocking collectives: none -> 17.2 us  [local(): sums = lax.all_gather(sums, 'dp', axis=0)]
    unnamed x34 -> x100, local copies, waits for them, and re-layouts: 3.93 us -> 12.8 us
    ppermute x52 -> x33, waiting for transfers between devices: 88.2 us -> 81.2 us  [send(): return lax.ppermute(value, ('dp', 'mp'), pairs)]
    all_gather x4 -> x3, waiting for transfers between devices: 0.04 us -> 6.78 us  [the longest x1 6.78 us: local(): lax.all_gather(hidden_part, 'mp', axis=0, axis_index_groups=z_groups)]
    another operation x5 -> x4, other arithmetic: 2.99 us -> 8.8 us  [the longest x1 3.12 us: local(): cot_swapped = send(jnp.stack(cot_near), to_core)]
    select_n x5 -> x4, other arithmetic: 0.1 us -> 4.53 us  [the longest x2 2.48 us: to_owners(): first, second = (jnp.where(same, mine, other), jnp.where(same, other, mine))]
  transfers between devices with their start and end apart: 56 -> 37, of which waited for: 18 -> 18; matrix products, arithmetic and copies ran while one was open for 8% -> 11% of each run, Pallas kernels for 24% -> 19%
where the time goes in v2:
time: 273 us; the launch traced here: 272 us
  waiting for transfers between devices  88.1 us (32%)
  Pallas kernels  51.5 us (19%)
  starting transfers between devices  50.6 us (19%)
  other arithmetic  27.6 us (10%)
  local copies, waits for them, and re-layouts  23 us (8%)
  blocking collectives  17.2 us (6%)
  between operations  14.3 us (5%)
    ppermute x33, waiting for transfers between devices, send(): return lax.ppermute(value, ('dp', 'mp'), pairs)  81.2 us
    ppermute x33, starting transfers between devices, send(): return lax.ppermute(value, ('dp', 'mp'), pairs)  50.5 us
    pallas_call x3, Pallas kernels, dgrad(): pl.pallas_call(lambda *refs: dgrad_body(spatial, blocks, *refs), grid_spe...  26.6 us
    pallas_call x2, Pallas kernels, wgrad(): pl.pallas_call(lambda *refs: wgrad_body(first, spatial, len(left), *refs)...  24.8 us
    all_gather x1, blocking collectives, local(): sums = lax.all_gather(sums, 'dp', axis=0)  17.2 us
    unnamed x100, local copies, waits for them, and re-layouts  12.8 us
    all_gather x1, waiting for transfers between devices, local(): lax.all_gather(hidden_part, 'mp', axis=0, axis_index_groups=z_groups)  6.78 us
  transfers between devices with their start and end apart: 37, of which 18 were waited for; matrix products, arithmetic and copies ran while one was open for 11% of the time, Pallas kernels for 19%

profile of v2, /device:TPU:6, one launch (start us, length us, event | category | flops | bytes accessed | tf_op | source)
XLA Modules:
  0.0 272.2 jit_solution(18323243708300526463)
XLA Ops:
  8.2 1.5 collective-permute-start.1
  9.7 1.3 copy.77
  13.1 4.8 %collective-permute-done.4.refs_3_ = bf16[64,1024]{1,0:T(8,128)(2,1)S(1)} collective-permute-done((bf16[64,1024]{1,0:T(8,128)(2,1)S(1)}, bf16[64,1024]{1,0:T(8,128)(2,1)S(1)}, u32[]{:S(2)}, u32[]{:S(2)}) %collective-permute-start.4) | collective-permute-done | bytes 131104 | tf_op jit(solution)/shard_map/ppermute | solution.py:34
  17.8 1.7 collective-permute-done.3.refs_2_
  20.9 1.9 pad_maximum_fusion.3
  22.8 4.1 %collective-permute-start = (bf16[16,64,256]{2,1,0:T(8,128)(2,1)S(1)}, bf16[16,64,256]{2,1,0:T(8,128)(2,1)S(1)}, u32[]{:S(2)}, u32[]{:S(2)}) collective-permute-start(bf16[16,64,256]{2,1,0:T(8,128)(2,1)S(1)} %bitcast.121), channel_id=1, source_target_pairs={{0,4},{8,12},{1,5},{9,13},{2,6},{10,14},{3,7},{11,15},{32,36},{40,... | collective-permute-start | bytes 1572872 | tf_op jit(solution)/shard_map/ppermute | solution.py:34
  27.9 3.1 %collective-permute-start.7 = (bf16[3,128,256]{2,1,0:T(8,128)(2,1)S(1)}, bf16[3,128,256]{2,1,0:T(8,128)(2,1)S(1)}, u32[]{:S(2)}, u32[]{:S(2)}) collective-permute-start(bf16[3,128,256]{2,1,0:T(8,128)(2,1)S(1)} %copy-done.28), channel_id=1, source_target_pairs={{0,96},{8,104},{1,97},{9,105},{2,98},{10,106},{3,99},{11,107},{32,... | collective-permute-start | bytes 589832 | tf_op jit(solution)/shard_map/ppermute | solution.py:34
  32.7 5.5 %collective-permute-done.7.refs_3_ = bf16[3,128,256]{2,1,0:T(8,128)(2,1)S(1)} collective-permute-done((bf16[3,128,256]{2,1,0:T(8,128)(2,1)S(1)}, bf16[3,128,256]{2,1,0:T(8,128)(2,1)S(1)}, u32[]{:S(2)}, u32[]{:S(2)}) %collective-permute-start.7) | collective-permute-done | bytes 196640 | tf_op jit(solution)/shard_map/ppermute | solution.py:34
  38.2 1.7 collective-permute-done.6.refs_2_
  39.9 2.0 collective-permute-done.5.refs_1_
  43.3 2.1 pad_maximum_fusion.2.refs_4_
  48.1 1.5 collective-permute-start.10
  50.3 1.9 constant_dynamic-slice_fusion.1.refs_0_
  52.6 3.4 %collective-permute-done.10.refs_2_ = bf16[64,1024]{1,0:T(8,128)(2,1)S(1)} collective-permute-done((bf16[64,1024]{1,0:T(8,128)(2,1)S(1)}, bf16[64,1024]{1,0:T(8,128)(2,1)S(1)}, u32[]{:S(2)}, u32[]{:S(2)}) %collective-permute-start.10) | collective-permute-done | bytes 131104 | tf_op jit(solution)/shard_map/ppermute | solution.py:34
  58.8 8.3 %shard_map.122 = (bf16[1024,256]{1,0:T(8,128)(2,1)}, bf16[1024,256]{1,0:T(8,128)(2,1)}, bf16[1024,256]{1,0:T(8,128)(2,1)}, f32[1024,256]{1,0:T(8,128)}) custom-call(s32[13]{0:T(128)} %stack.130.refs_0_, bf16[16,64,256]{2,1,0:T(8,128)(2,1)} %bitcast.119, bf16[16,64,256]{2,1,0:T(8,128)(2,1)} %get-tuple-element.56.refs_2_.refs_3_, ...), custom_call_target="tpu_custom_call" | custom-call | flops 8049999872 | tf_op jit(solution)/shard_map/pallas_call | solution.py:145
  67.1 7.1 %collective-permute-done.12.refs_0_ = bf16[9,128,256]{2,1,0:T(8,128)(2,1)S(1)} collective-permute-done((bf16[9,128,256]{2,1,0:T(8,128)(2,1)}, bf16[9,128,256]{2,1,0:T(8,128)(2,1)S(1)}, u32[]{:S(2)}, u32[]{:S(2)}) %collective-permute-start.12) | collective-permute-done | bytes 589856 | tf_op jit(solution)/shard_map/ppermute | solution.py:34
  75.9 1.9 collective-permute-start.13
  77.8 2.0 collective-permute-start.14
  79.9 2.0 collective-permute-start.15
  82.9 1.7 pad_maximum_fusion.4
  84.7 7.3 %collective-permute-done.13.refs_0_ = bf16[1024,256]{1,0:T(8,128)(2,1)S(1)} collective-permute-done((bf16[1024,256]{1,0:T(8,128)(2,1)}, bf16[1024,256]{1,0:T(8,128)(2,1)S(1)}, u32[]{:S(2)}, u32[]{:S(2)}) %collective-permute-start.13) | collective-permute-done | bytes 524320 | tf_op jit(solution)/shard_map/ppermute | solution.py:34
  92.0 9.3 %collective-permute-done.14.refs_1_ = bf16[1024,256]{1,0:T(8,128)(2,1)S(1)} collective-permute-done((bf16[1024,256]{1,0:T(8,128)(2,1)}, bf16[1024,256]{1,0:T(8,128)(2,1)S(1)}, u32[]{:S(2)}, u32[]{:S(2)}) %collective-permute-start.14) | collective-permute-done | bytes 524320 | tf_op jit(solution)/shard_map/ppermute | solution.py:34
  101.3 1.8 collective-permute-done.15.refs_2_
  103.9 3.1 %pad_maximum_fusion = bf16[4,16,64,256]{3,2,1,0:T(8,128)(2,1)} fusion(bf16[1,16,64,256]{3,2,1,0:T(8,128)(2,1)} %bitcast.42, bf16[1,16,64,256]{3,2,1,0:T(8,128)(2,1)} %bitcast.41, bf16[1,16,64,256]{3,2,1,0:T(8,128)(2,1)} %bitcast.131, bf16[1,16,64,256]{3,2,1,0:T(8,128)(2,1)S(1)} %bitcast.123), kind=kLoop, calls=%fused_computation | loop fusion | flops 3145728 | bytes 4194304 | tf_op jit(solution)/shard_map/stack | solution.py:309
  107.7 1.8 collective-permute-start.18
  111.5 12.3 %collective-permute-done.18.refs_0_ = bf16[8,8,16,256]{3,2,1,0:T(8,128)(2,1)S(1)} collective-permute-done((bf16[8,8,16,256]{3,2,1,0:T(8,128)(2,1)S(1)}, bf16[8,8,16,256]{3,2,1,0:T(8,128)(2,1)S(1)}, u32[]{:S(2)}, u32[]{:S(2)}) %collective-permute-start.18) | collective-permute-done | bytes 524320 | tf_op jit(solution)/shard_map/ppermute | solution.py:34
  124.6 9.1 %shard_map.128 = (bf16[1024,256]{1,0:T(8,128)(2,1)}, bf16[1024,256]{1,0:T(8,128)(2,1)}) custom-call(s32[7]{0:T(128)} %stack.144.refs_0_, bf16[8,8,16,256]{3,2,1,0:T(8,128)(2,1)} %bitcast.115, bf16[8,8,16,256]{3,2,1,0:T(8,128)(2,1)} %get-tuple-element.76.refs_2_.refs_3_, bf16[9,2048,256]{2,1,0:T(8,128)(2,1)} %bitcast.141, bf16[8,9,128,256]{3,2,1,0:T(8,128)(2,1)} %bitcast.148, ...), custom_call_target="tpu_custom_call" | custom-call | flops 9660000256 | tf_op jit(solution)/shard_map/pallas_call | solution.py:145
  136.3 2.1 collective-permute-start.21
  138.4 6.8 %all-gather.13.cloned.1.call-done = bf16[256,4096]{1,0:T(8,128)(2,1)} async-done(((bf16[64,4096]{1,0:T(8,128)(2,1)}), bf16[256,4096]{1,0:T(8,128)(2,1)}) %all-gather.13.cloned.1.call-update) | async-done | bytes 2097168 | tf_op jit(solution)/shard_map/all_gather | solution.py:293
  145.2 9.3 %shard_map.130 = (bf16[1024,256]{1,0:T(8,128)(2,1)}, f32[1024,256]{1,0:T(8,128)}) custom-call(s32[7]{0:T(128)} %stack.122.refs_0_, bf16[8,8,16,256]{3,2,1,0:T(8,128)(2,1)} %bitcast.116, bf16[8,8,16,256]{3,2,1,0:T(8,128)(2,1)} %get-tuple-element.76.refs_2_.refs_3_, bf16[9,2048,256]{2,1,0:T(8,128)(2,1)} %bitcast.142, bf16[8,9,128,256]{3,2,1,0:T(8,128)(2,1)} %bitcast.150, ...), custom_call_target="tpu_custom_call" | custom-call | flops 9660000256 | tf_op jit(solution)/shard_map/pallas_call | solution.py:145
  155.9 3.0 %pad_maximum_fusion.1 = bf16[4,8,8,16,256]{4,3,2,1,0:T(8,128)(2,1)} fusion(bf16[1,8,8,16,256]{4,3,2,1,0:T(8,128)(2,1)} %bitcast.129, bf16[1,8,8,16,256]{4,3,2,1,0:T(8,128)(2,1)} %bitcast.52, bf16[1,8,8,16,256]{4,3,2,1,0:T(8,128)(2,1)} %bitcast.130, bf16[1,8,8,16,256]{4,3,2,1,0:T(8,128)(2,1)S(1)} %bitcast.118), kind=kLoop, calls=%fused_computation.1 | loop fusion | flops 3145728 | bytes 4194304 | tf_op jit(solution)/shard_map/stack | solution.py:322
  159.9 1.4 collective-permute-start.24
  161.3 8.4 %shard_map.133.refs_7_ = bf16[4,3,64,512]{3,2,1,0:T(8,128)(2,1)} custom-call(s32[4]{0:T(128)} %fusion.7.refs_0_, bf16[4,64,4096]{2,1,0:T(8,128)(2,1)} %bitcast.153, bf16[16,64,256]{2,1,0:T(8,128)(2,1)} %bitcast.120, bf16[16,64,256]{2,1,0:T(8,128)(2,1)} %get-tuple-element.56.refs_2_.refs_3_, bf16[16,64,256]{2,1,0:T(8,128)(2,1)} %get-tuple-element.74.refs_4_, ...), custom_call_target="tpu_custom_call" | custom-call | flops 9717499904 | tf_op jit(solution)/shard_map/pallas_call | solution.py:188
  169.8 5.9 %collective-permute-done.24.refs_0_ = bf16[1024,256]{1,0:T(8,128)(2,1)S(1)} collective-permute-done((bf16[1024,256]{1,0:T(8,128)(2,1)S(1)}, bf16[1024,256]{1,0:T(8,128)(2,1)S(1)}, u32[]{:S(2)}, u32[]{:S(2)}) %collective-permute-start.24) | collective-permute-done | bytes 524320 | tf_op jit(solution)/shard_map/ppermute | solution.py:34
  176.5 3.2 %fusion.8 = (f32[256]{0:T(256)S(1)}, f32[256]{0:T(256)S(1)}, f32[1024,256]{1,0:T(8,128)}) fusion(f32[256]{0:T(256)S(1)} %rsqrt.12, f32[256]{0:T(256)S(1)} %div.44, f32[16,64,256]{2,0,1:T(8,128)S(1)} %copy.78, f32[256]{0:T(256)S(1)} %copy-done.47, f32[256]{0:T(256)S(1)} %copy-done.46, bf16[1024,256]{1,0:T(8,128)(2,1)} %get-tuple-element.90, ...), kind=kLoop, calls=%fused_computation.59 | loop fusion | flops 5504512 | bytes 4724736 | tf_op jit(solution)/shard_map/reduce_sum | solution.py:336
  180.2 16.4 %shard_map.134.refs_1_ = bf16[4,9,64,512]{3,2,1,0:T(8,128)(2,1)} custom-call(s32[4]{0:T(128)} %and_select_fusion.refs_0_, bf16[4,64,4096]{2,1,0:T(8,128)(2,1)} %bitcast.155, bf16[8,8,16,256]{3,2,1,0:T(8,128)(2,1)} %bitcast.117, bf16[8,8,16,256]{3,2,1,0:T(8,128)(2,1)} %get-tuple-element.76.refs_2_.refs_3_, bf16[8,8,16,256]{3,2,1,0:T(8,128)(2,1)} %get-tuple-element.88.refs_4_, ...), custom_call_target="tpu_custom_call" | custom-call | flops 18342500352 | tf_op jit(solution)/shard_map/pallas_call | solution.py:188
  198.3 4.9 %collective-permute-start.28 = (bf16[9,64,512]{2,1,0:T(8,128)(2,1)S(1)}, bf16[9,64,512]{2,1,0:T(8,128)(2,1)}, u32[]{:S(2)}, u32[]{:S(2)}) collective-permute-start(bf16[9,64,512]{2,1,0:T(8,128)(2,1)S(1)} %get-tuple-element.108), channel_id=1, source_target_pairs={{0,96},{8,104},{1,97},{9,105},{2,98},{10,106},{3,99},{11,107},{32,... | collective-permute-start | bytes 1769480 | tf_op jit(solution)/shard_map/ppermute | solution.py:34
  205.1 17.2 %all-gather.4.refs_3_ = f32[16,2,256]{2,1,0:T(2,128)} all-gather(f32[1,2,256]{2,1,0:T(2,128)S(1)} %bitcast.143), channel_id=5, replica_groups=mesh['dp'=16,'mp'=8] {'dp'}, dimensions={0}, use_global_device_ids=true | all-gather | bytes 34816 | tf_op jit(solution)/shard_map/all_gather | solution.py:356
  222.6 1.4 fusion.5
  224.0 4.5 %collective-permute-done.28.refs_2_ = bf16[9,64,512]{2,1,0:T(8,128)(2,1)} collective-permute-done((bf16[9,64,512]{2,1,0:T(8,128)(2,1)S(1)}, bf16[9,64,512]{2,1,0:T(8,128)(2,1)}, u32[]{:S(2)}, u32[]{:S(2)}) %collective-permute-start.28) | collective-permute-done | bytes 589856 | tf_op jit(solution)/shard_map/ppermute | solution.py:34
  228.5 3.7 %collective-permute-done.26.refs_0_ = bf16[9,64,512]{2,1,0:T(8,128)(2,1)} collective-permute-done((bf16[9,64,512]{2,1,0:T(8,128)(2,1)S(1)}, bf16[9,64,512]{2,1,0:T(8,128)(2,1)}, u32[]{:S(2)}, u32[]{:S(2)}) %collective-permute-start.26) | collective-permute-done | bytes 589856 | tf_op jit(solution)/shard_map/ppermute | solution.py:34
  232.1 1.8 fusion.2
  234.8 1.9 collective-permute-start.29
  236.7 2.6 collective-permute-start.30
  239.3 1.6 broadcast_select_fusion.6
  240.9 6.5 %collective-permute-start.31 = (bf16[3,64,256]{2,1,0:T(8,128)(2,1)}, bf16[3,64,256]{2,1,0:T(8,128)(2,1)S(1)}, u32[]{:S(2)}, u32[]{:S(2)}) collective-permute-start(bf16[3,64,256]{2,1,0:T(8,128)(2,1)} %get-tuple-element.99), channel_id=1, source_target_pairs={{0,0},{8,4},{1,1},{9,5},{2,2},{10,6},{3,3},{11,7},{32,32},{40,36},... | collective-permute-start | bytes 294920 | tf_op jit(solution)/shard_map/ppermute | solution.py:34
  247.5 2.3 collective-permute-start.32
  250.3 9.8 %collective-permute-done.31.refs_2_ = bf16[3,64,256]{2,1,0:T(8,128)(2,1)S(1)} collective-permute-done((bf16[3,64,256]{2,1,0:T(8,128)(2,1)}, bf16[3,64,256]{2,1,0:T(8,128)(2,1)S(1)}, u32[]{:S(2)}, u32[]{:S(2)}) %collective-permute-start.31) | collective-permute-done | bytes 98336 | tf_op jit(solution)/shard_map/ppermute | solution.py:34
  (211 shorter events, 39.2 us)
Async XLA Ops:
  7.2 51.7 %all-gather.9.cloned.1.call-start = ((), (), s32[]{:S(2)}) async-start(), calls=%async_computation.2 | async-start | bytes 2621440 | tf_op jit(solution)/shard_map/all_gather | solution.py:257
  8.2 11.3 %collective-permute-start.1 = (bf16[3,128,256]{2,1,0:T(8,128)(2,1)S(1)}, bf16[3,128,256]{2,1,0:T(8,128)(2,1)S(1)}, u32[]{:S(2)}, u32[]{:S(2)}) collective-permute-start(bf16[3,128,256]{2,1,0:T(8,128)(2,1)S(1)} %constant_dynamic-slice_fusion.2), channel_id=1, source_target_pairs={{0,4},{8,12},{1,5},{9,13},{2,6},{10,14},{3,7},{11,15},{32,36},{40,... | collective-permute-start | bytes 589832 | tf_op jit(solution)/shard_map/ppermute | solution.py:34
  9.7 13.1 %copy-start.4 = (bf16[1,16,8,8,256]{4,3,2,1,0:T(8,128)(2,1)S(1)}, bf16[1,16,8,8,256]{4,3,2,1,0:T(8,128)(2,1)}, u32[]{:S(2)}) copy-start(bf16[1,16,8,8,256]{4,3,2,1,0:T(8,128)(2,1)} %param.10) | copy-start | bytes 1572868
  9.7 17.2 %copy-start.1 = (bf16[1,16,8,8,256]{4,3,2,1,0:T(8,128)(2,1)S(1)}, bf16[1,16,8,8,256]{4,3,2,1,0:T(8,128)(2,1)}, u32[]{:S(2)}) copy-start(bf16[1,16,8,8,256]{4,3,2,1,0:T(8,128)(2,1)} %param.8) | copy-start | bytes 1572868
  11.1 6.7 %collective-permute-start.4 = (bf16[64,1024]{1,0:T(8,128)(2,1)S(1)}, bf16[64,1024]{1,0:T(8,128)(2,1)S(1)}, u32[]{:S(2)}, u32[]{:S(2)}) collective-permute-start(bf16[64,1024]{1,0:T(8,128)(2,1)S(1)} %get-tuple-element.120), channel_id=1, source_target_pairs={{0,24},{8,16},{1,25},{9,17},{2,26},{10,18},{3,27},{11,19},{32,56},... | collective-permute-start | bytes 393224 | tf_op jit(solution)/shard_map/ppermute | solution.py:34
  11.2 8.3 %collective-permute-start.3 = (bf16[64,1024]{1,0:T(8,128)(2,1)S(1)}, bf16[64,1024]{1,0:T(8,128)(2,1)S(1)}, u32[]{:S(2)}, u32[]{:S(2)}) collective-permute-start(bf16[64,1024]{1,0:T(8,128)(2,1)S(1)} %get-tuple-element.121), channel_id=1, source_target_pairs={{0,16},{8,24},{1,17},{9,25},{2,18},{10,26},{3,19},{11,27},{32,48},... | collective-permute-start | bytes 393224 | tf_op jit(solution)/shard_map/ppermute | solution.py:34
  12.4 7.1 %collective-permute-start.2 = (bf16[64,1024]{1,0:T(8,128)(2,1)S(1)}, bf16[64,1024]{1,0:T(8,128)(2,1)S(1)}, u32[]{:S(2)}, u32[]{:S(2)}) collective-permute-start(bf16[64,1024]{1,0:T(8,128)(2,1)S(1)} %get-tuple-element.122), channel_id=1, source_target_pairs={{0,8},{8,0},{1,9},{9,1},{2,10},{10,2},{3,11},{11,3},{32,40},{40,32... | collective-permute-start | bytes 393224 | tf_op jit(solution)/shard_map/ppermute | solution.py:34
  22.8 101.8 %all-gather.11.cloned.1.call-start = ((), (), s32[]{:S(2)}) async-start(), calls=%async_computation.3 | async-start | bytes 5308416 | tf_op jit(solution)/shard_map/all_gather | solution.py:299
  22.8 19.0 %collective-permute-start = (bf16[16,64,256]{2,1,0:T(8,128)(2,1)S(1)}, bf16[16,64,256]{2,1,0:T(8,128)(2,1)S(1)}, u32[]{:S(2)}, u32[]{:S(2)}) collective-permute-start(bf16[16,64,256]{2,1,0:T(8,128)(2,1)S(1)} %bitcast.121), channel_id=1, source_target_pairs={{0,4},{8,12},{1,5},{9,13},{2,6},{10,14},{3,7},{11,15},{32,36},{40,... | collective-permute-start | bytes 1572872 | tf_op jit(solution)/shard_map/ppermute | solution.py:34
  27.9 10.3 %collective-permute-start.7 = (bf16[3,128,256]{2,1,0:T(8,128)(2,1)S(1)}, bf16[3,128,256]{2,1,0:T(8,128)(2,1)S(1)}, u32[]{:S(2)}, u32[]{:S(2)}) collective-permute-start(bf16[3,128,256]{2,1,0:T(8,128)(2,1)S(1)} %copy-done.28), channel_id=1, source_target_pairs={{0,96},{8,104},{1,97},{9,105},{2,98},{10,106},{3,99},{11,107},{32,... | collective-permute-start | bytes 589832 | tf_op jit(solution)/shard_map/ppermute | solution.py:34
  30.9 8.9 %collective-permute-start.6 = (bf16[3,128,256]{2,1,0:T(8,128)(2,1)S(1)}, bf16[3,128,256]{2,1,0:T(8,128)(2,1)S(1)}, u32[]{:S(2)}, u32[]{:S(2)}) collective-permute-start(bf16[3,128,256]{2,1,0:T(8,128)(2,1)S(1)} %copy-done.28), channel_id=1, source_target_pairs={{0,64},{8,72},{1,65},{9,73},{2,66},{10,74},{3,67},{11,75},{32,96},... | collective-permute-start | bytes 589832 | tf_op jit(solution)/shard_map/ppermute | solution.py:34
  31.6 10.3 %collective-permute-start.5 = (bf16[3,128,256]{2,1,0:T(8,128)(2,1)S(1)}, bf16[3,128,256]{2,1,0:T(8,128)(2,1)S(1)}, u32[]{:S(2)}, u32[]{:S(2)}) collective-permute-start(bf16[3,128,256]{2,1,0:T(8,128)(2,1)S(1)} %copy-done.28), channel_id=1, source_target_pairs={{0,32},{8,40},{1,33},{9,41},{2,34},{10,42},{3,35},{11,43},{32,64},... | collective-permute-start | bytes 589832 | tf_op jit(solution)/shard_map/ppermute | solution.py:34
  45.5 10.6 %collective-permute-start.8 = (bf16[4,3,128,256]{3,2,1,0:T(8,128)(2,1)}, bf16[4,3,128,256]{3,2,1,0:T(8,128)(2,1)S(1)}, u32[]{:S(2)}, u32[]{:S(2)}) collective-permute-start(bf16[4,3,128,256]{3,2,1,0:T(8,128)(2,1)} %pad_maximum_fusion.2.refs_4_), channel_id=1, source_target_pairs={{0,8},{8,0},{1,9},{9,1},{2,10},{10,2},{3,11},{11,3},{32,40},{40,32... | collective-permute-start | bytes 2359304 | tf_op jit(solution)/shard_map/ppermute | solution.py:34
  47.5 5.2 %collective-permute-start.11 = (bf16[64,1024]{1,0:T(8,128)(2,1)S(1)}, bf16[64,1024]{1,0:T(8,128)(2,1)S(1)}, u32[]{:S(2)}, u32[]{:S(2)}) collective-permute-start(bf16[64,1024]{1,0:T(8,128)(2,1)S(1)} %get-tuple-element.116), channel_id=1, source_target_pairs={{0,24},{8,16},{1,25},{9,17},{2,26},{10,18},{3,27},{11,19},{32,56},... | collective-permute-start | bytes 393224 | tf_op jit(solution)/shard_map/ppermute | solution.py:34
  48.1 8.0 %collective-permute-start.10 = (bf16[64,1024]{1,0:T(8,128)(2,1)S(1)}, bf16[64,1024]{1,0:T(8,128)(2,1)S(1)}, u32[]{:S(2)}, u32[]{:S(2)}) collective-permute-start(bf16[64,1024]{1,0:T(8,128)(2,1)S(1)} %get-tuple-element.117), channel_id=1, source_target_pairs={{0,16},{8,24},{1,17},{9,25},{2,18},{10,26},{3,19},{11,27},{32,48},... | collective-permute-start | bytes 393224 | tf_op jit(solution)/shard_map/ppermute | solution.py:34
  49.6 6.5 %collective-permute-start.9 = (bf16[64,1024]{1,0:T(8,128)(2,1)S(1)}, bf16[64,1024]{1,0:T(8,128)(2,1)S(1)}, u32[]{:S(2)}, u32[]{:S(2)}) collective-permute-start(bf16[64,1024]{1,0:T(8,128)(2,1)S(1)} %get-tuple-element.118), channel_id=1, source_target_pairs={{0,8},{8,0},{1,9},{9,1},{2,10},{10,2},{3,11},{11,3},{32,40},{40,32... | collective-permute-start | bytes 393224 | tf_op jit(solution)/shard_map/ppermute | solution.py:34
  57.7 16.5 %collective-permute-start.12 = (bf16[9,128,256]{2,1,0:T(8,128)(2,1)}, bf16[9,128,256]{2,1,0:T(8,128)(2,1)S(1)}, u32[]{:S(2)}, u32[]{:S(2)}) collective-permute-start(bf16[9,128,256]{2,1,0:T(8,128)(2,1)} %shard_map.123), channel_id=1, source_target_pairs={{0,4},{8,12},{1,5},{9,13},{2,6},{10,14},{3,7},{11,15},{32,36},{40,... | collective-permute-start | bytes 1769480 | tf_op jit(solution)/shard_map/ppermute | solution.py:34
  67.1 8.0 %copy-start.5 = (bf16[1,16,8,8,256]{4,3,2,1,0:T(8,128)(2,1)S(1)}, bf16[1,16,8,8,256]{4,3,2,1,0:T(8,128)(2,1)}, u32[]{:S(2)}) copy-start(bf16[1,16,8,8,256]{4,3,2,1,0:T(8,128)(2,1)} %param.10) | copy-start | bytes 1572868
  75.0 7.8 %copy-start.35 = (bf16[64,1024]{1,0:T(8,128)(2,1)S(1)}, bf16[64,1024]{1,0:T(8,128)(2,1)}, u32[]{:S(2)}) copy-start(bf16[64,1024]{1,0:T(8,128)(2,1)} %get-tuple-element.81) | copy-start | bytes 393220
  75.0 7.8 %copy-start.37 = (bf16[64,1024]{1,0:T(8,128)(2,1)S(1)}, bf16[64,1024]{1,0:T(8,128)(2,1)}, u32[]{:S(2)}) copy-start(bf16[64,1024]{1,0:T(8,128)(2,1)} %get-tuple-element.80) | copy-start | bytes 393220
  75.0 7.8 %copy-start.39 = (bf16[64,1024]{1,0:T(8,128)(2,1)S(1)}, bf16[64,1024]{1,0:T(8,128)(2,1)}, u32[]{:S(2)}) copy-start(bf16[64,1024]{1,0:T(8,128)(2,1)} %get-tuple-element.79) | copy-start | bytes 393220
  75.1 70.1 %all-gather.13.cloned.1.call-start = ((), (), s32[]{:S(2)}) async-start(), calls=%async_computation.4 | async-start | bytes 2621440 | tf_op jit(solution)/shard_map/all_gather | solution.py:293
  75.9 16.1 %collective-permute-start.13 = (bf16[1024,256]{1,0:T(8,128)(2,1)}, bf16[1024,256]{1,0:T(8,128)(2,1)S(1)}, u32[]{:S(2)}, u32[]{:S(2)}) collective-permute-start(bf16[1024,256]{1,0:T(8,128)(2,1)} %get-tuple-element.68), channel_id=1, source_target_pairs={{0,1},{8,9},{1,2},{9,10},{2,3},{10,11},{3,0},{11,8},{32,33},{40,41... | collective-permute-start | bytes 1572872 | tf_op jit(solution)/shard_map/ppermute | solution.py:34
  77.8 23.5 %collective-permute-start.14 = (bf16[1024,256]{1,0:T(8,128)(2,1)}, bf16[1024,256]{1,0:T(8,128)(2,1)S(1)}, u32[]{:S(2)}, u32[]{:S(2)}) collective-permute-start(bf16[1024,256]{1,0:T(8,128)(2,1)} %get-tuple-element.69), channel_id=1, source_target_pairs={{0,3},{8,11},{1,0},{9,8},{2,1},{10,9},{3,2},{11,10},{32,35},{40,43... | collective-permute-start | bytes 1572872 | tf_op jit(solution)/shard_map/ppermute | solution.py:34
  79.9 23.3 %collective-permute-start.15 = (bf16[1024,256]{1,0:T(8,128)(2,1)}, bf16[1024,256]{1,0:T(8,128)(2,1)S(1)}, u32[]{:S(2)}, u32[]{:S(2)}) collective-permute-start(bf16[1024,256]{1,0:T(8,128)(2,1)} %get-tuple-element.70), channel_id=1, source_target_pairs={{0,2},{8,10},{1,3},{9,11},{2,0},{10,8},{3,1},{11,9},{32,34},{40,42... | collective-permute-start | bytes 1572872 | tf_op jit(solution)/shard_map/ppermute | solution.py:34
  81.8 21.3 %collective-permute-start.17 = (bf16[16,64,256]{2,1,0:T(8,128)(2,1)}, bf16[16,64,256]{2,1,0:T(8,128)(2,1)}, u32[]{:S(2)}, u32[]{:S(2)}) collective-permute-start(bf16[16,64,256]{2,1,0:T(8,128)(2,1)} %shard_map.125), channel_id=1, source_target_pairs={{0,20},{8,28},{1,21},{9,29},{2,22},{10,30},{3,23},{11,31},{32,52},... | collective-permute-start | bytes 1572872 | tf_op jit(solution)/shard_map/ppermute | solution.py:34
  82.9 20.3 %collective-permute-start.16 = (bf16[16,64,256]{2,1,0:T(8,128)(2,1)}, bf16[16,64,256]{2,1,0:T(8,128)(2,1)}, u32[]{:S(2)}, u32[]{:S(2)}) collective-permute-start(bf16[16,64,256]{2,1,0:T(8,128)(2,1)} %shard_map.125), channel_id=1, source_target_pairs={{0,16},{8,24},{1,17},{9,25},{2,18},{10,26},{3,19},{11,27},{32,48},... | collective-permute-start | bytes 1572872 | tf_op jit(solution)/shard_map/ppermute | solution.py:34
  84.7 154.6 %reduce-scatter.2.cloned.1.call-start = ((), (), s32[]{:S(2)}) async-start(), calls=%async_computation.1 | async-start | bytes 983040 | tf_op jit(solution)/shard_map/reduce_scatter | solution.py:326
  92.0 11.1 %copy-start.16 = (bf16[1024,256]{1,0:T(8,128)(2,1)}, bf16[1024,256]{1,0:T(8,128)(2,1)S(1)}, u32[]{:S(2)}) copy-start(bf16[1024,256]{1,0:T(8,128)(2,1)S(1)} %collective-permute-done.13.refs_0_) | copy-start | bytes 1572868
  107.1 16.7 %collective-permute-start.19 = (bf16[4,16,64,256]{3,2,1,0:T(8,128)(2,1)}, bf16[4,16,64,256]{3,2,1,0:T(8,128)(2,1)}, u32[]{:S(2)}, u32[]{:S(2)}) collective-permute-start(bf16[4,16,64,256]{3,2,1,0:T(8,128)(2,1)} %pad_maximum_fusion), channel_id=1, source_target_pairs={{0,8},{8,0},{1,9},{9,1},{2,10},{10,2},{3,11},{11,3},{32,40},{40,32... | collective-permute-start | bytes 6291464 | tf_op jit(solution)/shard_map/ppermute | solution.py:34
  107.7 16.9 %copy-start.2 = (bf16[16,64,256]{2,0,1:T(8,128)(2,1)}, bf16[16,64,256]{2,0,1:T(8,128)(2,1)S(1)}, u32[]{:S(2)}) copy-start(bf16[16,64,256]{2,0,1:T(8,128)(2,1)S(1)} %copy.80) | copy-start | bytes 1572868
  107.7 16.1 %collective-permute-start.18 = (bf16[8,8,16,256]{3,2,1,0:T(8,128)(2,1)S(1)}, bf16[8,8,16,256]{3,2,1,0:T(8,128)(2,1)S(1)}, u32[]{:S(2)}, u32[]{:S(2)}) collective-permute-start(bf16[8,8,16,256]{3,2,1,0:T(8,128)(2,1)S(1)} %bitcast.113), channel_id=1, source_target_pairs={{0,4},{8,12},{1,5},{9,13},{2,6},{10,14},{3,7},{11,15},{32,36},{40,... | collective-permute-start | bytes 1572872 | tf_op jit(solution)/shard_map/ppermute | solution.py:34
  133.7 20.8 %collective-permute-start.23 = (bf16[8,8,16,256]{3,2,1,0:T(8,128)(2,1)}, bf16[8,8,16,256]{3,2,1,0:T(8,128)(2,1)S(1)}, u32[]{:S(2)}, u32[]{:S(2)}) collective-permute-start(bf16[8,8,16,256]{3,2,1,0:T(8,128)(2,1)} %shard_map.129.refs_6_), channel_id=1, source_target_pairs={{0,20},{8,28},{1,21},{9,29},{2,22},{10,30},{3,23},{11,31},{32,52},... | collective-permute-start | bytes 1572872 | tf_op jit(solution)/shard_map/ppermute | solution.py:34
  134.9 19.6 %collective-permute-start.22 = (bf16[8,8,16,256]{3,2,1,0:T(8,128)(2,1)}, bf16[8,8,16,256]{3,2,1,0:T(8,128)(2,1)}, u32[]{:S(2)}, u32[]{:S(2)}) collective-permute-start(bf16[8,8,16,256]{3,2,1,0:T(8,128)(2,1)} %shard_map.129.refs_6_), channel_id=1, source_target_pairs={{0,16},{8,24},{1,17},{9,25},{2,18},{10,26},{3,19},{11,27},{32,48},... | collective-permute-start | bytes 1572872 | tf_op jit(solution)/shard_map/ppermute | solution.py:34
  135.2 19.4 %collective-permute-start.20 = (bf16[1024,256]{1,0:T(8,128)(2,1)}, bf16[1024,256]{1,0:T(8,128)(2,1)S(1)}, u32[]{:S(2)}, u32[]{:S(2)}) collective-permute-start(bf16[1024,256]{1,0:T(8,128)(2,1)} %get-tuple-element.78.refs_1_), channel_id=1, source_target_pairs={{0,1},{8,9},{1,2},{9,10},{2,3},{10,11},{3,0},{11,8},{32,33},{40,41... | collective-permute-start | bytes 1572872 | tf_op jit(solution)/shard_map/ppermute | solution.py:34
  136.3 18.2 %collective-permute-start.21 = (bf16[1024,256]{1,0:T(8,128)(2,1)}, bf16[1024,256]{1,0:T(8,128)(2,1)S(1)}, u32[]{:S(2)}, u32[]{:S(2)}) collective-permute-start(bf16[1024,256]{1,0:T(8,128)(2,1)} %get-tuple-element.83), channel_id=1, source_target_pairs={{0,3},{8,11},{1,0},{9,8},{2,1},{10,9},{3,2},{11,10},{32,35},{40,43... | collective-permute-start | bytes 1572872 | tf_op jit(solution)/shard_map/ppermute | solution.py:34
  158.8 16.9 %collective-permute-start.25 = (bf16[4,8,8,16,256]{4,3,2,1,0:T(8,128)(2,1)}, bf16[4,8,8,16,256]{4,3,2,1,0:T(8,128)(2,1)}, u32[]{:S(2)}, u32[]{:S(2)}) collective-permute-start(bf16[4,8,8,16,256]{4,3,2,1,0:T(8,128)(2,1)} %pad_maximum_fusion.1), channel_id=1, source_target_pairs={{0,8},{8,0},{1,9},{9,1},{2,10},{10,2},{3,11},{11,3},{32,40},{40,32... | collective-permute-start | bytes 6291464 | tf_op jit(solution)/shard_map/ppermute | solution.py:34
  159.9 15.8 %collective-permute-start.24 = (bf16[1024,256]{1,0:T(8,128)(2,1)S(1)}, bf16[1024,256]{1,0:T(8,128)(2,1)S(1)}, u32[]{:S(2)}, u32[]{:S(2)}) collective-permute-start(bf16[1024,256]{1,0:T(8,128)(2,1)S(1)} %copy-done.33), channel_id=1, source_target_pairs={{0,2},{8,10},{1,3},{9,11},{2,0},{10,8},{3,1},{11,9},{32,34},{40,42... | collective-permute-start | bytes 1572872 | tf_op jit(solution)/shard_map/ppermute | solution.py:34
  198.2 24.1 %copy-start.7 = (f32[1024,256]{1,0:T(8,128)S(1)}, f32[1024,256]{1,0:T(8,128)}, u32[]{:S(2)}) copy-start(f32[1024,256]{1,0:T(8,128)} %get-tuple-element.107) | copy-start | bytes 3145732
  198.3 24.3 %copy-start.6 = (bf16[1,16,8,8,256]{4,3,2,1,0:T(8,128)(2,1)S(1)}, bf16[1,16,8,8,256]{4,3,2,1,0:T(8,128)(2,1)}, u32[]{:S(2)}) copy-start(bf16[1,16,8,8,256]{4,3,2,1,0:T(8,128)(2,1)} %param.10) | copy-start | bytes 1572868
  198.3 30.1 %collective-permute-start.28 = (bf16[9,64,512]{2,1,0:T(8,128)(2,1)S(1)}, bf16[9,64,512]{2,1,0:T(8,128)(2,1)}, u32[]{:S(2)}, u32[]{:S(2)}) collective-permute-start(bf16[9,64,512]{2,1,0:T(8,128)(2,1)S(1)} %get-tuple-element.108), channel_id=1, source_target_pairs={{0,96},{8,104},{1,97},{9,105},{2,98},{10,106},{3,99},{11,107},{32,... | collective-permute-start | bytes 1769480 | tf_op jit(solution)/shard_map/ppermute | solution.py:34
  203.2 25.3 %collective-permute-start.27 = (bf16[9,64,512]{2,1,0:T(8,128)(2,1)S(1)}, bf16[9,64,512]{2,1,0:T(8,128)(2,1)}, u32[]{:S(2)}, u32[]{:S(2)}) collective-permute-start(bf16[9,64,512]{2,1,0:T(8,128)(2,1)S(1)} %get-tuple-element.109), channel_id=1, source_target_pairs={{0,64},{8,72},{1,65},{9,73},{2,66},{10,74},{3,67},{11,75},{32,96},... | collective-permute-start | bytes 1769480 | tf_op jit(solution)/shard_map/ppermute | solution.py:34
  204.2 27.9 %collective-permute-start.26 = (bf16[9,64,512]{2,1,0:T(8,128)(2,1)S(1)}, bf16[9,64,512]{2,1,0:T(8,128)(2,1)}, u32[]{:S(2)}, u32[]{:S(2)}) collective-permute-start(bf16[9,64,512]{2,1,0:T(8,128)(2,1)S(1)} %get-tuple-element.110), channel_id=1, source_target_pairs={{0,32},{8,40},{1,33},{9,41},{2,34},{10,42},{3,35},{11,43},{32,64},... | collective-permute-start | bytes 1769480 | tf_op jit(solution)/shard_map/ppermute | solution.py:34
  232.1 8.8 %copy-start.32 = (f32[16,2,256]{2,1,0:T(2,128)S(1)}, f32[16,2,256]{2,1,0:T(2,128)}, u32[]{:S(2)}) copy-start(f32[16,2,256]{2,1,0:T(2,128)} %get-tuple-element.98.refs_1_) | copy-start | bytes 98308
  234.8 25.5 %collective-permute-start.29 = (bf16[9,64,256]{2,1,0:T(8,128)(2,1)}, bf16[9,64,256]{2,1,0:T(8,128)(2,1)S(1)}, u32[]{:S(2)}, u32[]{:S(2)}) collective-permute-start(bf16[9,64,256]{2,1,0:T(8,128)(2,1)} %get-tuple-element.96), channel_id=1, source_target_pairs={{0,0},{8,4},{1,1},{9,5},{2,2},{10,6},{3,3},{11,7},{32,32},{40,36},... | collective-permute-start | bytes 884744 | tf_op jit(solution)/shard_map/ppermute | solution.py:34
  236.7 23.6 %collective-permute-start.30 = (bf16[9,64,256]{2,1,0:T(8,128)(2,1)}, bf16[9,64,256]{2,1,0:T(8,128)(2,1)S(1)}, u32[]{:S(2)}, u32[]{:S(2)}) collective-permute-start(bf16[9,64,256]{2,1,0:T(8,128)(2,1)} %get-tuple-element.97), channel_id=1, source_target_pairs={{0,4},{8,0},{1,5},{9,1},{2,6},{10,2},{3,7},{11,3},{32,36},{40,32},... | collective-permute-start | bytes 884744 | tf_op jit(solution)/shard_map/ppermute | solution.py:34
  240.9 19.2 %collective-permute-start.31 = (bf16[3,64,256]{2,1,0:T(8,128)(2,1)}, bf16[3,64,256]{2,1,0:T(8,128)(2,1)S(1)}, u32[]{:S(2)}, u32[]{:S(2)}) collective-permute-start(bf16[3,64,256]{2,1,0:T(8,128)(2,1)} %get-tuple-element.99), channel_id=1, source_target_pairs={{0,0},{8,4},{1,1},{9,5},{2,2},{10,6},{3,3},{11,7},{32,32},{40,36},... | collective-permute-start | bytes 294920 | tf_op jit(solution)/shard_map/ppermute | solution.py:34
  247.5 12.7 %collective-permute-start.32 = (bf16[3,64,256]{2,1,0:T(8,128)(2,1)}, bf16[3,64,256]{2,1,0:T(8,128)(2,1)S(1)}, u32[]{:S(2)}, u32[]{:S(2)}) collective-permute-start(bf16[3,64,256]{2,1,0:T(8,128)(2,1)} %get-tuple-element.100), channel_id=1, source_target_pairs={{0,4},{8,0},{1,5},{9,1},{2,6},{10,2},{3,7},{11,3},{32,36},{40,32},... | collective-permute-start | bytes 294920 | tf_op jit(solution)/shard_map/ppermute | solution.py:34
  (38 other events, 78.9 us)
Sparse Core Ops, SparseCore 0:
  22.9 35.0 all-gather.8
  75.2 36.0 all-gather.10
  113.0 32.1 all-gather.12
  169.9 24.6 reduce-scatter.1

commit v3 on v2

--- a/solution.py
+++ b/solution.py
@@ -166,7 +166,7 @@
 
 def wgrad_body(first, spatial, lefts, index, *refs):
     left, (mine, other, pair, both, swapped) = refs[:lefts], refs[lefts : lefts + 5]
-    out, padded = refs[-2:]
+    outs, padded = refs[-5:-1] if spatial else refs[-2:-1], refs[-1]
     step = pl.program_id(0)
 
     @pl.when(step == 0)
@@ -180,11 +180,25 @@
     blocks = jnp.concatenate([ref[...].reshape(-1, 4 * ROWS) for ref in left], axis=0)
     result = contract_inner(blocks, right.reshape(4 * ROWS, 2 * CH))
     result = result.astype(BF)
+    if not spatial:
+        for block in range(4):
+            outs[0][index[block], 0] = result[block * SUB : (block + 1) * SUB]
+        return
     for block in range(4):
-        out[index[block], 0] = result[block * SUB : (block + 1) * SUB]
+        for place in range(4):
+
+            @pl.when(index[block] == place)
+            def _():
+                outs[place][0] = result[block * SUB : (block + 1) * SUB]
 
 
 def wgrad(spatial, first, taps, index, left, fields, *waits):
+    if spatial:
+        out_specs = [pl.BlockSpec((1, SUB, 2 * CH), lambda i, ix: (i, 0, 0))] * 4
+        out_shape = [jax.ShapeDtypeStruct((taps, SUB, 2 * CH), BF)] * 4
+    else:
+        out_specs = pl.BlockSpec((4, 1, SUB, 2 * CH), lambda i, ix: (0, i, 0, 0))
+        out_shape = jax.ShapeDtypeStruct((4, taps, SUB, 2 * CH), BF)
     return pl.pallas_call(
         lambda *refs: wgrad_body(first, spatial, len(left), *refs),
         grid_spec=pltpu.PrefetchScalarGridSpec(
@@ -192,10 +206,10 @@
             grid=(taps,),
             in_specs=[whole(f.shape) for f in left + fields]
             + [pl.BlockSpec(memory_space=pl.ANY)] * len(waits),
-            out_specs=pl.BlockSpec((4, 1, SUB, 2 * CH), lambda i, ix: (0, i, 0, 0)),
+            out_specs=out_specs,
             scratch_shapes=[pltpu.VMEM((4,) + pad_shape(spatial), BF)],
         ),
-        out_shape=jax.ShapeDtypeStruct((4, taps, SUB, 2 * CH), BF),
+        out_shape=out_shape,
         compiler_params=params(),
         cost_estimate=cost(4.7 + 1.25 * taps),
     )(index, *left, *fields, *waits)
@@ -251,15 +265,14 @@
         return lax.dynamic_slice_in_dim(kernel, start, 128, axis=1)
 
     tk_part = send(kernel_part(temporal_kernel), to_half)
-    own, parts = exchange(spatial_out.reshape(ROWS, CH).T.reshape(4, SUB, ROWS))
-    tk_part, *parts = together(tk_part, *parts)
+    tk_parts = [send(tk_part, to_y(k)) for k in (1, 2, 3)]
+    cot_other = send(after(cot, tk_part), to_half)
+    turned = spatial_out.reshape(ROWS, CH).T.reshape(4, SUB, ROWS)
+    own, parts = exchange(after(turned, tk_part))
+    cot_other, tk_one, tk_two, tk_three, *parts = together(cot_other, *tk_parts, *parts)
+    tk_near = jnp.stack([tk_part, tk_one, tk_two, tk_three])
     saved_part = jnp.concatenate([own, *parts], axis=1)
     saved_left = (lax.all_gather(saved_part, "mp", axis=0, axis_index_groups=z_groups),)
-
-    tk_parts = [send(tk_part, to_y(k)) for k in (1, 2, 3)]
-    cot_other = send(cot, to_half)
-    cot_other, *tk_parts = together(cot_other, *tk_parts)
-    tk_near = jnp.stack([tk_part, *tk_parts])
 
     flat_in = block_input.reshape(FR, HT * WD, CH).transpose(1, 0, 2).reshape(ROWS, CH).astype(F32)
     count = ROWS * (C // G)
@@ -287,48 +300,49 @@
         return mine + (one + three) + two
 
     tk_far = send(tk_near, to_core)
-    own, parts = exchange(hidden.T.reshape(4, SUB, ROWS))
-    tk_far, *parts = together(tk_far, *parts)
-    hidden_part = jnp.concatenate([own, *parts], axis=1)
-    hidden_left = (lax.all_gather(hidden_part, "mp", axis=0, axis_index_groups=z_groups),)
-
     arrays = (cot, cot_other, temporal_kernel, tk_near, tk_far)
     sk_part = send(after(kernel_part(spatial_kernel), tk_far), to_half)
-    up, down, far, mine = blocks_of(False, (1, 3, 2, 0), *arrays, *saved_left)
+    up, down, far, mine = blocks_of(False, (1, 3, 2, 0), *arrays)
     sk_part, up, down, far = together(sk_part, up, down, far)
     sk_other = lax.all_gather(sk_part, "dp", axis=0, axis_index_groups=y_core_groups)
-    up, down, far = send(up, to_z(1)), send(down, to_z(3)), send(far, to_z(2))
+
+    up, down = send(up, to_z(1)), send(down, to_z(3))
     cot_late = after(cot, mine)
     cot_pair, cot_both = send(cot_late, to_pair), send(cot_late, to_both)
     up, down, far, cot_pair, cot_both = together(up, down, far, cot_pair, cot_both)
+
+    far = send(far, to_z(2))
+    cot_near = (cot, cot_other, cot_pair, cot_both)
+    cot_swapped = send(jnp.stack(cot_near), to_core)
+    own, parts = exchange(after(hidden.T.reshape(4, SUB, ROWS), up))
+    far, cot_swapped, *parts = together(far, cot_swapped, *parts)
+    hidden_part = jnp.concatenate([own, *parts], axis=1)
+    hidden_left = (lax.all_gather(hidden_part, "mp", axis=0, axis_index_groups=z_groups),)
     saved_grad = total_of(mine, (up, far, down)).astype(BF)
     saved_grad = saved_grad.reshape(FR, HT * WD, CH).transpose(1, 0, 2).reshape(HT, WD, FR, CH)
 
     sg_other = send(saved_grad, to_half)
-    cot_near = (cot, cot_other, cot_pair, cot_both)
-    cot_swapped = send(jnp.stack(cot_near), to_core)
-    sg_other, cot_swapped = together(sg_other, cot_swapped)
+    slots = jnp.array([[0, 2, 1, 3], [2, 0, 3, 1]], jnp.int32)[half]
+    fields = cot_near + (cot_swapped,)
+    temporal_parts = wgrad(False, 0, 3, slots, saved_left, fields, saved_grad)
+    sg_other, temporal_parts = together(sg_other, temporal_parts)
+    temporal_total = lax.psum_scatter(
+        temporal_parts, "dp", scatter_dimension=0, axis_index_groups=y_groups
+    )
 
     arrays = (saved_grad, sg_other, spatial_kernel, sk_other, sk_other)
     up, down = blocks_of(True, (1, 3), *arrays)
     sg_late = after(saved_grad, up)
     up, down = send(up, to_z(1)), send(down, to_z(3))
     sg_pair, sg_both = send(sg_late, to_pair), send(sg_late, to_both)
-    far, mine = blocks_of(True, (2, 0), *arrays, sg_late, *hidden_left)
+    far, mine = blocks_of(True, (2, 0), *arrays, sg_late)
     up, down, far, sg_pair, sg_both = together(up, down, far, sg_pair, sg_both)
 
+    sg_near = (saved_grad, sg_other, sg_pair, sg_both)
+    sg_fields = sg_near + (send(jnp.stack(sg_near), to_core),)
     far = send(far, to_z(2))
-    sg_near = (saved_grad, sg_other, sg_pair, sg_both)
-    sg_swapped = send(jnp.stack(sg_near), to_core)
-
-    slots = jnp.array([[0, 2, 1, 3], [2, 0, 3, 1]], jnp.int32)[half]
-    temporal_parts = wgrad(False, 0, 3, slots, saved_left, cot_near + (cot_swapped,), up)
-    temporal_total = lax.psum_scatter(
-        temporal_parts, "dp", scatter_dimension=0, axis_index_groups=y_groups
-    )
-    far, sg_swapped = together(far, sg_swapped)
-    order = (slots - y) % 4
-    parts = wgrad(True, 0, 9, order, hidden_left, sg_near + (sg_swapped,), temporal_parts)
+    parts = wgrad(True, 0, 9, (slots - y) % 4, hidden_left, sg_fields)
+    far, *parts = together(far, *parts)
     hidden_grad = total_of(mine, (up, far, down))
 
     normed_grad = hidden_grad * gate * (1.0 + normed * (1.0 - gate))
@@ -352,18 +366,17 @@
         low, high = jnp.where(half == 0, first, second), jnp.where(half == 0, second, first)
         return jnp.concatenate([low, high], axis=1).astype(F32)
 
-    sums = after(jnp.stack([gain_sum, bias_sum]), parts)
-    sums = lax.all_gather(sums, "dp", axis=0)
+    sums = lax.all_gather(jnp.stack([gain_sum, bias_sum]), "dp", axis=0)
+    temporal_owned = to_owners(after(temporal_total, parts[0]))
     others = [send(parts[k], to_y(k)) for k in (1, 2, 3)]
-    *others, sums = together(*others, sums)
+    *others, sums, tk_first, tk_second = together(*others, sums, *temporal_owned)
     total = parts[0].astype(F32)
     for other in others:
         total = total + other.astype(F32)
-    owned_parts = together(*to_owners(total), *to_owners(after(temporal_total, sums)))
-    spatial_owned, temporal_owned = owned_parts[:2], owned_parts[2:]
+    first, second = to_owners(total)
     sums = jnp.sum(sums, axis=0)
-    temporal_grad = owned(*temporal_owned)
-    spatial_grad = owned(*spatial_owned).reshape(3, 3, CH // 2, CH)
+    temporal_grad = owned(tk_first, tk_second)
+    spatial_grad = owned(first, second).reshape(3, 3, CH // 2, CH)
     return (input_grad, spatial_grad, temporal_grad, sums[0], sums[1])
 
 

time: 273 us -> 253 us (0.927)
  waiting for transfers between devices: 88.1 us -> 67.3 us
  other arithmetic: 27.6 us -> 23.5 us
  blocking collectives: 17.2 us -> 20.3 us
    ppermute x33, waiting for transfers between devices: 81.2 us -> 67.2 us  [send(): return lax.ppermute(value, ('dp', 'mp'), pairs)]
    all_gather x1, waiting for transfers between devices: 6.78 us -> 0.01 us  [local(): lax.all_gather(hidden_part, 'mp', axis=0, axis_index_groups=z_groups)]
    all_gather x1, blocking collectives: 17.2 us -> 20.3 us  [local(): sums = lax.all_gather(jnp.stack([gain_sum, bias_sum]), 'dp', axis=0)]
    another operation x3 -> x2, other arithmetic: 5.68 us -> 4.28 us  [the longest x1 3.06 us: local(): sg_fields = sg_near + (send(jnp.stack(sg_near), to_core),)]
    unnamed x100 -> x105, local copies, waits for them, and re-layouts: 12.8 us -> 12 us
  transfers between devices with their start and end apart: 37 -> 37, of which waited for: 18 -> 16; matrix products, arithmetic and copies ran while one was open for 11% -> 13% of each run, Pallas kernels for 19% -> 21%
where the time goes in v3:
time: 253 us; the launch traced here: 252 us
  waiting for transfers between devices  67.3 us (27%)
  Pallas kernels  52.7 us (21%)
  starting transfers between devices  48.1 us (19%)
  local copies, waits for them, and re-layouts  25.6 us (10%)
  other arithmetic  23.5 us (9%)
  blocking collectives  20.3 us (8%)
  between operations  14.4 us (6%)
    ppermute x33, waiting for transfers between devices, send(): return lax.ppermute(value, ('dp', 'mp'), pairs)  67.2 us
    ppermute x33, starting transfers between devices, send(): return lax.ppermute(value, ('dp', 'mp'), pairs)  47.8 us
    pallas_call x3, Pallas kernels, dgrad(): pl.pallas_call(lambda *refs: dgrad_body(spatial, blocks, *refs), grid_spe...  26.7 us
    pallas_call x2, Pallas kernels, wgrad(): pl.pallas_call(lambda *refs: wgrad_body(first, spatial, len(left), *refs)...  26 us
    all_gather x1, blocking collectives, local(): sums = lax.all_gather(jnp.stack([gain_sum, bias_sum]), 'dp', axis=0)  20.3 us
    unnamed x105, local copies, waits for them, and re-layouts  12 us
  transfers between devices with their start and end apart: 37, of which 16 were waited for; matrix products, arithmetic and copies ran while one was open for 13% of the time, Pallas kernels for 21%

profile of v3, /device:TPU:6, one launch (start us, length us, event | category | flops | bytes accessed | tf_op | source)
XLA Modules:
  0.0 251.8 jit_solution(2772418210530267040)
XLA Ops:
  8.3 1.5 collective-permute-start
  9.8 1.9 copy.86.refs_0_
  11.6 4.9 %collective-permute-done.refs_1_ = bf16[3,128,256]{2,1,0:T(8,128)(2,1)S(1)} collective-permute-done((bf16[3,128,256]{2,1,0:T(8,128)(2,1)S(1)}, bf16[3,128,256]{2,1,0:T(8,128)(2,1)S(1)}, u32[]{:S(2)}, u32[]{:S(2)}) %collective-permute-start) | collective-permute-done | bytes 196640 | tf_op jit(solution)/shard_map/ppermute | solution.py:34
  17.2 1.4 collective-permute-start.1
  20.9 1.6 collective-permute-start.2
  22.6 2.9 %collective-permute-start.3 = (bf16[3,128,256]{2,1,0:T(8,128)(2,1)S(1)}, bf16[3,128,256]{2,1,0:T(8,128)(2,1)S(1)}, u32[]{:S(2)}, u32[]{:S(2)}) collective-permute-start(bf16[3,128,256]{2,1,0:T(8,128)(2,1)S(1)} %copy-done.25), channel_id=1, source_target_pairs={{0,64},{8,72},{1,65},{9,73},{2,66},{10,74},{3,67},{11,75},{32,96},... | collective-permute-start | bytes 589832 | tf_op jit(solution)/shard_map/ppermute | solution.py:34
  26.8 5.3 %collective-permute-done.6.refs_5_ = bf16[64,1024]{1,0:T(8,128)(2,1)S(1)} collective-permute-done((bf16[64,1024]{1,0:T(8,128)(2,1)S(1)}, bf16[64,1024]{1,0:T(8,128)(2,1)S(1)}, u32[]{:S(2)}, u32[]{:S(2)}) %collective-permute-start.6) | collective-permute-done | bytes 131104 | tf_op jit(solution)/shard_map/ppermute | solution.py:34
  32.1 4.9 %collective-permute-done.7.refs_6_ = bf16[64,1024]{1,0:T(8,128)(2,1)S(1)} collective-permute-done((bf16[64,1024]{1,0:T(8,128)(2,1)S(1)}, bf16[64,1024]{1,0:T(8,128)(2,1)S(1)}, u32[]{:S(2)}, u32[]{:S(2)}) %collective-permute-start.7) | collective-permute-done | bytes 131104 | tf_op jit(solution)/shard_map/ppermute | solution.py:34
  38.7 1.9 pad_maximum_fusion.3
  43.2 1.9 constant_dynamic-slice_fusion.1.refs_0_
  46.1 3.3 %collective-permute-start.9 = (bf16[9,128,256]{2,1,0:T(8,128)(2,1)}, bf16[9,128,256]{2,1,0:T(8,128)(2,1)S(1)}, u32[]{:S(2)}, u32[]{:S(2)}) collective-permute-start(bf16[9,128,256]{2,1,0:T(8,128)(2,1)} %shard_map.123), channel_id=1, source_target_pairs={{0,4},{8,12},{1,5},{9,13},{2,6},{10,14},{3,7},{11,15},{32,36},{40,... | collective-permute-start | bytes 1769480 | tf_op jit(solution)/shard_map/ppermute | solution.py:34
  49.4 8.3 %shard_map.122 = (bf16[1024,256]{1,0:T(8,128)(2,1)}, bf16[1024,256]{1,0:T(8,128)(2,1)}, bf16[1024,256]{1,0:T(8,128)(2,1)}, f32[1024,256]{1,0:T(8,128)}) custom-call(s32[13]{0:T(128)} %stack.130.refs_0_, bf16[16,64,256]{2,1,0:T(8,128)(2,1)} %bitcast.104, bf16[16,64,256]{2,1,0:T(8,128)(2,1)} %get-tuple-element.60.refs_2_.refs_3_, ...), custom_call_target="tpu_custom_call" | custom-call | flops 8049999872 | tf_op jit(solution)/shard_map/pallas_call | solution.py:145
  57.7 5.8 %collective-permute-done.9.refs_0_ = bf16[9,128,256]{2,1,0:T(8,128)(2,1)S(1)} collective-permute-done((bf16[9,128,256]{2,1,0:T(8,128)(2,1)}, bf16[9,128,256]{2,1,0:T(8,128)(2,1)S(1)}, u32[]{:S(2)}, u32[]{:S(2)}) %collective-permute-start.9) | collective-permute-done | bytes 589856 | tf_op jit(solution)/shard_map/ppermute | solution.py:34
  66.4 2.6 %collective-permute-start.13 = (bf16[16,64,256]{2,1,0:T(8,128)(2,1)}, bf16[16,64,256]{2,1,0:T(8,128)(2,1)S(1)}, u32[]{:S(2)}, u32[]{:S(2)}) collective-permute-start(bf16[16,64,256]{2,1,0:T(8,128)(2,1)} %shard_map.125), channel_id=1, source_target_pairs={{0,20},{8,28},{1,21},{9,29},{2,22},{10,30},{3,23},{11,31},{32,52},... | collective-permute-start | bytes 1572872 | tf_op jit(solution)/shard_map/ppermute | solution.py:34
  69.0 1.9 collective-permute-start.10
  71.0 2.1 collective-permute-start.11
  73.1 5.8 %collective-permute-done.12.refs_3_ = bf16[16,64,256]{2,1,0:T(8,128)(2,1)S(1)} collective-permute-done((bf16[16,64,256]{2,1,0:T(8,128)(2,1)}, bf16[16,64,256]{2,1,0:T(8,128)(2,1)S(1)}, u32[]{:S(2)}, u32[]{:S(2)}) %collective-permute-start.12) | collective-permute-done | bytes 524320 | tf_op jit(solution)/shard_map/ppermute | solution.py:34
  78.9 2.1 collective-permute-done.13.refs_4_
  81.0 4.9 %collective-permute-done.10.refs_0_ = bf16[1024,256]{1,0:T(8,128)(2,1)S(1)} collective-permute-done((bf16[1024,256]{1,0:T(8,128)(2,1)}, bf16[1024,256]{1,0:T(8,128)(2,1)S(1)}, u32[]{:S(2)}, u32[]{:S(2)}) %collective-permute-start.10) | collective-permute-done | bytes 524320 | tf_op jit(solution)/shard_map/ppermute | solution.py:34
  86.9 3.1 %pad_maximum_fusion = bf16[4,16,64,256]{3,2,1,0:T(8,128)(2,1)} fusion(bf16[1,16,64,256]{3,2,1,0:T(8,128)(2,1)} %bitcast.123, bf16[1,16,64,256]{3,2,1,0:T(8,128)(2,1)} %bitcast.122, bf16[1,16,64,256]{3,2,1,0:T(8,128)(2,1)S(1)} %bitcast.120, bf16[1,16,64,256]{3,2,1,0:T(8,128)(2,1)S(1)} %bitcast.107), kind=kLoop, calls=%fused_computation | loop fusion | flops 3145728 | bytes 4194304 | tf_op jit(solution)/shard_map/stack | solution.py:316
  91.9 1.5 collective-permute-start.14
  94.7 2.0 dynamic-slice_bitcast_fusion
  101.1 2.4 collective-permute-done.17.refs_3_
  103.5 1.6 collective-permute-done.18.refs_4_
  105.1 3.0 %collective-permute-done.14.refs_0_ = bf16[1024,256]{1,0:T(8,128)(2,1)} collective-permute-done((bf16[1024,256]{1,0:T(8,128)(2,1)}, bf16[1024,256]{1,0:T(8,128)(2,1)}, u32[]{:S(2)}, u32[]{:S(2)}) %collective-permute-start.14) | collective-permute-done | bytes 524320 | tf_op jit(solution)/shard_map/ppermute | solution.py:34
  109.9 1.5 collective-permute-start.19
  113.3 8.4 %shard_map.129.refs_1_ = bf16[4,3,64,512]{3,2,1,0:T(8,128)(2,1)} custom-call(s32[4]{0:T(128)} %fusion.4.refs_0_, bf16[4,64,4096]{2,1,0:T(8,128)(2,1)} %bitcast.144, bf16[16,64,256]{2,1,0:T(8,128)(2,1)} %bitcast.105, bf16[16,64,256]{2,1,0:T(8,128)(2,1)} %get-tuple-element.60.refs_2_.refs_3_, bf16[16,64,256]{2,1,0:T(8,128)(2,1)} %get-tuple-element.74.refs_4_, ...), custom_call_target="tpu_custom_call" | custom-call | flops 9717499904 | tf_op jit(solution)/shard_map/pallas_call | solution.py:202
  121.7 3.2 %collective-permute-done.19.refs_0_ = bf16[8,8,16,256]{3,2,1,0:T(8,128)(2,1)S(1)} collective-permute-done((bf16[8,8,16,256]{3,2,1,0:T(8,128)(2,1)S(1)}, bf16[8,8,16,256]{3,2,1,0:T(8,128)(2,1)S(1)}, u32[]{:S(2)}, u32[]{:S(2)}) %collective-permute-start.19) | collective-permute-done | bytes 524320 | tf_op jit(solution)/shard_map/ppermute | solution.py:34
  125.8 9.1 %shard_map.131 = (bf16[1024,256]{1,0:T(8,128)(2,1)}, bf16[1024,256]{1,0:T(8,128)(2,1)}) custom-call(s32[7]{0:T(128)} %stack.144.refs_0_, bf16[8,8,16,256]{3,2,1,0:T(8,128)(2,1)} %bitcast.113, bf16[8,8,16,256]{3,2,1,0:T(8,128)(2,1)} %get-tuple-element.81.refs_2_.refs_3_, bf16[9,2048,256]{2,1,0:T(8,128)(2,1)} %bitcast.134, bf16[8,9,128,256]{3,2,1,0:T(8,128)(2,1)} %bitcast.140, ...), custom_call_target="tpu_custom_call" | custom-call | flops 9660000256 | tf_op jit(solution)/shard_map/pallas_call | solution.py:145
  137.1 3.1 %collective-permute-start.21 = (bf16[1024,256]{1,0:T(8,128)(2,1)}, bf16[1024,256]{1,0:T(8,128)(2,1)S(1)}, u32[]{:S(2)}, u32[]{:S(2)}) collective-permute-start(bf16[1024,256]{1,0:T(8,128)(2,1)} %get-tuple-element.85), channel_id=1, source_target_pairs={{0,3},{8,11},{1,0},{9,8},{2,1},{10,9},{3,2},{11,10},{32,35},{40,43... | collective-permute-start | bytes 1572872 | tf_op jit(solution)/shard_map/ppermute | solution.py:34
  140.2 9.3 %shard_map.133 = (bf16[1024,256]{1,0:T(8,128)(2,1)}, f32[1024,256]{1,0:T(8,128)}) custom-call(s32[7]{0:T(128)} %stack.122.refs_0_, bf16[8,8,16,256]{3,2,1,0:T(8,128)(2,1)} %bitcast.114, bf16[8,8,16,256]{3,2,1,0:T(8,128)(2,1)} %get-tuple-element.81.refs_2_.refs_3_, bf16[9,2048,256]{2,1,0:T(8,128)(2,1)} %bitcast.135, bf16[8,9,128,256]{3,2,1,0:T(8,128)(2,1)} %bitcast.142, ...), custom_call_target="tpu_custom_call" | custom-call | flops 9660000256 | tf_op jit(solution)/shard_map/pallas_call | solution.py:145
  149.4 5.4 %collective-permute-done.20.refs_0_ = bf16[1024,256]{1,0:T(8,128)(2,1)S(1)} collective-permute-done((bf16[1024,256]{1,0:T(8,128)(2,1)}, bf16[1024,256]{1,0:T(8,128)(2,1)S(1)}, u32[]{:S(2)}, u32[]{:S(2)}) %collective-permute-start.20) | collective-permute-done | bytes 524320 | tf_op jit(solution)/shard_map/ppermute | solution.py:34
  156.0 3.1 %pad_maximum_fusion.1 = bf16[4,8,8,16,256]{4,3,2,1,0:T(8,128)(2,1)} fusion(bf16[1,8,8,16,256]{4,3,2,1,0:T(8,128)(2,1)} %bitcast.54, bf16[1,8,8,16,256]{4,3,2,1,0:T(8,128)(2,1)} %bitcast.121, bf16[1,8,8,16,256]{4,3,2,1,0:T(8,128)(2,1)} %bitcast.124, bf16[1,8,8,16,256]{4,3,2,1,0:T(8,128)(2,1)S(1)} %bitcast.116), kind=kLoop, calls=%fused_computation.1 | loop fusion | flops 3145728 | bytes 4194304 | tf_op jit(solution)/shard_map/stack | solution.py:342
  159.6 1.7 collective-permute-start.24
  161.3 2.3 collective-permute-done.25.refs_6_
  163.5 17.5 %shard_map.135 = (bf16[9,64,512]{2,1,0:T(8,128)(2,1)}, bf16[9,64,512]{2,1,0:T(8,128)(2,1)}, bf16[9,64,512]{2,1,0:T(8,128)(2,1)}, bf16[9,64,512]{2,1,0:T(8,128)(2,1)}) custom-call(s32[4]{0:T(128)} %and_select_fusion.refs_0_, bf16[4,64,4096]{2,1,0:T(8,128)(2,1)} %bitcast.145, bf16[8,8,16,256]{3,2,1,0:T(8,128)(2,1)} %bitcast.115, ...), custom_call_target="tpu_custom_call" | custom-call | flops 18342500352 | tf_op jit(solution)/shard_map/pallas_call | solution.py:202
  182.5 2.3 fusion.5
  185.5 1.5 collective-permute-start.26
  187.0 2.7 %collective-permute-start.27 = (bf16[9,64,512]{2,1,0:T(8,128)(2,1)}, bf16[9,64,512]{2,1,0:T(8,128)(2,1)}, u32[]{:S(2)}, u32[]{:S(2)}) collective-permute-start(bf16[9,64,512]{2,1,0:T(8,128)(2,1)} %get-tuple-element.102), channel_id=1, source_target_pairs={{0,64},{8,72},{1,65},{9,73},{2,66},{10,74},{3,67},{11,75},{32,96},... | collective-permute-start | bytes 1769480 | tf_op jit(solution)/shard_map/ppermute | solution.py:34
  189.7 1.5 collective-permute-start.28
  191.2 1.7 broadcast_select_fusion.6
  192.9 2.2 collective-permute-start.29
  195.1 1.9 collective-permute-start.30
  198.7 20.3 %all-gather.4.refs_3_ = f32[16,2,256]{2,1,0:T(2,128)} all-gather(f32[1,2,256]{2,1,0:T(2,128)S(1)} %maximum_bitcast_fusion), channel_id=5, replica_groups=mesh['dp'=16,'mp'=8] {'dp'}, dimensions={0}, use_global_device_ids=true | all-gather | bytes 34816 | tf_op jit(solution)/shard_map/all_gather | solution.py:369
  220.3 1.8 add_convert_fusion
  222.9 3.4 %collective-permute-start.31 = (bf16[9,64,256]{2,1,0:T(8,128)(2,1)}, bf16[9,64,256]{2,1,0:T(8,128)(2,1)S(1)}, u32[]{:S(2)}, u32[]{:S(2)}) collective-permute-start(bf16[9,64,256]{2,1,0:T(8,128)(2,1)} %get-tuple-element.110), channel_id=1, source_target_pairs={{0,0},{8,4},{1,1},{9,5},{2,2},{10,6},{3,3},{11,7},{32,32},{40,36},... | collective-permute-start | bytes 884744 | tf_op jit(solution)/shard_map/ppermute | solution.py:34
  226.3 1.9 collective-permute-start.32
  229.7 13.3 %collective-permute-done.31 = bf16[9,64,256]{2,1,0:T(8,128)(2,1)S(1)} collective-permute-done((bf16[9,64,256]{2,1,0:T(8,128)(2,1)}, bf16[9,64,256]{2,1,0:T(8,128)(2,1)S(1)}, u32[]{:S(2)}, u32[]{:S(2)}) %collective-permute-start.31) | collective-permute-done | bytes 294944 | tf_op jit(solution)/shard_map/ppermute | solution.py:34
  (215 shorter events, 39.7 us)
Async XLA Ops:
  7.2 11.4 %copy-start.32 = (bf16[1,16,8,8,256]{4,3,2,1,0:T(8,128)(2,1)S(1)}, bf16[1,16,8,8,256]{4,3,2,1,0:T(8,128)(2,1)}, u32[]{:S(2)}) copy-start(bf16[1,16,8,8,256]{4,3,2,1,0:T(8,128)(2,1)} %param.9) | copy-start | bytes 1572868
  7.2 106.1 %all-gather.9.cloned.1.call-start = ((), (), s32[]{:S(2)}) async-start(), calls=%async_computation.2 | async-start | bytes 2621440 | tf_op jit(solution)/shard_map/all_gather | solution.py:275
  8.3 8.2 %collective-permute-start = (bf16[3,128,256]{2,1,0:T(8,128)(2,1)S(1)}, bf16[3,128,256]{2,1,0:T(8,128)(2,1)S(1)}, u32[]{:S(2)}, u32[]{:S(2)}) collective-permute-start(bf16[3,128,256]{2,1,0:T(8,128)(2,1)S(1)} %constant_dynamic-slice_fusion.2), channel_id=1, source_target_pairs={{0,4},{8,12},{1,5},{9,13},{2,6},{10,14},{3,7},{11,15},{32,36},{40,... | collective-permute-start | bytes 589832 | tf_op jit(solution)/shard_map/ppermute | solution.py:34
  17.2 19.9 %collective-permute-start.1 = (bf16[16,64,256]{2,1,0:T(8,128)(2,1)}, bf16[16,64,256]{2,1,0:T(8,128)(2,1)S(1)}, u32[]{:S(2)}, u32[]{:S(2)}) collective-permute-start(bf16[16,64,256]{2,1,0:T(8,128)(2,1)} %shard_map.119), channel_id=1, source_target_pairs={{0,4},{8,12},{1,5},{9,13},{2,6},{10,14},{3,7},{11,15},{32,36},{40,... | collective-permute-start | bytes 1572872 | tf_op jit(solution)/shard_map/ppermute | solution.py:34
  20.7 4.7 %collective-permute-start.5 = (bf16[64,1024]{1,0:T(8,128)(2,1)S(1)}, bf16[64,1024]{1,0:T(8,128)(2,1)S(1)}, u32[]{:S(2)}, u32[]{:S(2)}) collective-permute-start(bf16[64,1024]{1,0:T(8,128)(2,1)S(1)} %get-tuple-element.129), channel_id=1, source_target_pairs={{0,8},{8,0},{1,9},{9,1},{2,10},{10,2},{3,11},{11,3},{32,40},{40,32... | collective-permute-start | bytes 393224 | tf_op jit(solution)/shard_map/ppermute | solution.py:34
  20.8 11.3 %collective-permute-start.6 = (bf16[64,1024]{1,0:T(8,128)(2,1)S(1)}, bf16[64,1024]{1,0:T(8,128)(2,1)S(1)}, u32[]{:S(2)}, u32[]{:S(2)}) collective-permute-start(bf16[64,1024]{1,0:T(8,128)(2,1)S(1)} %get-tuple-element.128), channel_id=1, source_target_pairs={{0,16},{8,24},{1,17},{9,25},{2,18},{10,26},{3,19},{11,27},{32,48},... | collective-permute-start | bytes 393224 | tf_op jit(solution)/shard_map/ppermute | solution.py:34
  20.9 16.1 %collective-permute-start.2 = (bf16[3,128,256]{2,1,0:T(8,128)(2,1)S(1)}, bf16[3,128,256]{2,1,0:T(8,128)(2,1)S(1)}, u32[]{:S(2)}, u32[]{:S(2)}) collective-permute-start(bf16[3,128,256]{2,1,0:T(8,128)(2,1)S(1)} %copy-done.25), channel_id=1, source_target_pairs={{0,32},{8,40},{1,33},{9,41},{2,34},{10,42},{3,35},{11,43},{32,64},... | collective-permute-start | bytes 589832 | tf_op jit(solution)/shard_map/ppermute | solution.py:34
  22.6 14.5 %collective-permute-start.3 = (bf16[3,128,256]{2,1,0:T(8,128)(2,1)S(1)}, bf16[3,128,256]{2,1,0:T(8,128)(2,1)S(1)}, u32[]{:S(2)}, u32[]{:S(2)}) collective-permute-start(bf16[3,128,256]{2,1,0:T(8,128)(2,1)S(1)} %copy-done.25), channel_id=1, source_target_pairs={{0,64},{8,72},{1,65},{9,73},{2,66},{10,74},{3,67},{11,75},{32,96},... | collective-permute-start | bytes 589832 | tf_op jit(solution)/shard_map/ppermute | solution.py:34
  25.5 11.6 %copy-start.39 = (bf16[64,1024]{1,0:T(8,128)(2,1)}, bf16[64,1024]{1,0:T(8,128)(2,1)S(1)}, u32[]{:S(2)}) copy-start(bf16[64,1024]{1,0:T(8,128)(2,1)S(1)} %collective-permute-done.5.refs_4_) | copy-start | bytes 393220
  25.5 11.6 %collective-permute-start.4 = (bf16[3,128,256]{2,1,0:T(8,128)(2,1)S(1)}, bf16[3,128,256]{2,1,0:T(8,128)(2,1)S(1)}, u32[]{:S(2)}, u32[]{:S(2)}) collective-permute-start(bf16[3,128,256]{2,1,0:T(8,128)(2,1)S(1)} %copy-done.25), channel_id=1, source_target_pairs={{0,96},{8,104},{1,97},{9,105},{2,98},{10,106},{3,99},{11,107},{32,... | collective-permute-start | bytes 589832 | tf_op jit(solution)/shard_map/ppermute | solution.py:34
  32.1 4.9 %collective-permute-start.7 = (bf16[64,1024]{1,0:T(8,128)(2,1)S(1)}, bf16[64,1024]{1,0:T(8,128)(2,1)S(1)}, u32[]{:S(2)}, u32[]{:S(2)}) collective-permute-start(bf16[64,1024]{1,0:T(8,128)(2,1)S(1)} %get-tuple-element.127), channel_id=1, source_target_pairs={{0,24},{8,16},{1,25},{9,17},{2,26},{10,18},{3,27},{11,19},{32,56},... | collective-permute-start | bytes 393224 | tf_op jit(solution)/shard_map/ppermute | solution.py:34
  40.6 85.2 %all-gather.11.cloned.1.call-start = ((), (), s32[]{:S(2)}) async-start(), calls=%async_computation.3 | async-start | bytes 5308416 | tf_op jit(solution)/shard_map/all_gather | solution.py:307
  41.9 7.5 %copy-start.26 = (bf16[4,3,128,256]{3,2,1,0:T(8,128)(2,1)}, bf16[4,3,128,256]{3,2,1,0:T(8,128)(2,1)S(1)}, u32[]{:S(2)}) copy-start(bf16[4,3,128,256]{3,2,1,0:T(8,128)(2,1)S(1)} %pad_maximum_fusion.2.refs_4_) | copy-start | bytes 2359300
  41.9 3.3 %collective-permute-start.8 = (bf16[4,3,128,256]{3,2,1,0:T(8,128)(2,1)S(1)}, bf16[4,3,128,256]{3,2,1,0:T(8,128)(2,1)S(1)}, u32[]{:S(2)}, u32[]{:S(2)}) collective-permute-start(bf16[4,3,128,256]{3,2,1,0:T(8,128)(2,1)S(1)} %pad_maximum_fusion.2.refs_4_), channel_id=1, source_target_pairs={{0,8},{8,0},{1,9},{9,1},{2,10},{10,2},{3,11},{11,3},{32,40},{40,32... | collective-permute-start | bytes 2359304 | tf_op jit(solution)/shard_map/ppermute | solution.py:34
  46.1 17.4 %collective-permute-start.9 = (bf16[9,128,256]{2,1,0:T(8,128)(2,1)}, bf16[9,128,256]{2,1,0:T(8,128)(2,1)S(1)}, u32[]{:S(2)}, u32[]{:S(2)}) collective-permute-start(bf16[9,128,256]{2,1,0:T(8,128)(2,1)} %shard_map.123), channel_id=1, source_target_pairs={{0,4},{8,12},{1,5},{9,13},{2,6},{10,14},{3,7},{11,15},{32,36},{40,... | collective-permute-start | bytes 1769480 | tf_op jit(solution)/shard_map/ppermute | solution.py:34
  64.3 96.9 %all-gather.13.cloned.1.call-start = ((), (), s32[]{:S(2)}) async-start(), calls=%async_computation.4 | async-start | bytes 2621440 | tf_op jit(solution)/shard_map/all_gather | solution.py:320
  65.2 21.7 %copy-start.19 = (bf16[16,64,256]{2,1,0:T(8,128)(2,1)S(1)}, bf16[16,64,256]{2,1,0:T(8,128)(2,1)}, u32[]{:S(2)}) copy-start(bf16[16,64,256]{2,1,0:T(8,128)(2,1)} %get-tuple-element.60.refs_2_.refs_3_) | copy-start | bytes 1572868
  65.2 13.7 %collective-permute-start.12 = (bf16[16,64,256]{2,1,0:T(8,128)(2,1)}, bf16[16,64,256]{2,1,0:T(8,128)(2,1)S(1)}, u32[]{:S(2)}, u32[]{:S(2)}) collective-permute-start(bf16[16,64,256]{2,1,0:T(8,128)(2,1)} %shard_map.125), channel_id=1, source_target_pairs={{0,16},{8,24},{1,17},{9,25},{2,18},{10,26},{3,19},{11,27},{32,48},... | collective-permute-start | bytes 1572872 | tf_op jit(solution)/shard_map/ppermute | solution.py:34
  66.4 14.6 %collective-permute-start.13 = (bf16[16,64,256]{2,1,0:T(8,128)(2,1)}, bf16[16,64,256]{2,1,0:T(8,128)(2,1)S(1)}, u32[]{:S(2)}, u32[]{:S(2)}) collective-permute-start(bf16[16,64,256]{2,1,0:T(8,128)(2,1)} %shard_map.125), channel_id=1, source_target_pairs={{0,20},{8,28},{1,21},{9,29},{2,22},{10,30},{3,23},{11,31},{32,52},... | collective-permute-start | bytes 1572872 | tf_op jit(solution)/shard_map/ppermute | solution.py:34
  69.0 16.9 %collective-permute-start.10 = (bf16[1024,256]{1,0:T(8,128)(2,1)}, bf16[1024,256]{1,0:T(8,128)(2,1)S(1)}, u32[]{:S(2)}, u32[]{:S(2)}) collective-permute-start(bf16[1024,256]{1,0:T(8,128)(2,1)} %get-tuple-element.68), channel_id=1, source_target_pairs={{0,1},{8,9},{1,2},{9,10},{2,3},{10,11},{3,0},{11,8},{32,33},{40,41... | collective-permute-start | bytes 1572872 | tf_op jit(solution)/shard_map/ppermute | solution.py:34
  71.0 15.0 %collective-permute-start.11 = (bf16[1024,256]{1,0:T(8,128)(2,1)}, bf16[1024,256]{1,0:T(8,128)(2,1)S(1)}, u32[]{:S(2)}, u32[]{:S(2)}) collective-permute-start(bf16[1024,256]{1,0:T(8,128)(2,1)} %get-tuple-element.69), channel_id=1, source_target_pairs={{0,3},{8,11},{1,0},{9,8},{2,1},{10,9},{3,2},{11,10},{32,35},{40,43... | collective-permute-start | bytes 1572872 | tf_op jit(solution)/shard_map/ppermute | solution.py:34
  90.0 18.1 %collective-permute-start.15 = (bf16[4,16,64,256]{3,2,1,0:T(8,128)(2,1)}, bf16[4,16,64,256]{3,2,1,0:T(8,128)(2,1)}, u32[]{:S(2)}, u32[]{:S(2)}) collective-permute-start(bf16[4,16,64,256]{3,2,1,0:T(8,128)(2,1)} %pad_maximum_fusion), channel_id=1, source_target_pairs={{0,8},{8,0},{1,9},{9,1},{2,10},{10,2},{3,11},{11,3},{32,40},{40,32... | collective-permute-start | bytes 6291464 | tf_op jit(solution)/shard_map/ppermute | solution.py:34
  91.9 16.2 %collective-permute-start.14 = (bf16[1024,256]{1,0:T(8,128)(2,1)}, bf16[1024,256]{1,0:T(8,128)(2,1)}, u32[]{:S(2)}, u32[]{:S(2)}) collective-permute-start(bf16[1024,256]{1,0:T(8,128)(2,1)} %get-tuple-element.73), channel_id=1, source_target_pairs={{0,2},{8,10},{1,3},{9,11},{2,0},{10,8},{3,1},{11,9},{32,34},{40,42... | collective-permute-start | bytes 1572872 | tf_op jit(solution)/shard_map/ppermute | solution.py:34
  94.7 13.4 %copy-start.5 = (bf16[1024,256]{1,0:T(8,128)(2,1)S(1)}, bf16[1024,256]{1,0:T(8,128)(2,1)}, u32[]{:S(2)}) copy-start(bf16[1024,256]{1,0:T(8,128)(2,1)} %get-tuple-element.71.refs_1_) | copy-start | bytes 1572868
  94.7 13.4 %copy-start.8 = (f32[1024,256]{1,0:T(8,128)S(1)}, f32[1024,256]{1,0:T(8,128)}, u32[]{:S(2)}) copy-start(f32[1024,256]{1,0:T(8,128)} %get-tuple-element.64.refs_1_) | copy-start | bytes 3145732
  94.7 13.4 %copy-start.17 = (bf16[1024,256]{1,0:T(8,128)(2,1)S(1)}, bf16[1024,256]{1,0:T(8,128)(2,1)}, u32[]{:S(2)}) copy-start(bf16[1024,256]{1,0:T(8,128)(2,1)} %get-tuple-element.72) | copy-start | bytes 1572868
  96.8 4.3 %collective-permute-start.16 = (bf16[64,1024]{1,0:T(8,128)(2,1)}, bf16[64,1024]{1,0:T(8,128)(2,1)S(1)}, u32[]{:S(2)}, u32[]{:S(2)}) collective-permute-start(bf16[64,1024]{1,0:T(8,128)(2,1)} %get-tuple-element.125), channel_id=1, source_target_pairs={{0,8},{8,0},{1,9},{9,1},{2,10},{10,2},{3,11},{11,3},{32,40},{40,32... | collective-permute-start | bytes 393224 | tf_op jit(solution)/shard_map/ppermute | solution.py:34
  97.0 6.5 %collective-permute-start.17 = (bf16[64,1024]{1,0:T(8,128)(2,1)}, bf16[64,1024]{1,0:T(8,128)(2,1)S(1)}, u32[]{:S(2)}, u32[]{:S(2)}) collective-permute-start(bf16[64,1024]{1,0:T(8,128)(2,1)} %get-tuple-element.124), channel_id=1, source_target_pairs={{0,16},{8,24},{1,17},{9,25},{2,18},{10,26},{3,19},{11,27},{32,48},... | collective-permute-start | bytes 393224 | tf_op jit(solution)/shard_map/ppermute | solution.py:34
  97.8 7.2 %collective-permute-start.18 = (bf16[64,1024]{1,0:T(8,128)(2,1)}, bf16[64,1024]{1,0:T(8,128)(2,1)S(1)}, u32[]{:S(2)}, u32[]{:S(2)}) collective-permute-start(bf16[64,1024]{1,0:T(8,128)(2,1)} %get-tuple-element.123), channel_id=1, source_target_pairs={{0,24},{8,16},{1,25},{9,17},{2,26},{10,18},{3,27},{11,19},{32,56},... | collective-permute-start | bytes 393224 | tf_op jit(solution)/shard_map/ppermute | solution.py:34
  109.9 15.1 %collective-permute-start.19 = (bf16[8,8,16,256]{3,2,1,0:T(8,128)(2,1)S(1)}, bf16[8,8,16,256]{3,2,1,0:T(8,128)(2,1)S(1)}, u32[]{:S(2)}, u32[]{:S(2)}) collective-permute-start(bf16[8,8,16,256]{3,2,1,0:T(8,128)(2,1)S(1)} %bitcast.110), channel_id=1, source_target_pairs={{0,4},{8,12},{1,5},{9,13},{2,6},{10,14},{3,7},{11,15},{32,36},{40,... | collective-permute-start | bytes 1572872 | tf_op jit(solution)/shard_map/ppermute | solution.py:34
  113.0 78.1 %reduce-scatter.2.cloned.1.call-start = ((), (), s32[]{:S(2)}) async-start(), calls=%async_computation.1 | async-start | bytes 983040 | tf_op jit(solution)/shard_map/reduce_scatter | solution.py:329
  134.9 19.9 %collective-permute-start.20 = (bf16[1024,256]{1,0:T(8,128)(2,1)}, bf16[1024,256]{1,0:T(8,128)(2,1)S(1)}, u32[]{:S(2)}, u32[]{:S(2)}) collective-permute-start(bf16[1024,256]{1,0:T(8,128)(2,1)} %get-tuple-element.83.refs_1_), channel_id=1, source_target_pairs={{0,1},{8,9},{1,2},{9,10},{2,3},{10,11},{3,0},{11,8},{32,33},{40,41... | collective-permute-start | bytes 1572872 | tf_op jit(solution)/shard_map/ppermute | solution.py:34
  135.1 19.8 %collective-permute-start.22 = (bf16[8,8,16,256]{3,2,1,0:T(8,128)(2,1)}, bf16[8,8,16,256]{3,2,1,0:T(8,128)(2,1)S(1)}, u32[]{:S(2)}, u32[]{:S(2)}) collective-permute-start(bf16[8,8,16,256]{3,2,1,0:T(8,128)(2,1)} %shard_map.132.refs_6_), channel_id=1, source_target_pairs={{0,16},{8,24},{1,17},{9,25},{2,18},{10,26},{3,19},{11,27},{32,48},... | collective-permute-start | bytes 1572872 | tf_op jit(solution)/shard_map/ppermute | solution.py:34
  135.9 18.9 %collective-permute-start.23 = (bf16[8,8,16,256]{3,2,1,0:T(8,128)(2,1)}, bf16[8,8,16,256]{3,2,1,0:T(8,128)(2,1)}, u32[]{:S(2)}, u32[]{:S(2)}) collective-permute-start(bf16[8,8,16,256]{3,2,1,0:T(8,128)(2,1)} %shard_map.132.refs_6_), channel_id=1, source_target_pairs={{0,20},{8,28},{1,21},{9,29},{2,22},{10,30},{3,23},{11,31},{32,52},... | collective-permute-start | bytes 1572872 | tf_op jit(solution)/shard_map/ppermute | solution.py:34
  137.1 17.7 %collective-permute-start.21 = (bf16[1024,256]{1,0:T(8,128)(2,1)}, bf16[1024,256]{1,0:T(8,128)(2,1)S(1)}, u32[]{:S(2)}, u32[]{:S(2)}) collective-permute-start(bf16[1024,256]{1,0:T(8,128)(2,1)} %get-tuple-element.85), channel_id=1, source_target_pairs={{0,3},{8,11},{1,0},{9,8},{2,1},{10,9},{3,2},{11,10},{32,35},{40,43... | collective-permute-start | bytes 1572872 | tf_op jit(solution)/shard_map/ppermute | solution.py:34
  159.0 4.5 %collective-permute-start.25 = (bf16[4,8,8,16,256]{4,3,2,1,0:T(8,128)(2,1)}, bf16[4,8,8,16,256]{4,3,2,1,0:T(8,128)(2,1)}, u32[]{:S(2)}, u32[]{:S(2)}) collective-permute-start(bf16[4,8,8,16,256]{4,3,2,1,0:T(8,128)(2,1)} %pad_maximum_fusion.1), channel_id=1, source_target_pairs={{0,8},{8,0},{1,9},{9,1},{2,10},{10,2},{3,11},{11,3},{32,40},{40,32... | collective-permute-start | bytes 6291464 | tf_op jit(solution)/shard_map/ppermute | solution.py:34
  159.6 21.5 %collective-permute-start.24 = (bf16[1024,256]{1,0:T(8,128)(2,1)S(1)}, bf16[1024,256]{1,0:T(8,128)(2,1)S(1)}, u32[]{:S(2)}, u32[]{:S(2)}) collective-permute-start(bf16[1024,256]{1,0:T(8,128)(2,1)S(1)} %copy-done.31), channel_id=1, source_target_pairs={{0,2},{8,10},{1,3},{9,11},{2,0},{10,8},{3,1},{11,9},{32,34},{40,42... | collective-permute-start | bytes 1572872 | tf_op jit(solution)/shard_map/ppermute | solution.py:34
  185.5 33.5 %collective-permute-start.26 = (bf16[9,64,512]{2,1,0:T(8,128)(2,1)}, bf16[9,64,512]{2,1,0:T(8,128)(2,1)S(1)}, u32[]{:S(2)}, u32[]{:S(2)}) collective-permute-start(bf16[9,64,512]{2,1,0:T(8,128)(2,1)} %get-tuple-element.101), channel_id=1, source_target_pairs={{0,32},{8,40},{1,33},{9,41},{2,34},{10,42},{3,35},{11,43},{32,64},... | collective-permute-start | bytes 1769480 | tf_op jit(solution)/shard_map/ppermute | solution.py:34
  187.0 33.2 %collective-permute-start.27 = (bf16[9,64,512]{2,1,0:T(8,128)(2,1)}, bf16[9,64,512]{2,1,0:T(8,128)(2,1)}, u32[]{:S(2)}, u32[]{:S(2)}) collective-permute-start(bf16[9,64,512]{2,1,0:T(8,128)(2,1)} %get-tuple-element.102), channel_id=1, source_target_pairs={{0,64},{8,72},{1,65},{9,73},{2,66},{10,74},{3,67},{11,75},{32,96},... | collective-permute-start | bytes 1769480 | tf_op jit(solution)/shard_map/ppermute | solution.py:34
  189.7 30.5 %collective-permute-start.28 = (bf16[9,64,512]{2,1,0:T(8,128)(2,1)}, bf16[9,64,512]{2,1,0:T(8,128)(2,1)}, u32[]{:S(2)}, u32[]{:S(2)}) collective-permute-start(bf16[9,64,512]{2,1,0:T(8,128)(2,1)} %get-tuple-element.103), channel_id=1, source_target_pairs={{0,96},{8,104},{1,97},{9,105},{2,98},{10,106},{3,99},{11,107},{32,... | collective-permute-start | bytes 1769480 | tf_op jit(solution)/shard_map/ppermute | solution.py:34
  192.9 26.1 %collective-permute-start.29 = (bf16[3,64,256]{2,1,0:T(8,128)(2,1)}, bf16[3,64,256]{2,1,0:T(8,128)(2,1)S(1)}, u32[]{:S(2)}, u32[]{:S(2)}) collective-permute-start(bf16[3,64,256]{2,1,0:T(8,128)(2,1)} %get-tuple-element.105), channel_id=1, source_target_pairs={{0,0},{8,4},{1,1},{9,5},{2,2},{10,6},{3,3},{11,7},{32,32},{40,36},... | collective-permute-start | bytes 294920 | tf_op jit(solution)/shard_map/ppermute | solution.py:34
  195.1 23.9 %collective-permute-start.30 = (bf16[3,64,256]{2,1,0:T(8,128)(2,1)}, bf16[3,64,256]{2,1,0:T(8,128)(2,1)S(1)}, u32[]{:S(2)}, u32[]{:S(2)}) collective-permute-start(bf16[3,64,256]{2,1,0:T(8,128)(2,1)} %get-tuple-element.106), channel_id=1, source_target_pairs={{0,4},{8,0},{1,5},{9,1},{2,6},{10,2},{3,7},{11,3},{32,36},{40,32},... | collective-permute-start | bytes 294920 | tf_op jit(solution)/shard_map/ppermute | solution.py:34
  197.2 23.0 %copy-start.2 = (bf16[9,64,512]{2,1,0:T(8,128)(2,1)S(1)}, bf16[9,64,512]{2,1,0:T(8,128)(2,1)}, u32[]{:S(2)}) copy-start(bf16[9,64,512]{2,1,0:T(8,128)(2,1)} %get-tuple-element.100.refs_1_) | copy-start | bytes 1769476
  220.2 8.0 %copy-start.47 = (f32[16,2,256]{2,1,0:T(2,128)S(1)}, f32[16,2,256]{2,1,0:T(2,128)}, u32[]{:S(2)}) copy-start(f32[16,2,256]{2,1,0:T(2,128)} %get-tuple-element.114) | copy-start | bytes 98308
  220.2 8.0 %copy-start.44 = (bf16[3,64,256]{2,1,0:T(8,128)(2,1)S(1)}, bf16[3,64,256]{2,1,0:T(8,128)(2,1)}, u32[]{:S(2)}) copy-start(bf16[3,64,256]{2,1,0:T(8,128)(2,1)} %get-tuple-element.112) | copy-start | bytes 294916
  220.3 8.0 %copy-start.46 = (bf16[3,64,256]{2,1,0:T(8,128)(2,1)S(1)}, bf16[3,64,256]{2,1,0:T(8,128)(2,1)}, u32[]{:S(2)}) copy-start(bf16[3,64,256]{2,1,0:T(8,128)(2,1)} %get-tuple-element.113) | copy-start | bytes 294916
  222.9 20.1 %collective-permute-start.31 = (bf16[9,64,256]{2,1,0:T(8,128)(2,1)}, bf16[9,64,256]{2,1,0:T(8,128)(2,1)S(1)}, u32[]{:S(2)}, u32[]{:S(2)}) collective-permute-start(bf16[9,64,256]{2,1,0:T(8,128)(2,1)} %get-tuple-element.110), channel_id=1, source_target_pairs={{0,0},{8,4},{1,1},{9,5},{2,2},{10,6},{3,3},{11,7},{32,32},{40,36},... | collective-permute-start | bytes 884744 | tf_op jit(solution)/shard_map/ppermute | solution.py:34
  226.3 17.8 %collective-permute-start.32 = (bf16[9,64,256]{2,1,0:T(8,128)(2,1)}, bf16[9,64,256]{2,1,0:T(8,128)(2,1)S(1)}, u32[]{:S(2)}, u32[]{:S(2)}) collective-permute-start(bf16[9,64,256]{2,1,0:T(8,128)(2,1)} %get-tuple-element.111), channel_id=1, source_target_pairs={{0,4},{8,0},{1,5},{9,1},{2,6},{10,2},{3,7},{11,3},{32,36},{40,32},... | collective-permute-start | bytes 884744 | tf_op jit(solution)/shard_map/ppermute | solution.py:34
  (40 other events, 108.4 us)
Sparse Core Ops, SparseCore 0:
  40.7 35.4 all-gather.8
  77.9 33.2 all-gather.10
  113.2 36.1 all-gather.12
  159.7 22.2 reduce-scatter.1

commit v4 on v3

--- a/solution.py
+++ b/solution.py
@@ -93,9 +93,14 @@
 def fill(padded, mine, other, spatial):
     if spatial:
         inner = (pl.ds(1, HT), pl.ds(1, WD), slice(None))
+        for edge in (0, HT + 1):
+            padded[edge] = jnp.zeros((WD + 2, FR, 2 * CH), BF)
+        for edge in (0, WD + 1):
+            padded[pl.ds(1, HT), pl.ds(edge, 1)] = jnp.zeros((HT, 1, FR, 2 * CH), BF)
     else:
         inner = (pl.ds(1, FR), slice(None))
-    padded[...] = jnp.zeros(padded.shape, BF)
+        for edge in (0, FR + 1):
+            padded[edge] = jnp.zeros((HT * WD, 2 * CH), BF)
     padded[inner + (pl.ds(0, CH),)] = mine
     padded[inner + (pl.ds(CH, CH),)] = other
 
@@ -164,17 +169,19 @@
     )(index, mine, other, w_mine, w_near, w_far, *waits)
 
 
-def wgrad_body(first, spatial, lefts, index, *refs):
-    left, (mine, other, pair, both, swapped) = refs[:lefts], refs[lefts : lefts + 5]
+def wgrad_body(first, spatial, lefts, fields, index, *refs):
+    left, (mine, other, pair, both, *swapped) = refs[:lefts], refs[lefts : lefts + fields]
+    if len(swapped) == 1:
+        swapped = [swapped[0].at[i] for i in range(4)]
     outs, padded = refs[-5:-1] if spatial else refs[-2:-1], refs[-1]
     step = pl.program_id(0)
 
     @pl.when(step == 0)
     def _():
         fill(padded.at[0], mine[...], other[...], spatial)
-        fill(padded.at[1], swapped[0], swapped[1], spatial)
+        fill(padded.at[1], swapped[0][...], swapped[1][...], spatial)
         fill(padded.at[2], pair[...], both[...], spatial)
-        fill(padded.at[3], swapped[2], swapped[3], spatial)
+        fill(padded.at[3], swapped[2][...], swapped[3][...], spatial)
 
     right = padded[(slice(None),) + tap_rows(spatial, step + first)]
     blocks = jnp.concatenate([ref[...].reshape(-1, 4 * ROWS) for ref in left], axis=0)
@@ -200,7 +207,7 @@
         out_specs = pl.BlockSpec((4, 1, SUB, 2 * CH), lambda i, ix: (0, i, 0, 0))
         out_shape = jax.ShapeDtypeStruct((4, taps, SUB, 2 * CH), BF)
     return pl.pallas_call(
-        lambda *refs: wgrad_body(first, spatial, len(left), *refs),
+        lambda *refs: wgrad_body(first, spatial, len(left), len(fields), *refs),
         grid_spec=pltpu.PrefetchScalarGridSpec(
             num_scalar_prefetch=1,
             grid=(taps,),
@@ -311,11 +318,11 @@
     cot_pair, cot_both = send(cot_late, to_pair), send(cot_late, to_both)
     up, down, far, cot_pair, cot_both = together(up, down, far, cot_pair, cot_both)
 
-    far = send(far, to_z(2))
+    own, parts = exchange(after(hidden.T.reshape(4, SUB, ROWS), up))
     cot_near = (cot, cot_other, cot_pair, cot_both)
     cot_swapped = send(jnp.stack(cot_near), to_core)
-    own, parts = exchange(after(hidden.T.reshape(4, SUB, ROWS), up))
-    far, cot_swapped, *parts = together(far, cot_swapped, *parts)
+    far = send(far, to_z(2))
+    cot_swapped, *parts, far = together(cot_swapped, *parts, far)
     hidden_part = jnp.concatenate([own, *parts], axis=1)
     hidden_left = (lax.all_gather(hidden_part, "mp", axis=0, axis_index_groups=z_groups),)
     saved_grad = total_of(mine, (up, far, down)).astype(BF)
@@ -339,8 +346,8 @@
     up, down, far, sg_pair, sg_both = together(up, down, far, sg_pair, sg_both)
 
     sg_near = (saved_grad, sg_other, sg_pair, sg_both)
-    sg_fields = sg_near + (send(jnp.stack(sg_near), to_core),)
     far = send(far, to_z(2))
+    sg_fields = sg_near + tuple(send(value, to_core) for value in sg_near)
     parts = wgrad(True, 0, 9, (slots - y) % 4, hidden_left, sg_fields)
     far, *parts = together(far, *parts)
     hidden_grad = total_of(mine, (up, far, down))
@@ -367,16 +374,15 @@
         return jnp.concatenate([low, high], axis=1).astype(F32)
 
     sums = lax.all_gather(jnp.stack([gain_sum, bias_sum]), "dp", axis=0)
-    temporal_owned = to_owners(after(temporal_total, parts[0]))
     others = [send(parts[k], to_y(k)) for k in (1, 2, 3)]
-    *others, sums, tk_first, tk_second = together(*others, sums, *temporal_owned)
+    *others, sums = together(*others, sums)
     total = parts[0].astype(F32)
     for other in others:
         total = total + other.astype(F32)
-    first, second = to_owners(total)
+    temporal_total = after(temporal_total, parts[0])
+    grads = owned(*to_owners(jnp.concatenate([total.astype(BF), temporal_total])))
+    spatial_grad, temporal_grad = grads[:9].reshape(3, 3, CH // 2, CH), grads[9:]
     sums = jnp.sum(sums, axis=0)
-    temporal_grad = owned(tk_first, tk_second)
-    spatial_grad = owned(first, second).reshape(3, 3, CH // 2, CH)
     return (input_grad, spatial_grad, temporal_grad, sums[0], sums[1])
 
 

time: 253 us -> 245 us (0.968)
  other arithmetic: 23.5 us -> 19 us
    another operation x1 -> x0, other arithmetic: 3.06 us -> none  [local(): sg_fields = sg_near + (send(jnp.stack(sg_near), to_core),)]
    ppermute x33 -> x34, starting transfers between devices: 47.8 us -> 45.2 us  [send(): return lax.ppermute(value, ('dp', 'mp'), pairs)]
    ppermute x33 -> x34, waiting for transfers between devices: 67.2 us -> 67.9 us  [send(): return lax.ppermute(value, ('dp', 'mp'), pairs)]
    unnamed x105 -> x101, local copies, waits for them, and re-layouts: 12 us -> 11.9 us
  transfers between devices with their start and end apart: 37 -> 38, of which waited for: 16 -> 16; matrix products, arithmetic and copies ran while one was open for 13% -> 12% of each run, Pallas kernels for 21% -> 22%
where the time goes in v4:
time: 245 us
  waiting for transfers between devices  68 us (28%)
  Pallas kernels  52.6 us (21%)
  starting transfers between devices  45.6 us (19%)
  local copies, waits for them, and re-layouts  26.7 us (11%)
  other arithmetic  19 us (8%)
  blocking collectives  18.4 us (8%)
  between operations  14.3 us (6%)
    ppermute x34, waiting for transfers between devices, send(): return lax.ppermute(value, ('dp', 'mp'), pairs)  67.9 us
    ppermute x34, starting transfers between devices, send(): return lax.ppermute(value, ('dp', 'mp'), pairs)  45.2 us
    pallas_call x3, Pallas kernels, dgrad(): pl.pallas_call(lambda *refs: dgrad_body(spatial, blocks, *refs), grid_spe...  26.7 us
    pallas_call x2, Pallas kernels, wgrad(): pl.pallas_call(lambda *refs: wgrad_body(first, spatial, len(left), len(fi...  25.9 us
    all_gather x1, blocking collectives, local(): sums = lax.all_gather(jnp.stack([gain_sum, bias_sum]), 'dp', axis=0)  18.4 us
    unnamed x101, local copies, waits for them, and re-layouts  11.9 us
  transfers between devices with their start and end apart: 38, of which 16 were waited for; matrix products, arithmetic and copies ran while one was open for 12% of the time, Pallas kernels for 22%

profile of v4, /device:TPU:6, one launch (start us, length us, event | category | flops | bytes accessed | tf_op | source)
XLA Modules:
  0.0 244.6 jit_solution(11408957701487780127)
XLA Ops:
  8.3 1.5 collective-permute-start
  9.8 1.9 copy.82.refs_0_
  11.6 4.9 %collective-permute-done.refs_1_ = bf16[3,128,256]{2,1,0:T(8,128)(2,1)S(1)} collective-permute-done((bf16[3,128,256]{2,1,0:T(8,128)(2,1)S(1)}, bf16[3,128,256]{2,1,0:T(8,128)(2,1)S(1)}, u32[]{:S(2)}, u32[]{:S(2)}) %collective-permute-start) | collective-permute-done | bytes 196640 | tf_op jit(solution)/shard_map/ppermute | solution.py:34
  17.2 1.4 collective-permute-start.1
  20.9 1.6 collective-permute-start.2
  22.6 2.9 %collective-permute-start.3 = (bf16[3,128,256]{2,1,0:T(8,128)(2,1)S(1)}, bf16[3,128,256]{2,1,0:T(8,128)(2,1)S(1)}, u32[]{:S(2)}, u32[]{:S(2)}) collective-permute-start(bf16[3,128,256]{2,1,0:T(8,128)(2,1)S(1)} %copy-done.22), channel_id=1, source_target_pairs={{0,64},{8,72},{1,65},{9,73},{2,66},{10,74},{3,67},{11,75},{32,96},... | collective-permute-start | bytes 589832 | tf_op jit(solution)/shard_map/ppermute | solution.py:34
  25.5 1.3 collective-permute-start.4
  26.8 5.3 %collective-permute-done.6.refs_5_ = bf16[64,1024]{1,0:T(8,128)(2,1)S(1)} collective-permute-done((bf16[64,1024]{1,0:T(8,128)(2,1)S(1)}, bf16[64,1024]{1,0:T(8,128)(2,1)S(1)}, u32[]{:S(2)}, u32[]{:S(2)}) %collective-permute-start.6) | collective-permute-done | bytes 131104 | tf_op jit(solution)/shard_map/ppermute | solution.py:34
  32.1 4.9 %collective-permute-done.7.refs_6_ = bf16[64,1024]{1,0:T(8,128)(2,1)S(1)} collective-permute-done((bf16[64,1024]{1,0:T(8,128)(2,1)S(1)}, bf16[64,1024]{1,0:T(8,128)(2,1)S(1)}, u32[]{:S(2)}, u32[]{:S(2)}) %collective-permute-start.7) | collective-permute-done | bytes 131104 | tf_op jit(solution)/shard_map/ppermute | solution.py:34
  38.7 1.9 pad_maximum_fusion.2
  40.6 1.2 pad_maximum_fusion.1.refs_4_
  43.2 1.9 constant_dynamic-slice_fusion.1.refs_0_
  46.0 3.3 %collective-permute-start.9 = (bf16[9,128,256]{2,1,0:T(8,128)(2,1)}, bf16[9,128,256]{2,1,0:T(8,128)(2,1)S(1)}, u32[]{:S(2)}, u32[]{:S(2)}) collective-permute-start(bf16[9,128,256]{2,1,0:T(8,128)(2,1)} %shard_map.123), channel_id=1, source_target_pairs={{0,4},{8,12},{1,5},{9,13},{2,6},{10,14},{3,7},{11,15},{32,36},{40,... | collective-permute-start | bytes 1769480 | tf_op jit(solution)/shard_map/ppermute | solution.py:34
  49.4 8.3 %shard_map.122 = (bf16[1024,256]{1,0:T(8,128)(2,1)}, bf16[1024,256]{1,0:T(8,128)(2,1)}, bf16[1024,256]{1,0:T(8,128)(2,1)}, f32[1024,256]{1,0:T(8,128)}) custom-call(s32[13]{0:T(128)} %stack.118.refs_0_, bf16[16,64,256]{2,1,0:T(8,128)(2,1)} %bitcast.98, bf16[16,64,256]{2,1,0:T(8,128)(2,1)} %get-tuple-element.56.refs_2_.refs_3_, ...), custom_call_target="tpu_custom_call" | custom-call | flops 8049999872 | tf_op jit(solution)/shard_map/pallas_call | solution.py:150
  57.7 5.8 %collective-permute-done.9.refs_0_ = bf16[9,128,256]{2,1,0:T(8,128)(2,1)S(1)} collective-permute-done((bf16[9,128,256]{2,1,0:T(8,128)(2,1)}, bf16[9,128,256]{2,1,0:T(8,128)(2,1)S(1)}, u32[]{:S(2)}, u32[]{:S(2)}) %collective-permute-start.9) | collective-permute-done | bytes 589856 | tf_op jit(solution)/shard_map/ppermute | solution.py:34
  66.3 2.6 %collective-permute-start.13 = (bf16[16,64,256]{2,1,0:T(8,128)(2,1)}, bf16[16,64,256]{2,1,0:T(8,128)(2,1)S(1)}, u32[]{:S(2)}, u32[]{:S(2)}) collective-permute-start(bf16[16,64,256]{2,1,0:T(8,128)(2,1)} %shard_map.125), channel_id=1, source_target_pairs={{0,20},{8,28},{1,21},{9,29},{2,22},{10,30},{3,23},{11,31},{32,52},... | collective-permute-start | bytes 1572872 | tf_op jit(solution)/shard_map/ppermute | solution.py:34
  69.0 1.9 collective-permute-start.10
  70.9 2.1 collective-permute-start.11
  73.0 5.8 %collective-permute-done.12.refs_3_ = bf16[16,64,256]{2,1,0:T(8,128)(2,1)S(1)} collective-permute-done((bf16[16,64,256]{2,1,0:T(8,128)(2,1)}, bf16[16,64,256]{2,1,0:T(8,128)(2,1)S(1)}, u32[]{:S(2)}, u32[]{:S(2)}) %collective-permute-start.12) | collective-permute-done | bytes 524320 | tf_op jit(solution)/shard_map/ppermute | solution.py:34
  78.9 2.1 collective-permute-done.13.refs_4_
  81.0 4.9 %collective-permute-done.10.refs_0_ = bf16[1024,256]{1,0:T(8,128)(2,1)S(1)} collective-permute-done((bf16[1024,256]{1,0:T(8,128)(2,1)}, bf16[1024,256]{1,0:T(8,128)(2,1)S(1)}, u32[]{:S(2)}, u32[]{:S(2)}) %collective-permute-start.10) | collective-permute-done | bytes 524320 | tf_op jit(solution)/shard_map/ppermute | solution.py:34
  86.9 3.1 %pad_maximum_fusion = bf16[4,16,64,256]{3,2,1,0:T(8,128)(2,1)} fusion(bf16[1,16,64,256]{3,2,1,0:T(8,128)(2,1)} %bitcast.116, bf16[1,16,64,256]{3,2,1,0:T(8,128)(2,1)} %bitcast.115, bf16[1,16,64,256]{3,2,1,0:T(8,128)(2,1)S(1)} %bitcast.114, bf16[1,16,64,256]{3,2,1,0:T(8,128)(2,1)S(1)} %bitcast.101), kind=kLoop, calls=%fused_computation | loop fusion | flops 3145728 | bytes 4194304 | tf_op jit(solution)/shard_map/stack | solution.py:323
  91.7 1.6 collective-permute-start.18
  94.7 2.0 dynamic-slice_bitcast_fusion
  101.1 2.4 collective-permute-done.16.refs_2_
  103.5 1.6 collective-permute-done.17.refs_3_
  105.1 2.9 %collective-permute-done.18.refs_4_ = bf16[1024,256]{1,0:T(8,128)(2,1)} collective-permute-done((bf16[1024,256]{1,0:T(8,128)(2,1)}, bf16[1024,256]{1,0:T(8,128)(2,1)}, u32[]{:S(2)}, u32[]{:S(2)}) %collective-permute-start.18) | collective-permute-done | bytes 524320 | tf_op jit(solution)/shard_map/ppermute | solution.py:34
  108.1 1.3 add_convert_fusion.1
  109.7 1.5 collective-permute-start.19
  113.2 8.4 %shard_map.129.refs_1_ = bf16[4,3,64,512]{3,2,1,0:T(8,128)(2,1)} custom-call(s32[4]{0:T(128)} %fusion.5.refs_0_, bf16[4,64,4096]{2,1,0:T(8,128)(2,1)} %bitcast.135, bf16[16,64,256]{2,1,0:T(8,128)(2,1)} %bitcast.99, bf16[16,64,256]{2,1,0:T(8,128)(2,1)} %get-tuple-element.56.refs_2_.refs_3_, bf16[16,64,256]{2,1,0:T(8,128)(2,1)} %get-tuple-element.69.refs_4_, ...), custom_call_target="tpu_custom_call" | custom-call | flops 9717499904 | tf_op jit(solution)/shard_map/pallas_call | solution.py:209
  121.7 3.2 %collective-permute-done.19.refs_0_ = bf16[8,8,16,256]{3,2,1,0:T(8,128)(2,1)S(1)} collective-permute-done((bf16[8,8,16,256]{3,2,1,0:T(8,128)(2,1)S(1)}, bf16[8,8,16,256]{3,2,1,0:T(8,128)(2,1)S(1)}, u32[]{:S(2)}, u32[]{:S(2)}) %collective-permute-start.19) | collective-permute-done | bytes 524320 | tf_op jit(solution)/shard_map/ppermute | solution.py:34
  125.7 9.1 %shard_map.131 = (bf16[1024,256]{1,0:T(8,128)(2,1)}, bf16[1024,256]{1,0:T(8,128)(2,1)}) custom-call(s32[7]{0:T(128)} %stack.132.refs_0_, bf16[8,8,16,256]{3,2,1,0:T(8,128)(2,1)} %bitcast.110, bf16[8,8,16,256]{3,2,1,0:T(8,128)(2,1)} %get-tuple-element.77.refs_2_.refs_3_, bf16[9,2048,256]{2,1,0:T(8,128)(2,1)} %bitcast.125, bf16[8,9,128,256]{3,2,1,0:T(8,128)(2,1)} %bitcast.131, ...), custom_call_target="tpu_custom_call" | custom-call | flops 9660000256 | tf_op jit(solution)/shard_map/pallas_call | solution.py:150
  137.1 2.9 %collective-permute-start.21 = (bf16[1024,256]{1,0:T(8,128)(2,1)}, bf16[1024,256]{1,0:T(8,128)(2,1)S(1)}, u32[]{:S(2)}, u32[]{:S(2)}) collective-permute-start(bf16[1024,256]{1,0:T(8,128)(2,1)} %get-tuple-element.81), channel_id=1, source_target_pairs={{0,3},{8,11},{1,0},{9,8},{2,1},{10,9},{3,2},{11,10},{32,35},{40,43... | collective-permute-start | bytes 1572872 | tf_op jit(solution)/shard_map/ppermute | solution.py:34
  140.0 9.3 %shard_map.133 = (bf16[1024,256]{1,0:T(8,128)(2,1)}, f32[1024,256]{1,0:T(8,128)}) custom-call(s32[7]{0:T(128)} %stack.110.refs_0_, bf16[8,8,16,256]{3,2,1,0:T(8,128)(2,1)} %bitcast.111, bf16[8,8,16,256]{3,2,1,0:T(8,128)(2,1)} %get-tuple-element.77.refs_2_.refs_3_, bf16[9,2048,256]{2,1,0:T(8,128)(2,1)} %bitcast.126, bf16[8,9,128,256]{3,2,1,0:T(8,128)(2,1)} %bitcast.133, ...), custom_call_target="tpu_custom_call" | custom-call | flops 9660000256 | tf_op jit(solution)/shard_map/pallas_call | solution.py:150
  149.4 5.3 %collective-permute-done.20.refs_0_ = bf16[1024,256]{1,0:T(8,128)(2,1)S(1)} collective-permute-done((bf16[1024,256]{1,0:T(8,128)(2,1)}, bf16[1024,256]{1,0:T(8,128)(2,1)S(1)}, u32[]{:S(2)}, u32[]{:S(2)}) %collective-permute-start.20) | collective-permute-done | bytes 524320 | tf_op jit(solution)/shard_map/ppermute | solution.py:34
  156.8 1.7 collective-permute-start.24
  159.5 17.5 %shard_map.135 = (bf16[9,64,512]{2,1,0:T(8,128)(2,1)}, bf16[9,64,512]{2,1,0:T(8,128)(2,1)}, bf16[9,64,512]{2,1,0:T(8,128)(2,1)}, bf16[9,64,512]{2,1,0:T(8,128)(2,1)}) custom-call(s32[4]{0:T(128)} %and_select_fusion.refs_0_, bf16[4,64,4096]{2,1,0:T(8,128)(2,1)} %bitcast.136, bf16[8,8,16,256]{3,2,1,0:T(8,128)(2,1)} %bitcast.112, ...), custom_call_target="tpu_custom_call" | custom-call | flops 18342500352 | tf_op jit(solution)/shard_map/pallas_call | solution.py:209
  177.8 1.5 collective-permute-start.29
  179.3 2.7 %collective-permute-start.30 = (bf16[9,64,512]{2,1,0:T(8,128)(2,1)}, bf16[9,64,512]{2,1,0:T(8,128)(2,1)}, u32[]{:S(2)}, u32[]{:S(2)}) collective-permute-start(bf16[9,64,512]{2,1,0:T(8,128)(2,1)} %get-tuple-element.98), channel_id=1, source_target_pairs={{0,64},{8,72},{1,65},{9,73},{2,66},{10,74},{3,67},{11,75},{32,96},... | collective-permute-start | bytes 1769480 | tf_op jit(solution)/shard_map/ppermute | solution.py:34
  182.0 1.5 collective-permute-start.31
  183.5 2.3 fusion.6
  186.6 18.4 %all-gather.4.refs_3_ = f32[16,2,256]{2,1,0:T(2,128)} all-gather(f32[1,2,256]{2,1,0:T(2,128)S(1)} %maximum_bitcast_fusion), channel_id=5, replica_groups=mesh['dp'=16,'mp'=8] {'dp'}, dimensions={0}, use_global_device_ids=true | all-gather | bytes 34816 | tf_op jit(solution)/shard_map/all_gather | solution.py:376
  206.2 2.1 collective-permute-done.30.refs_1_
  208.3 1.9 add_convert_fusion
  211.3 4.2 %collective-permute-start.32 = (bf16[12,64,256]{2,1,0:T(8,128)(2,1)}, bf16[12,64,256]{2,1,0:T(8,128)(2,1)S(1)}, u32[]{:S(2)}, u32[]{:S(2)}) collective-permute-start(bf16[12,64,256]{2,1,0:T(8,128)(2,1)} %get-tuple-element.104), channel_id=1, source_target_pairs={{0,0},{8,4},{1,1},{9,5},{2,2},{10,6},{3,3},{11,7},{32,32},{40,36},... | collective-permute-start | bytes 1179656 | tf_op jit(solution)/shard_map/ppermute | solution.py:34
  215.5 1.9 collective-permute-start.33
  217.4 1.4 fusion.2
  219.4 15.8 %collective-permute-done.32 = bf16[12,64,256]{2,1,0:T(8,128)(2,1)S(1)} collective-permute-done((bf16[12,64,256]{2,1,0:T(8,128)(2,1)}, bf16[12,64,256]{2,1,0:T(8,128)(2,1)S(1)}, u32[]{:S(2)}, u32[]{:S(2)}) %collective-permute-start.32) | collective-permute-done | bytes 393248 | tf_op jit(solution)/shard_map/ppermute | solution.py:34
  (210 shorter events, 35.0 us)
Async XLA Ops:
  7.2 11.4 %copy-start.31 = (bf16[1,16,8,8,256]{4,3,2,1,0:T(8,128)(2,1)S(1)}, bf16[1,16,8,8,256]{4,3,2,1,0:T(8,128)(2,1)}, u32[]{:S(2)}) copy-start(bf16[1,16,8,8,256]{4,3,2,1,0:T(8,128)(2,1)} %param.9) | copy-start | bytes 1572868
  7.2 106.0 %all-gather.9.cloned.1.call-start = ((), (), s32[]{:S(2)}) async-start(), calls=%async_computation.2 | async-start | bytes 2621440 | tf_op jit(solution)/shard_map/all_gather | solution.py:282
  8.3 8.2 %collective-permute-start = (bf16[3,128,256]{2,1,0:T(8,128)(2,1)S(1)}, bf16[3,128,256]{2,1,0:T(8,128)(2,1)S(1)}, u32[]{:S(2)}, u32[]{:S(2)}) collective-permute-start(bf16[3,128,256]{2,1,0:T(8,128)(2,1)S(1)} %constant_dynamic-slice_fusion.2), channel_id=1, source_target_pairs={{0,4},{8,12},{1,5},{9,13},{2,6},{10,14},{3,7},{11,15},{32,36},{40,... | collective-permute-start | bytes 589832 | tf_op jit(solution)/shard_map/ppermute | solution.py:34
  17.2 19.9 %collective-permute-start.1 = (bf16[16,64,256]{2,1,0:T(8,128)(2,1)}, bf16[16,64,256]{2,1,0:T(8,128)(2,1)S(1)}, u32[]{:S(2)}, u32[]{:S(2)}) collective-permute-start(bf16[16,64,256]{2,1,0:T(8,128)(2,1)} %shard_map.119), channel_id=1, source_target_pairs={{0,4},{8,12},{1,5},{9,13},{2,6},{10,14},{3,7},{11,15},{32,36},{40,... | collective-permute-start | bytes 1572872 | tf_op jit(solution)/shard_map/ppermute | solution.py:34
  20.7 4.7 %collective-permute-start.5 = (bf16[64,1024]{1,0:T(8,128)(2,1)S(1)}, bf16[64,1024]{1,0:T(8,128)(2,1)S(1)}, u32[]{:S(2)}, u32[]{:S(2)}) collective-permute-start(bf16[64,1024]{1,0:T(8,128)(2,1)S(1)} %get-tuple-element.121), channel_id=1, source_target_pairs={{0,8},{8,0},{1,9},{9,1},{2,10},{10,2},{3,11},{11,3},{32,40},{40,32... | collective-permute-start | bytes 393224 | tf_op jit(solution)/shard_map/ppermute | solution.py:34
  20.8 11.3 %collective-permute-start.6 = (bf16[64,1024]{1,0:T(8,128)(2,1)S(1)}, bf16[64,1024]{1,0:T(8,128)(2,1)S(1)}, u32[]{:S(2)}, u32[]{:S(2)}) collective-permute-start(bf16[64,1024]{1,0:T(8,128)(2,1)S(1)} %get-tuple-element.120), channel_id=1, source_target_pairs={{0,16},{8,24},{1,17},{9,25},{2,18},{10,26},{3,19},{11,27},{32,48},... | collective-permute-start | bytes 393224 | tf_op jit(solution)/shard_map/ppermute | solution.py:34
  20.9 16.1 %collective-permute-start.2 = (bf16[3,128,256]{2,1,0:T(8,128)(2,1)S(1)}, bf16[3,128,256]{2,1,0:T(8,128)(2,1)S(1)}, u32[]{:S(2)}, u32[]{:S(2)}) collective-permute-start(bf16[3,128,256]{2,1,0:T(8,128)(2,1)S(1)} %copy-done.22), channel_id=1, source_target_pairs={{0,32},{8,40},{1,33},{9,41},{2,34},{10,42},{3,35},{11,43},{32,64},... | collective-permute-start | bytes 589832 | tf_op jit(solution)/shard_map/ppermute | solution.py:34
  22.6 14.5 %collective-permute-start.3 = (bf16[3,128,256]{2,1,0:T(8,128)(2,1)S(1)}, bf16[3,128,256]{2,1,0:T(8,128)(2,1)S(1)}, u32[]{:S(2)}, u32[]{:S(2)}) collective-permute-start(bf16[3,128,256]{2,1,0:T(8,128)(2,1)S(1)} %copy-done.22), channel_id=1, source_target_pairs={{0,64},{8,72},{1,65},{9,73},{2,66},{10,74},{3,67},{11,75},{32,96},... | collective-permute-start | bytes 589832 | tf_op jit(solution)/shard_map/ppermute | solution.py:34
  25.5 11.6 %copy-start.39 = (bf16[64,1024]{1,0:T(8,128)(2,1)}, bf16[64,1024]{1,0:T(8,128)(2,1)S(1)}, u32[]{:S(2)}) copy-start(bf16[64,1024]{1,0:T(8,128)(2,1)S(1)} %collective-permute-done.5.refs_4_) | copy-start | bytes 393220
  25.5 11.6 %collective-permute-start.4 = (bf16[3,128,256]{2,1,0:T(8,128)(2,1)S(1)}, bf16[3,128,256]{2,1,0:T(8,128)(2,1)S(1)}, u32[]{:S(2)}, u32[]{:S(2)}) collective-permute-start(bf16[3,128,256]{2,1,0:T(8,128)(2,1)S(1)} %copy-done.22), channel_id=1, source_target_pairs={{0,96},{8,104},{1,97},{9,105},{2,98},{10,106},{3,99},{11,107},{32,... | collective-permute-start | bytes 589832 | tf_op jit(solution)/shard_map/ppermute | solution.py:34
  32.1 4.9 %collective-permute-start.7 = (bf16[64,1024]{1,0:T(8,128)(2,1)S(1)}, bf16[64,1024]{1,0:T(8,128)(2,1)S(1)}, u32[]{:S(2)}, u32[]{:S(2)}) collective-permute-start(bf16[64,1024]{1,0:T(8,128)(2,1)S(1)} %get-tuple-element.119), channel_id=1, source_target_pairs={{0,24},{8,16},{1,25},{9,17},{2,26},{10,18},{3,27},{11,19},{32,56},... | collective-permute-start | bytes 393224 | tf_op jit(solution)/shard_map/ppermute | solution.py:34
  40.6 85.1 %all-gather.11.cloned.1.call-start = ((), (), s32[]{:S(2)}) async-start(), calls=%async_computation.3 | async-start | bytes 5308416 | tf_op jit(solution)/shard_map/all_gather | solution.py:314
  41.9 7.5 %copy-start.23 = (bf16[4,3,128,256]{3,2,1,0:T(8,128)(2,1)}, bf16[4,3,128,256]{3,2,1,0:T(8,128)(2,1)S(1)}, u32[]{:S(2)}) copy-start(bf16[4,3,128,256]{3,2,1,0:T(8,128)(2,1)S(1)} %pad_maximum_fusion.1.refs_4_) | copy-start | bytes 2359300
  41.9 3.3 %collective-permute-start.8 = (bf16[4,3,128,256]{3,2,1,0:T(8,128)(2,1)S(1)}, bf16[4,3,128,256]{3,2,1,0:T(8,128)(2,1)S(1)}, u32[]{:S(2)}, u32[]{:S(2)}) collective-permute-start(bf16[4,3,128,256]{3,2,1,0:T(8,128)(2,1)S(1)} %pad_maximum_fusion.1.refs_4_), channel_id=1, source_target_pairs={{0,8},{8,0},{1,9},{9,1},{2,10},{10,2},{3,11},{11,3},{32,40},{40,32... | collective-permute-start | bytes 2359304 | tf_op jit(solution)/shard_map/ppermute | solution.py:34
  46.0 17.4 %collective-permute-start.9 = (bf16[9,128,256]{2,1,0:T(8,128)(2,1)}, bf16[9,128,256]{2,1,0:T(8,128)(2,1)S(1)}, u32[]{:S(2)}, u32[]{:S(2)}) collective-permute-start(bf16[9,128,256]{2,1,0:T(8,128)(2,1)} %shard_map.123), channel_id=1, source_target_pairs={{0,4},{8,12},{1,5},{9,13},{2,6},{10,14},{3,7},{11,15},{32,36},{40,... | collective-permute-start | bytes 1769480 | tf_op jit(solution)/shard_map/ppermute | solution.py:34
  64.3 94.2 %all-gather.13.cloned.1.call-start = ((), (), s32[]{:S(2)}) async-start(), calls=%async_computation.4 | async-start | bytes 2621440 | tf_op jit(solution)/shard_map/all_gather | solution.py:327
  65.2 21.7 %copy-start.18 = (bf16[16,64,256]{2,1,0:T(8,128)(2,1)S(1)}, bf16[16,64,256]{2,1,0:T(8,128)(2,1)}, u32[]{:S(2)}) copy-start(bf16[16,64,256]{2,1,0:T(8,128)(2,1)} %get-tuple-element.56.refs_2_.refs_3_) | copy-start | bytes 1572868
  65.2 13.7 %collective-permute-start.12 = (bf16[16,64,256]{2,1,0:T(8,128)(2,1)}, bf16[16,64,256]{2,1,0:T(8,128)(2,1)S(1)}, u32[]{:S(2)}, u32[]{:S(2)}) collective-permute-start(bf16[16,64,256]{2,1,0:T(8,128)(2,1)} %shard_map.125), channel_id=1, source_target_pairs={{0,16},{8,24},{1,17},{9,25},{2,18},{10,26},{3,19},{11,27},{32,48},... | collective-permute-start | bytes 1572872 | tf_op jit(solution)/shard_map/ppermute | solution.py:34
  66.3 14.6 %collective-permute-start.13 = (bf16[16,64,256]{2,1,0:T(8,128)(2,1)}, bf16[16,64,256]{2,1,0:T(8,128)(2,1)S(1)}, u32[]{:S(2)}, u32[]{:S(2)}) collective-permute-start(bf16[16,64,256]{2,1,0:T(8,128)(2,1)} %shard_map.125), channel_id=1, source_target_pairs={{0,20},{8,28},{1,21},{9,29},{2,22},{10,30},{3,23},{11,31},{32,52},... | collective-permute-start | bytes 1572872 | tf_op jit(solution)/shard_map/ppermute | solution.py:34
  69.0 16.9 %collective-permute-start.10 = (bf16[1024,256]{1,0:T(8,128)(2,1)}, bf16[1024,256]{1,0:T(8,128)(2,1)S(1)}, u32[]{:S(2)}, u32[]{:S(2)}) collective-permute-start(bf16[1024,256]{1,0:T(8,128)(2,1)} %get-tuple-element.64), channel_id=1, source_target_pairs={{0,1},{8,9},{1,2},{9,10},{2,3},{10,11},{3,0},{11,8},{32,33},{40,41... | collective-permute-start | bytes 1572872 | tf_op jit(solution)/shard_map/ppermute | solution.py:34
  70.9 15.0 %collective-permute-start.11 = (bf16[1024,256]{1,0:T(8,128)(2,1)}, bf16[1024,256]{1,0:T(8,128)(2,1)S(1)}, u32[]{:S(2)}, u32[]{:S(2)}) collective-permute-start(bf16[1024,256]{1,0:T(8,128)(2,1)} %get-tuple-element.65), channel_id=1, source_target_pairs={{0,3},{8,11},{1,0},{9,8},{2,1},{10,9},{3,2},{11,10},{32,35},{40,43... | collective-permute-start | bytes 1572872 | tf_op jit(solution)/shard_map/ppermute | solution.py:34
  89.9 18.1 %collective-permute-start.14 = (bf16[4,16,64,256]{3,2,1,0:T(8,128)(2,1)}, bf16[4,16,64,256]{3,2,1,0:T(8,128)(2,1)}, u32[]{:S(2)}, u32[]{:S(2)}) collective-permute-start(bf16[4,16,64,256]{3,2,1,0:T(8,128)(2,1)} %pad_maximum_fusion), channel_id=1, source_target_pairs={{0,8},{8,0},{1,9},{9,1},{2,10},{10,2},{3,11},{11,3},{32,40},{40,32... | collective-permute-start | bytes 6291464 | tf_op jit(solution)/shard_map/ppermute | solution.py:34
  91.7 16.2 %collective-permute-start.18 = (bf16[1024,256]{1,0:T(8,128)(2,1)}, bf16[1024,256]{1,0:T(8,128)(2,1)}, u32[]{:S(2)}, u32[]{:S(2)}) collective-permute-start(bf16[1024,256]{1,0:T(8,128)(2,1)} %get-tuple-element.71), channel_id=1, source_target_pairs={{0,2},{8,10},{1,3},{9,11},{2,0},{10,8},{3,1},{11,9},{32,34},{40,42... | collective-permute-start | bytes 1572872 | tf_op jit(solution)/shard_map/ppermute | solution.py:34
  94.7 13.3 %copy-start.5 = (bf16[1024,256]{1,0:T(8,128)(2,1)S(1)}, bf16[1024,256]{1,0:T(8,128)(2,1)}, u32[]{:S(2)}) copy-start(bf16[1024,256]{1,0:T(8,128)(2,1)} %get-tuple-element.67.refs_1_) | copy-start | bytes 1572868
  94.7 13.3 %copy-start.6 = (f32[1024,256]{1,0:T(8,128)S(1)}, f32[1024,256]{1,0:T(8,128)}, u32[]{:S(2)}) copy-start(f32[1024,256]{1,0:T(8,128)} %get-tuple-element.60.refs_1_) | copy-start | bytes 3145732
  94.7 13.3 %copy-start.16 = (bf16[1024,256]{1,0:T(8,128)(2,1)S(1)}, bf16[1024,256]{1,0:T(8,128)(2,1)}, u32[]{:S(2)}) copy-start(bf16[1024,256]{1,0:T(8,128)(2,1)} %get-tuple-element.68) | copy-start | bytes 1572868
  96.8 4.3 %collective-permute-start.15 = (bf16[64,1024]{1,0:T(8,128)(2,1)}, bf16[64,1024]{1,0:T(8,128)(2,1)S(1)}, u32[]{:S(2)}, u32[]{:S(2)}) collective-permute-start(bf16[64,1024]{1,0:T(8,128)(2,1)} %get-tuple-element.117), channel_id=1, source_target_pairs={{0,8},{8,0},{1,9},{9,1},{2,10},{10,2},{3,11},{11,3},{32,40},{40,32... | collective-permute-start | bytes 393224 | tf_op jit(solution)/shard_map/ppermute | solution.py:34
  97.0 6.5 %collective-permute-start.16 = (bf16[64,1024]{1,0:T(8,128)(2,1)}, bf16[64,1024]{1,0:T(8,128)(2,1)S(1)}, u32[]{:S(2)}, u32[]{:S(2)}) collective-permute-start(bf16[64,1024]{1,0:T(8,128)(2,1)} %get-tuple-element.116), channel_id=1, source_target_pairs={{0,16},{8,24},{1,17},{9,25},{2,18},{10,26},{3,19},{11,27},{32,48},... | collective-permute-start | bytes 393224 | tf_op jit(solution)/shard_map/ppermute | solution.py:34
  97.8 7.2 %collective-permute-start.17 = (bf16[64,1024]{1,0:T(8,128)(2,1)}, bf16[64,1024]{1,0:T(8,128)(2,1)S(1)}, u32[]{:S(2)}, u32[]{:S(2)}) collective-permute-start(bf16[64,1024]{1,0:T(8,128)(2,1)} %get-tuple-element.115), channel_id=1, source_target_pairs={{0,24},{8,16},{1,25},{9,17},{2,26},{10,18},{3,27},{11,19},{32,56},... | collective-permute-start | bytes 393224 | tf_op jit(solution)/shard_map/ppermute | solution.py:34
  109.7 15.1 %collective-permute-start.19 = (bf16[8,8,16,256]{3,2,1,0:T(8,128)(2,1)S(1)}, bf16[8,8,16,256]{3,2,1,0:T(8,128)(2,1)S(1)}, u32[]{:S(2)}, u32[]{:S(2)}) collective-permute-start(bf16[8,8,16,256]{3,2,1,0:T(8,128)(2,1)S(1)} %bitcast.106), channel_id=1, source_target_pairs={{0,4},{8,12},{1,5},{9,13},{2,6},{10,14},{3,7},{11,15},{32,36},{40,... | collective-permute-start | bytes 1572872 | tf_op jit(solution)/shard_map/ppermute | solution.py:34
  112.1 46.5 %collective-permute-start.25 = (bf16[8,8,16,256]{3,2,1,0:T(8,128)(2,1)S(1)}, bf16[8,8,16,256]{3,2,1,0:T(8,128)(2,1)}, u32[]{:S(2)}, u32[]{:S(2)}) collective-permute-start(bf16[8,8,16,256]{3,2,1,0:T(8,128)(2,1)S(1)} %bitcast.108), channel_id=1, source_target_pairs={{0,8},{8,0},{1,9},{9,1},{2,10},{10,2},{3,11},{11,3},{32,40},{40,32... | collective-permute-start | bytes 1572872 | tf_op jit(solution)/shard_map/ppermute | solution.py:34
  113.0 73.6 %reduce-scatter.2.cloned.1.call-start = ((), (), s32[]{:S(2)}) async-start(), calls=%async_computation.1 | async-start | bytes 983040 | tf_op jit(solution)/shard_map/reduce_scatter | solution.py:336
  134.8 14.5 %collective-permute-start.22 = (bf16[8,8,16,256]{3,2,1,0:T(8,128)(2,1)}, bf16[8,8,16,256]{3,2,1,0:T(8,128)(2,1)S(1)}, u32[]{:S(2)}, u32[]{:S(2)}) collective-permute-start(bf16[8,8,16,256]{3,2,1,0:T(8,128)(2,1)} %shard_map.132.refs_6_), channel_id=1, source_target_pairs={{0,16},{8,24},{1,17},{9,25},{2,18},{10,26},{3,19},{11,27},{32,48},... | collective-permute-start | bytes 1572872 | tf_op jit(solution)/shard_map/ppermute | solution.py:34
  135.6 13.8 %collective-permute-start.23 = (bf16[8,8,16,256]{3,2,1,0:T(8,128)(2,1)}, bf16[8,8,16,256]{3,2,1,0:T(8,128)(2,1)S(1)}, u32[]{:S(2)}, u32[]{:S(2)}) collective-permute-start(bf16[8,8,16,256]{3,2,1,0:T(8,128)(2,1)} %shard_map.132.refs_6_), channel_id=1, source_target_pairs={{0,20},{8,28},{1,21},{9,29},{2,22},{10,30},{3,23},{11,31},{32,52},... | collective-permute-start | bytes 1572872 | tf_op jit(solution)/shard_map/ppermute | solution.py:34
  136.8 18.0 %collective-permute-start.20 = (bf16[1024,256]{1,0:T(8,128)(2,1)}, bf16[1024,256]{1,0:T(8,128)(2,1)S(1)}, u32[]{:S(2)}, u32[]{:S(2)}) collective-permute-start(bf16[1024,256]{1,0:T(8,128)(2,1)} %get-tuple-element.79.refs_1_), channel_id=1, source_target_pairs={{0,1},{8,9},{1,2},{9,10},{2,3},{10,11},{3,0},{11,8},{32,33},{40,41... | collective-permute-start | bytes 1572872 | tf_op jit(solution)/shard_map/ppermute | solution.py:34
  137.1 17.7 %collective-permute-start.21 = (bf16[1024,256]{1,0:T(8,128)(2,1)}, bf16[1024,256]{1,0:T(8,128)(2,1)S(1)}, u32[]{:S(2)}, u32[]{:S(2)}) collective-permute-start(bf16[1024,256]{1,0:T(8,128)(2,1)} %get-tuple-element.81), channel_id=1, source_target_pairs={{0,3},{8,11},{1,0},{9,8},{2,1},{10,9},{3,2},{11,10},{32,35},{40,43... | collective-permute-start | bytes 1572872 | tf_op jit(solution)/shard_map/ppermute | solution.py:34
  149.3 9.2 %collective-permute-start.26 = (bf16[8,8,16,256]{3,2,1,0:T(8,128)(2,1)}, bf16[8,8,16,256]{3,2,1,0:T(8,128)(2,1)}, u32[]{:S(2)}, u32[]{:S(2)}) collective-permute-start(bf16[8,8,16,256]{3,2,1,0:T(8,128)(2,1)} %get-tuple-element.77.refs_2_.refs_3_), channel_id=1, source_target_pairs={{0,8},{8,0},{1,9},{9,1},{2,10},{10,2},{3,11},{11,3},{32,40},{40,32... | collective-permute-start | bytes 1572872 | tf_op jit(solution)/shard_map/ppermute | solution.py:34
  155.8 2.7 %collective-permute-start.27 = (bf16[8,8,16,256]{3,2,1,0:T(8,128)(2,1)}, bf16[8,8,16,256]{3,2,1,0:T(8,128)(2,1)S(1)}, u32[]{:S(2)}, u32[]{:S(2)}) collective-permute-start(bf16[8,8,16,256]{3,2,1,0:T(8,128)(2,1)} %get-tuple-element.89.refs_4_), channel_id=1, source_target_pairs={{0,8},{8,0},{1,9},{9,1},{2,10},{10,2},{3,11},{11,3},{32,40},{40,32... | collective-permute-start | bytes 1572872 | tf_op jit(solution)/shard_map/ppermute | solution.py:34
  155.8 2.9 %collective-permute-start.28 = (bf16[8,8,16,256]{3,2,1,0:T(8,128)(2,1)}, bf16[8,8,16,256]{3,2,1,0:T(8,128)(2,1)S(1)}, u32[]{:S(2)}, u32[]{:S(2)}) collective-permute-start(bf16[8,8,16,256]{3,2,1,0:T(8,128)(2,1)} %get-tuple-element.90.refs_5_), channel_id=1, source_target_pairs={{0,8},{8,0},{1,9},{9,1},{2,10},{10,2},{3,11},{11,3},{32,40},{40,32... | collective-permute-start | bytes 1572872 | tf_op jit(solution)/shard_map/ppermute | solution.py:34
  156.8 20.2 %collective-permute-start.24 = (bf16[1024,256]{1,0:T(8,128)(2,1)}, bf16[1024,256]{1,0:T(8,128)(2,1)S(1)}, u32[]{:S(2)}, u32[]{:S(2)}) collective-permute-start(bf16[1024,256]{1,0:T(8,128)(2,1)} %get-tuple-element.85), channel_id=1, source_target_pairs={{0,2},{8,10},{1,3},{9,11},{2,0},{10,8},{3,1},{11,9},{32,34},{40,42... | collective-permute-start | bytes 1572872 | tf_op jit(solution)/shard_map/ppermute | solution.py:34
  177.8 28.4 %collective-permute-start.29 = (bf16[9,64,512]{2,1,0:T(8,128)(2,1)}, bf16[9,64,512]{2,1,0:T(8,128)(2,1)S(1)}, u32[]{:S(2)}, u32[]{:S(2)}) collective-permute-start(bf16[9,64,512]{2,1,0:T(8,128)(2,1)} %get-tuple-element.97), channel_id=1, source_target_pairs={{0,32},{8,40},{1,33},{9,41},{2,34},{10,42},{3,35},{11,43},{32,64},... | collective-permute-start | bytes 1769480 | tf_op jit(solution)/shard_map/ppermute | solution.py:34
  179.3 29.0 %collective-permute-start.30 = (bf16[9,64,512]{2,1,0:T(8,128)(2,1)}, bf16[9,64,512]{2,1,0:T(8,128)(2,1)}, u32[]{:S(2)}, u32[]{:S(2)}) collective-permute-start(bf16[9,64,512]{2,1,0:T(8,128)(2,1)} %get-tuple-element.98), channel_id=1, source_target_pairs={{0,64},{8,72},{1,65},{9,73},{2,66},{10,74},{3,67},{11,75},{32,96},... | collective-permute-start | bytes 1769480 | tf_op jit(solution)/shard_map/ppermute | solution.py:34
  182.0 26.3 %collective-permute-start.31 = (bf16[9,64,512]{2,1,0:T(8,128)(2,1)}, bf16[9,64,512]{2,1,0:T(8,128)(2,1)}, u32[]{:S(2)}, u32[]{:S(2)}) collective-permute-start(bf16[9,64,512]{2,1,0:T(8,128)(2,1)} %get-tuple-element.99), channel_id=1, source_target_pairs={{0,96},{8,104},{1,97},{9,105},{2,98},{10,106},{3,99},{11,107},{32,... | collective-permute-start | bytes 1769480 | tf_op jit(solution)/shard_map/ppermute | solution.py:34
  208.3 9.1 %copy-start.1 = (bf16[1,16,8,8,256]{4,3,2,1,0:T(8,128)(2,1)S(1)}, bf16[1,16,8,8,256]{4,3,2,1,0:T(8,128)(2,1)}, u32[]{:S(2)}) copy-start(bf16[1,16,8,8,256]{4,3,2,1,0:T(8,128)(2,1)} %param.10) | copy-start | bytes 1572868
  208.3 9.1 %copy-start.7 = (f32[1024,256]{1,0:T(8,128)S(1)}, f32[1024,256]{1,0:T(8,128)}, u32[]{:S(2)}) copy-start(f32[1024,256]{1,0:T(8,128)} %subtract_multiply_fusion) | copy-start | bytes 3145732
  210.2 8.6 %copy-start.43 = (f32[16,2,256]{2,1,0:T(2,128)S(1)}, f32[16,2,256]{2,1,0:T(2,128)}, u32[]{:S(2)}) copy-start(f32[16,2,256]{2,1,0:T(2,128)} %get-tuple-element.106) | copy-start | bytes 98308
  211.3 24.0 %collective-permute-start.32 = (bf16[12,64,256]{2,1,0:T(8,128)(2,1)}, bf16[12,64,256]{2,1,0:T(8,128)(2,1)S(1)}, u32[]{:S(2)}, u32[]{:S(2)}) collective-permute-start(bf16[12,64,256]{2,1,0:T(8,128)(2,1)} %get-tuple-element.104), channel_id=1, source_target_pairs={{0,0},{8,4},{1,1},{9,5},{2,2},{10,6},{3,3},{11,7},{32,32},{40,36},... | collective-permute-start | bytes 1179656 | tf_op jit(solution)/shard_map/ppermute | solution.py:34
  215.5 20.5 %collective-permute-start.33 = (bf16[12,64,256]{2,1,0:T(8,128)(2,1)}, bf16[12,64,256]{2,1,0:T(8,128)(2,1)S(1)}, u32[]{:S(2)}, u32[]{:S(2)}) collective-permute-start(bf16[12,64,256]{2,1,0:T(8,128)(2,1)} %get-tuple-element.105), channel_id=1, source_target_pairs={{0,4},{8,0},{1,5},{9,1},{2,6},{10,2},{3,7},{11,3},{32,36},{40,32},... | collective-permute-start | bytes 1179656 | tf_op jit(solution)/shard_map/ppermute | solution.py:34
  (39 other events, 116.8 us)
Sparse Core Ops, SparseCore 0:
  40.7 35.4 all-gather.8
  77.9 33.2 all-gather.10
  113.1 34.6 all-gather.12
  157.0 22.1 reduce-scatter.1

commit v5 on v4

--- a/solution.py
+++ b/solution.py
@@ -272,14 +272,16 @@
         return lax.dynamic_slice_in_dim(kernel, start, 128, axis=1)
 
     tk_part = send(kernel_part(temporal_kernel), to_half)
-    tk_parts = [send(tk_part, to_y(k)) for k in (1, 2, 3)]
-    cot_other = send(after(cot, tk_part), to_half)
-    turned = spatial_out.reshape(ROWS, CH).T.reshape(4, SUB, ROWS)
-    own, parts = exchange(after(turned, tk_part))
-    cot_other, tk_one, tk_two, tk_three, *parts = together(cot_other, *tk_parts, *parts)
-    tk_near = jnp.stack([tk_part, tk_one, tk_two, tk_three])
+    own, parts = exchange(spatial_out.reshape(ROWS, CH).T.reshape(4, SUB, ROWS))
+    tk_part, *parts = together(tk_part, *parts)
     saved_part = jnp.concatenate([own, *parts], axis=1)
     saved_left = (lax.all_gather(saved_part, "mp", axis=0, axis_index_groups=z_groups),)
+
+    tk_parts = [send(tk_part, to_y(k)) for k in (1, 2, 3)]
+    cot_other = send(cot, to_half)
+    sk_part = kernel_part(spatial_kernel)
+    cot_other, sk_part, *tk_parts = together(cot_other, sk_part, *tk_parts)
+    tk_near = jnp.stack([tk_part, *tk_parts])
 
     flat_in = block_input.reshape(FR, HT * WD, CH).transpose(1, 0, 2).reshape(ROWS, CH).astype(F32)
     count = ROWS * (C // G)
@@ -308,7 +310,7 @@
 
     tk_far = send(tk_near, to_core)
     arrays = (cot, cot_other, temporal_kernel, tk_near, tk_far)
-    sk_part = send(after(kernel_part(spatial_kernel), tk_far), to_half)
+    sk_part = send(after(sk_part, tk_far), to_half)
     up, down, far, mine = blocks_of(False, (1, 3, 2, 0), *arrays)
     sk_part, up, down, far = together(sk_part, up, down, far)
     sk_other = lax.all_gather(sk_part, "dp", axis=0, axis_index_groups=y_core_groups)

time: 245 us -> 242 us (0.988)
    unnamed x101 -> x100, local copies, waits for them, and re-layouts: 11.9 us -> 10.7 us
  transfers between devices with their start and end apart: 38 -> 38, of which waited for: 16 -> 18; matrix products, arithmetic and copies ran while one was open for 12% -> 11% of each run, Pallas kernels for 22% -> 22%
where the time goes in v5:
time: 242 us
  waiting for transfers between devices  66.2 us (27%)
  Pallas kernels  52.6 us (22%)
  starting transfers between devices  46.5 us (19%)
  local copies, waits for them, and re-layouts  24.5 us (10%)
  other arithmetic  19 us (8%)
  blocking collectives  18.4 us (8%)
  between operations  14.5 us (6%)
    ppermute x34, waiting for transfers between devices, send(): return lax.ppermute(value, ('dp', 'mp'), pairs)  66.2 us
    ppermute x34, starting transfers between devices, send(): return lax.ppermute(value, ('dp', 'mp'), pairs)  46.2 us
    pallas_call x3, Pallas kernels, dgrad(): pl.pallas_call(lambda *refs: dgrad_body(spatial, blocks, *refs), grid_spe...  26.7 us
    pallas_call x2, Pallas kernels, wgrad(): pl.pallas_call(lambda *refs: wgrad_body(first, spatial, len(left), len(fi...  25.9 us
    all_gather x1, blocking collectives, local(): sums = lax.all_gather(jnp.stack([gain_sum, bias_sum]), 'dp', axis=0)  18.4 us
    unnamed x100, local copies, waits for them, and re-layouts  10.7 us
  transfers between devices with their start and end apart: 38, of which 18 were waited for; matrix products, arithmetic and copies ran while one was open for 11% of the time, Pallas kernels for 22%

profile of v5, /device:TPU:6, one launch (start us, length us, event | category | flops | bytes accessed | tf_op | source)
XLA Modules:
  0.0 241.8 jit_solution(12263292637849940622)
XLA Ops:
  8.2 1.5 collective-permute-start.1
  9.7 1.3 copy.74
  11.3 1.8 collective-permute-start.4
  13.0 4.8 %collective-permute-done.3.refs_2_ = bf16[64,1024]{1,0:T(8,128)(2,1)S(1)} collective-permute-done((bf16[64,1024]{1,0:T(8,128)(2,1)S(1)}, bf16[64,1024]{1,0:T(8,128)(2,1)S(1)}, u32[]{:S(2)}, u32[]{:S(2)}) %collective-permute-start.3) | collective-permute-done | bytes 131104 | tf_op jit(solution)/shard_map/ppermute | solution.py:34
  17.8 1.7 collective-permute-done.4.refs_3_
  20.8 1.9 pad_maximum_fusion.2
  22.8 2.9 %collective-permute-start = (bf16[16,64,256]{2,1,0:T(8,128)(2,1)S(1)}, bf16[16,64,256]{2,1,0:T(8,128)(2,1)S(1)}, u32[]{:S(2)}, u32[]{:S(2)}) collective-permute-start(bf16[16,64,256]{2,1,0:T(8,128)(2,1)S(1)} %bitcast.100), channel_id=1, source_target_pairs={{0,4},{8,12},{1,5},{9,13},{2,6},{10,14},{3,7},{11,15},{32,36},{40,... | collective-permute-start | bytes 1572872 | tf_op jit(solution)/shard_map/ppermute | solution.py:34
  25.8 1.6 collective-permute-start.5
  27.3 2.9 %collective-permute-start.6 = (bf16[3,128,256]{2,1,0:T(8,128)(2,1)}, bf16[3,128,256]{2,1,0:T(8,128)(2,1)S(1)}, u32[]{:S(2)}, u32[]{:S(2)}) collective-permute-start(bf16[3,128,256]{2,1,0:T(8,128)(2,1)} %get-tuple-element.58), channel_id=1, source_target_pairs={{0,64},{8,72},{1,65},{9,73},{2,66},{10,74},{3,67},{11,75},{32,96},... | collective-permute-start | bytes 589832 | tf_op jit(solution)/shard_map/ppermute | solution.py:34
  30.2 1.3 collective-permute-start.7
  31.6 1.9 constant_dynamic-slice_fusion.2.refs_1_
  34.8 5.4 %collective-permute-done.6.refs_3_ = bf16[3,128,256]{2,1,0:T(8,128)(2,1)S(1)} collective-permute-done((bf16[3,128,256]{2,1,0:T(8,128)(2,1)}, bf16[3,128,256]{2,1,0:T(8,128)(2,1)S(1)}, u32[]{:S(2)}, u32[]{:S(2)}) %collective-permute-start.6) | collective-permute-done | bytes 196640 | tf_op jit(solution)/shard_map/ppermute | solution.py:34
  43.8 1.5 collective-permute-done.8.refs_5_.refs_1_
  47.4 8.3 %shard_map.121 = (bf16[1024,256]{1,0:T(8,128)(2,1)}, bf16[1024,256]{1,0:T(8,128)(2,1)}, bf16[1024,256]{1,0:T(8,128)(2,1)}, f32[1024,256]{1,0:T(8,128)}) custom-call(s32[13]{0:T(128)} %stack.118.refs_0_, bf16[16,64,256]{2,1,0:T(8,128)(2,1)} %bitcast.98, bf16[16,64,256]{2,1,0:T(8,128)(2,1)} %get-tuple-element.59.refs_2_.refs_3_, ...), custom_call_target="tpu_custom_call" | custom-call | flops 8049999872 | tf_op jit(solution)/shard_map/pallas_call | solution.py:150
  55.6 7.6 %collective-permute-done.9.refs_0_ = bf16[9,128,256]{2,1,0:T(8,128)(2,1)S(1)} collective-permute-done((bf16[9,128,256]{2,1,0:T(8,128)(2,1)}, bf16[9,128,256]{2,1,0:T(8,128)(2,1)S(1)}, u32[]{:S(2)}, u32[]{:S(2)}) %collective-permute-start.9) | collective-permute-done | bytes 589856 | tf_op jit(solution)/shard_map/ppermute | solution.py:34
  65.0 1.7 collective-permute-start.13
  66.7 1.9 collective-permute-start.10
  68.7 2.2 collective-permute-start.11
  70.9 7.5 %collective-permute-done.12.refs_3_ = bf16[16,64,256]{2,1,0:T(8,128)(2,1)S(1)} collective-permute-done((bf16[16,64,256]{2,1,0:T(8,128)(2,1)}, bf16[16,64,256]{2,1,0:T(8,128)(2,1)S(1)}, u32[]{:S(2)}, u32[]{:S(2)}) %collective-permute-start.12) | collective-permute-done | bytes 524320 | tf_op jit(solution)/shard_map/ppermute | solution.py:34
  79.6 2.5 %collective-permute-done.10.refs_0_ = bf16[1024,256]{1,0:T(8,128)(2,1)S(1)} collective-permute-done((bf16[1024,256]{1,0:T(8,128)(2,1)}, bf16[1024,256]{1,0:T(8,128)(2,1)S(1)}, u32[]{:S(2)}, u32[]{:S(2)}) %collective-permute-start.10) | collective-permute-done | bytes 524320 | tf_op jit(solution)/shard_map/ppermute | solution.py:34
  83.0 3.0 %pad_maximum_fusion = bf16[4,16,64,256]{3,2,1,0:T(8,128)(2,1)} fusion(bf16[1,16,64,256]{3,2,1,0:T(8,128)(2,1)} %bitcast.115, bf16[1,16,64,256]{3,2,1,0:T(8,128)(2,1)} %bitcast.114, bf16[1,16,64,256]{3,2,1,0:T(8,128)(2,1)S(1)} %bitcast.116, bf16[1,16,64,256]{3,2,1,0:T(8,128)(2,1)S(1)} %bitcast.102), kind=kLoop, calls=%fused_computation | loop fusion | flops 3145728 | bytes 4194304 | tf_op jit(solution)/shard_map/stack | solution.py:325
  87.9 2.8 %collective-permute-start.18 = (bf16[1024,256]{1,0:T(8,128)(2,1)}, bf16[1024,256]{1,0:T(8,128)(2,1)}, u32[]{:S(2)}, u32[]{:S(2)}) collective-permute-start(bf16[1024,256]{1,0:T(8,128)(2,1)} %get-tuple-element.75), channel_id=1, source_target_pairs={{0,2},{8,10},{1,3},{9,11},{2,0},{10,8},{3,1},{11,9},{32,34},{40,42... | collective-permute-start | bytes 1572872 | tf_op jit(solution)/shard_map/ppermute | solution.py:34
  92.0 2.0 dynamic-slice_bitcast_fusion
  98.2 2.6 %collective-permute-done.16.refs_2_ = bf16[64,1024]{1,0:T(8,128)(2,1)S(1)} collective-permute-done((bf16[64,1024]{1,0:T(8,128)(2,1)}, bf16[64,1024]{1,0:T(8,128)(2,1)S(1)}, u32[]{:S(2)}, u32[]{:S(2)}) %collective-permute-start.16) | collective-permute-done | bytes 131104 | tf_op jit(solution)/shard_map/ppermute | solution.py:34
  100.8 1.5 collective-permute-done.17.refs_3_
  102.3 1.8 collective-permute-done.18.refs_4_
  104.2 1.3 add_convert_fusion.1
  105.8 2.2 collective-permute-start.19
  110.0 8.4 %shard_map.128.refs_1_ = bf16[4,3,64,512]{3,2,1,0:T(8,128)(2,1)} custom-call(s32[4]{0:T(128)} %fusion.5.refs_0_, bf16[4,64,4096]{2,1,0:T(8,128)(2,1)} %bitcast.135, bf16[16,64,256]{2,1,0:T(8,128)(2,1)} %bitcast.99, bf16[16,64,256]{2,1,0:T(8,128)(2,1)} %get-tuple-element.59.refs_2_.refs_3_, bf16[16,64,256]{2,1,0:T(8,128)(2,1)} %get-tuple-element.73.refs_4_, ...), custom_call_target="tpu_custom_call" | custom-call | flops 9717499904 | tf_op jit(solution)/shard_map/pallas_call | solution.py:209
  118.4 2.6 %collective-permute-done.19.refs_0_ = bf16[8,8,16,256]{3,2,1,0:T(8,128)(2,1)S(1)} collective-permute-done((bf16[8,8,16,256]{3,2,1,0:T(8,128)(2,1)S(1)}, bf16[8,8,16,256]{3,2,1,0:T(8,128)(2,1)S(1)}, u32[]{:S(2)}, u32[]{:S(2)}) %collective-permute-start.19) | collective-permute-done | bytes 524320 | tf_op jit(solution)/shard_map/ppermute | solution.py:34
  121.8 9.1 %shard_map.130 = (bf16[1024,256]{1,0:T(8,128)(2,1)}, bf16[1024,256]{1,0:T(8,128)(2,1)}) custom-call(s32[7]{0:T(128)} %stack.132.refs_0_, bf16[8,8,16,256]{3,2,1,0:T(8,128)(2,1)} %bitcast.109, bf16[8,8,16,256]{3,2,1,0:T(8,128)(2,1)} %get-tuple-element.81.refs_2_.refs_3_, bf16[9,2048,256]{2,1,0:T(8,128)(2,1)} %bitcast.125, bf16[8,9,128,256]{3,2,1,0:T(8,128)(2,1)} %bitcast.131, ...), custom_call_target="tpu_custom_call" | custom-call | flops 9660000256 | tf_op jit(solution)/shard_map/pallas_call | solution.py:150
  131.5 2.1 collective-permute-start.23
  134.7 2.2 collective-permute-start.21
  136.8 9.3 %shard_map.132 = (bf16[1024,256]{1,0:T(8,128)(2,1)}, f32[1024,256]{1,0:T(8,128)}) custom-call(s32[7]{0:T(128)} %stack.110.refs_0_, bf16[8,8,16,256]{3,2,1,0:T(8,128)(2,1)} %bitcast.110, bf16[8,8,16,256]{3,2,1,0:T(8,128)(2,1)} %get-tuple-element.81.refs_2_.refs_3_, bf16[9,2048,256]{2,1,0:T(8,128)(2,1)} %bitcast.126, bf16[8,9,128,256]{3,2,1,0:T(8,128)(2,1)} %bitcast.133, ...), custom_call_target="tpu_custom_call" | custom-call | flops 9660000256 | tf_op jit(solution)/shard_map/pallas_call | solution.py:150
  146.3 5.7 %collective-permute-done.20.refs_0_ = bf16[1024,256]{1,0:T(8,128)(2,1)S(1)} collective-permute-done((bf16[1024,256]{1,0:T(8,128)(2,1)}, bf16[1024,256]{1,0:T(8,128)(2,1)S(1)}, u32[]{:S(2)}, u32[]{:S(2)}) %collective-permute-start.20) | collective-permute-done | bytes 524320 | tf_op jit(solution)/shard_map/ppermute | solution.py:34
  154.0 1.7 collective-permute-start.24
  156.7 17.5 %shard_map.134 = (bf16[9,64,512]{2,1,0:T(8,128)(2,1)}, bf16[9,64,512]{2,1,0:T(8,128)(2,1)}, bf16[9,64,512]{2,1,0:T(8,128)(2,1)}, bf16[9,64,512]{2,1,0:T(8,128)(2,1)}) custom-call(s32[4]{0:T(128)} %and_select_fusion.refs_0_, bf16[4,64,4096]{2,1,0:T(8,128)(2,1)} %bitcast.136, bf16[8,8,16,256]{3,2,1,0:T(8,128)(2,1)} %bitcast.111, ...), custom_call_target="tpu_custom_call" | custom-call | flops 18342500352 | tf_op jit(solution)/shard_map/pallas_call | solution.py:209
  175.0 1.5 collective-permute-start.29
  176.5 2.7 %collective-permute-start.30 = (bf16[9,64,512]{2,1,0:T(8,128)(2,1)}, bf16[9,64,512]{2,1,0:T(8,128)(2,1)}, u32[]{:S(2)}, u32[]{:S(2)}) collective-permute-start(bf16[9,64,512]{2,1,0:T(8,128)(2,1)} %get-tuple-element.102), channel_id=1, source_target_pairs={{0,64},{8,72},{1,65},{9,73},{2,66},{10,74},{3,67},{11,75},{32,96},... | collective-permute-start | bytes 1769480 | tf_op jit(solution)/shard_map/ppermute | solution.py:34
  179.2 1.5 collective-permute-start.31
  180.7 2.3 fusion.6
  183.8 18.4 %all-gather.4.refs_3_ = f32[16,2,256]{2,1,0:T(2,128)} all-gather(f32[1,2,256]{2,1,0:T(2,128)S(1)} %maximum_bitcast_fusion), channel_id=5, replica_groups=mesh['dp'=16,'mp'=8] {'dp'}, dimensions={0}, use_global_device_ids=true | all-gather | bytes 34816 | tf_op jit(solution)/shard_map/all_gather | solution.py:378
  203.4 2.0 collective-permute-done.30.refs_1_
  205.5 1.9 add_convert_fusion
  208.4 4.3 %collective-permute-start.32 = (bf16[12,64,256]{2,1,0:T(8,128)(2,1)}, bf16[12,64,256]{2,1,0:T(8,128)(2,1)S(1)}, u32[]{:S(2)}, u32[]{:S(2)}) collective-permute-start(bf16[12,64,256]{2,1,0:T(8,128)(2,1)} %get-tuple-element.108), channel_id=1, source_target_pairs={{0,0},{8,4},{1,1},{9,5},{2,2},{10,6},{3,3},{11,7},{32,32},{40,36},... | collective-permute-start | bytes 1179656 | tf_op jit(solution)/shard_map/ppermute | solution.py:34
  212.7 1.9 collective-permute-start.33
  214.7 1.4 fusion.2
  216.6 15.8 %collective-permute-done.32 = bf16[12,64,256]{2,1,0:T(8,128)(2,1)S(1)} collective-permute-done((bf16[12,64,256]{2,1,0:T(8,128)(2,1)}, bf16[12,64,256]{2,1,0:T(8,128)(2,1)S(1)}, u32[]{:S(2)}, u32[]{:S(2)}) %collective-permute-start.32) | collective-permute-done | bytes 393248 | tf_op jit(solution)/shard_map/ppermute | solution.py:34
  (208 shorter events, 35.7 us)
Async XLA Ops:
  7.2 102.8 %all-gather.9.cloned.1.call-start = ((), (), s32[]{:S(2)}) async-start(), calls=%async_computation.2 | async-start | bytes 2621440 | tf_op jit(solution)/shard_map/all_gather | solution.py:278
  8.2 11.3 %collective-permute-start.1 = (bf16[3,128,256]{2,1,0:T(8,128)(2,1)S(1)}, bf16[3,128,256]{2,1,0:T(8,128)(2,1)S(1)}, u32[]{:S(2)}, u32[]{:S(2)}) collective-permute-start(bf16[3,128,256]{2,1,0:T(8,128)(2,1)S(1)} %constant_dynamic-slice_fusion.1), channel_id=1, source_target_pairs={{0,4},{8,12},{1,5},{9,13},{2,6},{10,14},{3,7},{11,15},{32,36},{40,... | collective-permute-start | bytes 589832 | tf_op jit(solution)/shard_map/ppermute | solution.py:34
  9.7 13.1 %copy-start.4 = (bf16[1,16,8,8,256]{4,3,2,1,0:T(8,128)(2,1)S(1)}, bf16[1,16,8,8,256]{4,3,2,1,0:T(8,128)(2,1)}, u32[]{:S(2)}) copy-start(bf16[1,16,8,8,256]{4,3,2,1,0:T(8,128)(2,1)} %param.10) | copy-start | bytes 1572868
  11.1 2.0 collective-permute-start.2
  11.2 6.6 %collective-permute-start.3 = (bf16[64,1024]{1,0:T(8,128)(2,1)S(1)}, bf16[64,1024]{1,0:T(8,128)(2,1)S(1)}, u32[]{:S(2)}, u32[]{:S(2)}) collective-permute-start(bf16[64,1024]{1,0:T(8,128)(2,1)S(1)} %get-tuple-element.124), channel_id=1, source_target_pairs={{0,16},{8,24},{1,17},{9,25},{2,18},{10,26},{3,19},{11,27},{32,48},... | collective-permute-start | bytes 393224 | tf_op jit(solution)/shard_map/ppermute | solution.py:34
  11.3 8.2 %collective-permute-start.4 = (bf16[64,1024]{1,0:T(8,128)(2,1)S(1)}, bf16[64,1024]{1,0:T(8,128)(2,1)S(1)}, u32[]{:S(2)}, u32[]{:S(2)}) collective-permute-start(bf16[64,1024]{1,0:T(8,128)(2,1)S(1)} %get-tuple-element.123), channel_id=1, source_target_pairs={{0,24},{8,16},{1,25},{9,17},{2,26},{10,18},{3,27},{11,19},{32,56},... | collective-permute-start | bytes 393224 | tf_op jit(solution)/shard_map/ppermute | solution.py:34
  20.8 20.9 %copy-start.24 = (bf16[3,128,256]{2,1,0:T(8,128)(2,1)S(1)}, bf16[3,128,256]{2,1,0:T(8,128)(2,1)}, u32[]{:S(2)}) copy-start(bf16[3,128,256]{2,1,0:T(8,128)(2,1)} %get-tuple-element.58) | copy-start | bytes 589828
  22.8 99.0 %all-gather.11.cloned.1.call-start = ((), (), s32[]{:S(2)}) async-start(), calls=%async_computation.3 | async-start | bytes 5308416 | tf_op jit(solution)/shard_map/all_gather | solution.py:316
  22.8 17.3 %collective-permute-start = (bf16[16,64,256]{2,1,0:T(8,128)(2,1)S(1)}, bf16[16,64,256]{2,1,0:T(8,128)(2,1)S(1)}, u32[]{:S(2)}, u32[]{:S(2)}) collective-permute-start(bf16[16,64,256]{2,1,0:T(8,128)(2,1)S(1)} %bitcast.100), channel_id=1, source_target_pairs={{0,4},{8,12},{1,5},{9,13},{2,6},{10,14},{3,7},{11,15},{32,36},{40,... | collective-permute-start | bytes 1572872 | tf_op jit(solution)/shard_map/ppermute | solution.py:34
  25.8 9.0 %collective-permute-start.5 = (bf16[3,128,256]{2,1,0:T(8,128)(2,1)}, bf16[3,128,256]{2,1,0:T(8,128)(2,1)S(1)}, u32[]{:S(2)}, u32[]{:S(2)}) collective-permute-start(bf16[3,128,256]{2,1,0:T(8,128)(2,1)} %get-tuple-element.58), channel_id=1, source_target_pairs={{0,32},{8,40},{1,33},{9,41},{2,34},{10,42},{3,35},{11,43},{32,64},... | collective-permute-start | bytes 589832 | tf_op jit(solution)/shard_map/ppermute | solution.py:34
  27.3 12.8 %collective-permute-start.6 = (bf16[3,128,256]{2,1,0:T(8,128)(2,1)}, bf16[3,128,256]{2,1,0:T(8,128)(2,1)S(1)}, u32[]{:S(2)}, u32[]{:S(2)}) collective-permute-start(bf16[3,128,256]{2,1,0:T(8,128)(2,1)} %get-tuple-element.58), channel_id=1, source_target_pairs={{0,64},{8,72},{1,65},{9,73},{2,66},{10,74},{3,67},{11,75},{32,96},... | collective-permute-start | bytes 589832 | tf_op jit(solution)/shard_map/ppermute | solution.py:34
  30.2 9.9 %collective-permute-start.7 = (bf16[3,128,256]{2,1,0:T(8,128)(2,1)}, bf16[3,128,256]{2,1,0:T(8,128)(2,1)S(1)}, u32[]{:S(2)}, u32[]{:S(2)}) collective-permute-start(bf16[3,128,256]{2,1,0:T(8,128)(2,1)} %get-tuple-element.58), channel_id=1, source_target_pairs={{0,96},{8,104},{1,97},{9,105},{2,98},{10,106},{3,99},{11,107},{32,... | collective-permute-start | bytes 589832 | tf_op jit(solution)/shard_map/ppermute | solution.py:34
  42.9 2.4 collective-permute-start.8
  46.2 17.1 %collective-permute-start.9 = (bf16[9,128,256]{2,1,0:T(8,128)(2,1)}, bf16[9,128,256]{2,1,0:T(8,128)(2,1)S(1)}, u32[]{:S(2)}, u32[]{:S(2)}) collective-permute-start(bf16[9,128,256]{2,1,0:T(8,128)(2,1)} %shard_map.122), channel_id=1, source_target_pairs={{0,4},{8,12},{1,5},{9,13},{2,6},{10,14},{3,7},{11,15},{32,36},{40,... | collective-permute-start | bytes 1769480 | tf_op jit(solution)/shard_map/ppermute | solution.py:34
  55.6 8.6 %copy-start.5 = (bf16[1,16,8,8,256]{4,3,2,1,0:T(8,128)(2,1)S(1)}, bf16[1,16,8,8,256]{4,3,2,1,0:T(8,128)(2,1)}, u32[]{:S(2)}) copy-start(bf16[1,16,8,8,256]{4,3,2,1,0:T(8,128)(2,1)} %param.10) | copy-start | bytes 1572868
  64.2 91.6 %all-gather.13.cloned.1.call-start = ((), (), s32[]{:S(2)}) async-start(), calls=%async_computation.4 | async-start | bytes 2621440 | tf_op jit(solution)/shard_map/all_gather | solution.py:329
  65.0 18.0 %copy-start.21 = (bf16[16,64,256]{2,1,0:T(8,128)(2,1)S(1)}, bf16[16,64,256]{2,1,0:T(8,128)(2,1)}, u32[]{:S(2)}) copy-start(bf16[16,64,256]{2,1,0:T(8,128)(2,1)} %get-tuple-element.59.refs_2_.refs_3_) | copy-start | bytes 1572868
  65.0 13.3 %collective-permute-start.12 = (bf16[16,64,256]{2,1,0:T(8,128)(2,1)}, bf16[16,64,256]{2,1,0:T(8,128)(2,1)S(1)}, u32[]{:S(2)}, u32[]{:S(2)}) collective-permute-start(bf16[16,64,256]{2,1,0:T(8,128)(2,1)} %shard_map.124), channel_id=1, source_target_pairs={{0,16},{8,24},{1,17},{9,25},{2,18},{10,26},{3,19},{11,27},{32,48},... | collective-permute-start | bytes 1572872 | tf_op jit(solution)/shard_map/ppermute | solution.py:34
  65.0 14.6 %collective-permute-start.13 = (bf16[16,64,256]{2,1,0:T(8,128)(2,1)}, bf16[16,64,256]{2,1,0:T(8,128)(2,1)S(1)}, u32[]{:S(2)}, u32[]{:S(2)}) collective-permute-start(bf16[16,64,256]{2,1,0:T(8,128)(2,1)} %shard_map.124), channel_id=1, source_target_pairs={{0,20},{8,28},{1,21},{9,29},{2,22},{10,30},{3,23},{11,31},{32,52},... | collective-permute-start | bytes 1572872 | tf_op jit(solution)/shard_map/ppermute | solution.py:34
  66.7 15.3 %collective-permute-start.10 = (bf16[1024,256]{1,0:T(8,128)(2,1)}, bf16[1024,256]{1,0:T(8,128)(2,1)S(1)}, u32[]{:S(2)}, u32[]{:S(2)}) collective-permute-start(bf16[1024,256]{1,0:T(8,128)(2,1)} %get-tuple-element.68), channel_id=1, source_target_pairs={{0,1},{8,9},{1,2},{9,10},{2,3},{10,11},{3,0},{11,8},{32,33},{40,41... | collective-permute-start | bytes 1572872 | tf_op jit(solution)/shard_map/ppermute | solution.py:34
  68.7 13.4 %collective-permute-start.11 = (bf16[1024,256]{1,0:T(8,128)(2,1)}, bf16[1024,256]{1,0:T(8,128)(2,1)S(1)}, u32[]{:S(2)}, u32[]{:S(2)}) collective-permute-start(bf16[1024,256]{1,0:T(8,128)(2,1)} %get-tuple-element.69), channel_id=1, source_target_pairs={{0,3},{8,11},{1,0},{9,8},{2,1},{10,9},{3,2},{11,10},{32,35},{40,43... | collective-permute-start | bytes 1572872 | tf_op jit(solution)/shard_map/ppermute | solution.py:34
  86.0 18.1 %collective-permute-start.14 = (bf16[4,16,64,256]{3,2,1,0:T(8,128)(2,1)}, bf16[4,16,64,256]{3,2,1,0:T(8,128)(2,1)}, u32[]{:S(2)}, u32[]{:S(2)}) collective-permute-start(bf16[4,16,64,256]{3,2,1,0:T(8,128)(2,1)} %pad_maximum_fusion), channel_id=1, source_target_pairs={{0,8},{8,0},{1,9},{9,1},{2,10},{10,2},{3,11},{11,3},{32,40},{40,32... | collective-permute-start | bytes 6291464 | tf_op jit(solution)/shard_map/ppermute | solution.py:34
  87.9 16.2 %collective-permute-start.18 = (bf16[1024,256]{1,0:T(8,128)(2,1)}, bf16[1024,256]{1,0:T(8,128)(2,1)}, u32[]{:S(2)}, u32[]{:S(2)}) collective-permute-start(bf16[1024,256]{1,0:T(8,128)(2,1)} %get-tuple-element.75), channel_id=1, source_target_pairs={{0,2},{8,10},{1,3},{9,11},{2,0},{10,8},{3,1},{11,9},{32,34},{40,42... | collective-permute-start | bytes 1572872 | tf_op jit(solution)/shard_map/ppermute | solution.py:34
  92.0 12.1 %copy-start.3 = (bf16[1024,256]{1,0:T(8,128)(2,1)S(1)}, bf16[1024,256]{1,0:T(8,128)(2,1)}, u32[]{:S(2)}) copy-start(bf16[1024,256]{1,0:T(8,128)(2,1)} %get-tuple-element.71.refs_1_) | copy-start | bytes 1572868
  92.0 12.2 %copy-start.7 = (f32[1024,256]{1,0:T(8,128)S(1)}, f32[1024,256]{1,0:T(8,128)}, u32[]{:S(2)}) copy-start(f32[1024,256]{1,0:T(8,128)} %get-tuple-element.63.refs_1_) | copy-start | bytes 3145732
  92.0 12.2 %copy-start.17 = (bf16[1024,256]{1,0:T(8,128)(2,1)S(1)}, bf16[1024,256]{1,0:T(8,128)(2,1)}, u32[]{:S(2)}) copy-start(bf16[1024,256]{1,0:T(8,128)(2,1)} %get-tuple-element.72) | copy-start | bytes 1572868
  94.0 4.2 %collective-permute-start.15 = (bf16[64,1024]{1,0:T(8,128)(2,1)}, bf16[64,1024]{1,0:T(8,128)(2,1)S(1)}, u32[]{:S(2)}, u32[]{:S(2)}) collective-permute-start(bf16[64,1024]{1,0:T(8,128)(2,1)} %get-tuple-element.121), channel_id=1, source_target_pairs={{0,8},{8,0},{1,9},{9,1},{2,10},{10,2},{3,11},{11,3},{32,40},{40,32... | collective-permute-start | bytes 393224 | tf_op jit(solution)/shard_map/ppermute | solution.py:34
  94.3 6.5 %collective-permute-start.16 = (bf16[64,1024]{1,0:T(8,128)(2,1)}, bf16[64,1024]{1,0:T(8,128)(2,1)S(1)}, u32[]{:S(2)}, u32[]{:S(2)}) collective-permute-start(bf16[64,1024]{1,0:T(8,128)(2,1)} %get-tuple-element.120), channel_id=1, source_target_pairs={{0,16},{8,24},{1,17},{9,25},{2,18},{10,26},{3,19},{11,27},{32,48},... | collective-permute-start | bytes 393224 | tf_op jit(solution)/shard_map/ppermute | solution.py:34
  94.9 7.3 %collective-permute-start.17 = (bf16[64,1024]{1,0:T(8,128)(2,1)}, bf16[64,1024]{1,0:T(8,128)(2,1)S(1)}, u32[]{:S(2)}, u32[]{:S(2)}) collective-permute-start(bf16[64,1024]{1,0:T(8,128)(2,1)} %get-tuple-element.119), channel_id=1, source_target_pairs={{0,24},{8,16},{1,25},{9,17},{2,26},{10,18},{3,27},{11,19},{32,56},... | collective-permute-start | bytes 393224 | tf_op jit(solution)/shard_map/ppermute | solution.py:34
  105.8 15.1 %collective-permute-start.19 = (bf16[8,8,16,256]{3,2,1,0:T(8,128)(2,1)S(1)}, bf16[8,8,16,256]{3,2,1,0:T(8,128)(2,1)S(1)}, u32[]{:S(2)}, u32[]{:S(2)}) collective-permute-start(bf16[8,8,16,256]{3,2,1,0:T(8,128)(2,1)S(1)} %bitcast.105), channel_id=1, source_target_pairs={{0,4},{8,12},{1,5},{9,13},{2,6},{10,14},{3,7},{11,15},{32,36},{40,... | collective-permute-start | bytes 1572872 | tf_op jit(solution)/shard_map/ppermute | solution.py:34
  108.8 46.9 %collective-permute-start.25 = (bf16[8,8,16,256]{3,2,1,0:T(8,128)(2,1)S(1)}, bf16[8,8,16,256]{3,2,1,0:T(8,128)(2,1)}, u32[]{:S(2)}, u32[]{:S(2)}) collective-permute-start(bf16[8,8,16,256]{3,2,1,0:T(8,128)(2,1)S(1)} %bitcast.107), channel_id=1, source_target_pairs={{0,8},{8,0},{1,9},{9,1},{2,10},{10,2},{3,11},{11,3},{32,40},{40,32... | collective-permute-start | bytes 1572872 | tf_op jit(solution)/shard_map/ppermute | solution.py:34
  109.7 74.1 %reduce-scatter.2.cloned.1.call-start = ((), (), s32[]{:S(2)}) async-start(), calls=%async_computation.1 | async-start | bytes 983040 | tf_op jit(solution)/shard_map/reduce_scatter | solution.py:338
  130.9 15.2 %collective-permute-start.22 = (bf16[8,8,16,256]{3,2,1,0:T(8,128)(2,1)}, bf16[8,8,16,256]{3,2,1,0:T(8,128)(2,1)S(1)}, u32[]{:S(2)}, u32[]{:S(2)}) collective-permute-start(bf16[8,8,16,256]{3,2,1,0:T(8,128)(2,1)} %shard_map.131.refs_6_), channel_id=1, source_target_pairs={{0,16},{8,24},{1,17},{9,25},{2,18},{10,26},{3,19},{11,27},{32,48},... | collective-permute-start | bytes 1572872 | tf_op jit(solution)/shard_map/ppermute | solution.py:34
  131.5 14.8 %collective-permute-start.23 = (bf16[8,8,16,256]{3,2,1,0:T(8,128)(2,1)}, bf16[8,8,16,256]{3,2,1,0:T(8,128)(2,1)S(1)}, u32[]{:S(2)}, u32[]{:S(2)}) collective-permute-start(bf16[8,8,16,256]{3,2,1,0:T(8,128)(2,1)} %shard_map.131.refs_6_), channel_id=1, source_target_pairs={{0,20},{8,28},{1,21},{9,29},{2,22},{10,30},{3,23},{11,31},{32,52},... | collective-permute-start | bytes 1572872 | tf_op jit(solution)/shard_map/ppermute | solution.py:34
  133.6 18.4 %collective-permute-start.20 = (bf16[1024,256]{1,0:T(8,128)(2,1)}, bf16[1024,256]{1,0:T(8,128)(2,1)S(1)}, u32[]{:S(2)}, u32[]{:S(2)}) collective-permute-start(bf16[1024,256]{1,0:T(8,128)(2,1)} %get-tuple-element.83.refs_1_), channel_id=1, source_target_pairs={{0,1},{8,9},{1,2},{9,10},{2,3},{10,11},{3,0},{11,8},{32,33},{40,41... | collective-permute-start | bytes 1572872 | tf_op jit(solution)/shard_map/ppermute | solution.py:34
  134.7 17.3 %collective-permute-start.21 = (bf16[1024,256]{1,0:T(8,128)(2,1)}, bf16[1024,256]{1,0:T(8,128)(2,1)S(1)}, u32[]{:S(2)}, u32[]{:S(2)}) collective-permute-start(bf16[1024,256]{1,0:T(8,128)(2,1)} %get-tuple-element.85), channel_id=1, source_target_pairs={{0,3},{8,11},{1,0},{9,8},{2,1},{10,9},{3,2},{11,10},{32,35},{40,43... | collective-permute-start | bytes 1572872 | tf_op jit(solution)/shard_map/ppermute | solution.py:34
  146.1 9.6 %collective-permute-start.26 = (bf16[8,8,16,256]{3,2,1,0:T(8,128)(2,1)}, bf16[8,8,16,256]{3,2,1,0:T(8,128)(2,1)}, u32[]{:S(2)}, u32[]{:S(2)}) collective-permute-start(bf16[8,8,16,256]{3,2,1,0:T(8,128)(2,1)} %get-tuple-element.81.refs_2_.refs_3_), channel_id=1, source_target_pairs={{0,8},{8,0},{1,9},{9,1},{2,10},{10,2},{3,11},{11,3},{32,40},{40,32... | collective-permute-start | bytes 1572872 | tf_op jit(solution)/shard_map/ppermute | solution.py:34
  153.0 2.8 %collective-permute-start.27 = (bf16[8,8,16,256]{3,2,1,0:T(8,128)(2,1)}, bf16[8,8,16,256]{3,2,1,0:T(8,128)(2,1)S(1)}, u32[]{:S(2)}, u32[]{:S(2)}) collective-permute-start(bf16[8,8,16,256]{3,2,1,0:T(8,128)(2,1)} %get-tuple-element.93.refs_4_), channel_id=1, source_target_pairs={{0,8},{8,0},{1,9},{9,1},{2,10},{10,2},{3,11},{11,3},{32,40},{40,32... | collective-permute-start | bytes 1572872 | tf_op jit(solution)/shard_map/ppermute | solution.py:34
  153.0 2.9 %collective-permute-start.28 = (bf16[8,8,16,256]{3,2,1,0:T(8,128)(2,1)}, bf16[8,8,16,256]{3,2,1,0:T(8,128)(2,1)S(1)}, u32[]{:S(2)}, u32[]{:S(2)}) collective-permute-start(bf16[8,8,16,256]{3,2,1,0:T(8,128)(2,1)} %get-tuple-element.94.refs_5_), channel_id=1, source_target_pairs={{0,8},{8,0},{1,9},{9,1},{2,10},{10,2},{3,11},{11,3},{32,40},{40,32... | collective-permute-start | bytes 1572872 | tf_op jit(solution)/shard_map/ppermute | solution.py:34
  154.0 20.2 %collective-permute-start.24 = (bf16[1024,256]{1,0:T(8,128)(2,1)}, bf16[1024,256]{1,0:T(8,128)(2,1)S(1)}, u32[]{:S(2)}, u32[]{:S(2)}) collective-permute-start(bf16[1024,256]{1,0:T(8,128)(2,1)} %get-tuple-element.89), channel_id=1, source_target_pairs={{0,2},{8,10},{1,3},{9,11},{2,0},{10,8},{3,1},{11,9},{32,34},{40,42... | collective-permute-start | bytes 1572872 | tf_op jit(solution)/shard_map/ppermute | solution.py:34
  175.0 28.4 %collective-permute-start.29 = (bf16[9,64,512]{2,1,0:T(8,128)(2,1)}, bf16[9,64,512]{2,1,0:T(8,128)(2,1)S(1)}, u32[]{:S(2)}, u32[]{:S(2)}) collective-permute-start(bf16[9,64,512]{2,1,0:T(8,128)(2,1)} %get-tuple-element.101), channel_id=1, source_target_pairs={{0,32},{8,40},{1,33},{9,41},{2,34},{10,42},{3,35},{11,43},{32,64},... | collective-permute-start | bytes 1769480 | tf_op jit(solution)/shard_map/ppermute | solution.py:34
  176.5 28.9 %collective-permute-start.30 = (bf16[9,64,512]{2,1,0:T(8,128)(2,1)}, bf16[9,64,512]{2,1,0:T(8,128)(2,1)}, u32[]{:S(2)}, u32[]{:S(2)}) collective-permute-start(bf16[9,64,512]{2,1,0:T(8,128)(2,1)} %get-tuple-element.102), channel_id=1, source_target_pairs={{0,64},{8,72},{1,65},{9,73},{2,66},{10,74},{3,67},{11,75},{32,96},... | collective-permute-start | bytes 1769480 | tf_op jit(solution)/shard_map/ppermute | solution.py:34
  179.2 26.2 %collective-permute-start.31 = (bf16[9,64,512]{2,1,0:T(8,128)(2,1)}, bf16[9,64,512]{2,1,0:T(8,128)(2,1)}, u32[]{:S(2)}, u32[]{:S(2)}) collective-permute-start(bf16[9,64,512]{2,1,0:T(8,128)(2,1)} %get-tuple-element.103), channel_id=1, source_target_pairs={{0,96},{8,104},{1,97},{9,105},{2,98},{10,106},{3,99},{11,107},{32,... | collective-permute-start | bytes 1769480 | tf_op jit(solution)/shard_map/ppermute | solution.py:34
  205.5 9.2 %copy-start.6 = (bf16[1,16,8,8,256]{4,3,2,1,0:T(8,128)(2,1)S(1)}, bf16[1,16,8,8,256]{4,3,2,1,0:T(8,128)(2,1)}, u32[]{:S(2)}) copy-start(bf16[1,16,8,8,256]{4,3,2,1,0:T(8,128)(2,1)} %param.10) | copy-start | bytes 1572868
  205.5 9.2 %copy-start.8 = (f32[1024,256]{1,0:T(8,128)S(1)}, f32[1024,256]{1,0:T(8,128)}, u32[]{:S(2)}) copy-start(f32[1024,256]{1,0:T(8,128)} %subtract_multiply_fusion) | copy-start | bytes 3145732
  207.4 8.7 %copy-start.43 = (f32[16,2,256]{2,1,0:T(2,128)S(1)}, f32[16,2,256]{2,1,0:T(2,128)}, u32[]{:S(2)}) copy-start(f32[16,2,256]{2,1,0:T(2,128)} %get-tuple-element.110) | copy-start | bytes 98308
  208.4 24.0 %collective-permute-start.32 = (bf16[12,64,256]{2,1,0:T(8,128)(2,1)}, bf16[12,64,256]{2,1,0:T(8,128)(2,1)S(1)}, u32[]{:S(2)}, u32[]{:S(2)}) collective-permute-start(bf16[12,64,256]{2,1,0:T(8,128)(2,1)} %get-tuple-element.108), channel_id=1, source_target_pairs={{0,0},{8,4},{1,1},{9,5},{2,2},{10,6},{3,3},{11,7},{32,32},{40,36},... | collective-permute-start | bytes 1179656 | tf_op jit(solution)/shard_map/ppermute | solution.py:34
  212.7 20.4 %collective-permute-start.33 = (bf16[12,64,256]{2,1,0:T(8,128)(2,1)}, bf16[12,64,256]{2,1,0:T(8,128)(2,1)S(1)}, u32[]{:S(2)}, u32[]{:S(2)}) collective-permute-start(bf16[12,64,256]{2,1,0:T(8,128)(2,1)} %get-tuple-element.109), channel_id=1, source_target_pairs={{0,4},{8,0},{1,5},{9,1},{2,6},{10,2},{3,7},{11,3},{32,36},{40,32},... | collective-permute-start | bytes 1179656 | tf_op jit(solution)/shard_map/ppermute | solution.py:34
  (39 other events, 115.8 us)
Sparse Core Ops, SparseCore 0:
  22.9 34.4 all-gather.8
  64.3 35.6 all-gather.10
  109.8 35.4 all-gather.12
  154.1 22.1 reduce-scatter.1
